TPU v7x, 32 devices: a whole 2x2x4 slice. The times are simulated.
32 devices in a mesh: stn: 16 (over z, x, core), blk: 2 (over y).
Axes of the slice: x: 2, y: 2, z: 4, core: 2. Of those that a mesh axis runs over, the one named last changes fastest.
Arguments:
- voltages: bfloat16 [1024, 2, 63, 2, 4096], P('stn', 'blk'), may hold values from -6 to 6
- station_map: int32 [512], replicated, may hold values from 0 to 511, each once
- chan_counts: int32 [16], replicated, may hold values from 1 to 3, 32 in all
Outputs:
- visibilities: bfloat16 [16, 3, 2, 1024, 1024], P('stn', None, None, 'blk')
Inputs may be any that keep to these rules, and one draw needn't show every extreme that they name: A permutation: stream rows 2 q and 2 q + 1 of voltages are the two polarizations of station station_map[q]. `chan_counts`: the counts sum to 32; the largest is 3; device d of stn correlates the consecutive channels that start at the sum of the counts before it.
All inputs are finite; a program needn't handle non-finite values.
Results may differ from a plain program's by a relative error of at most 0.0056.
Values may be sent and summed in bfloat16 or wider, within the bound.
No kernel may reach another device: no remote copies, remote signals or barrier semaphores. Data moves between devices by JAX's collectives and lax.ppermute only.
A program may use at most 384 MiB of HBM per device.

v0:
```python
import math

import jax
import jax.numpy as jnp
from jax import lax
from jax.sharding import PartitionSpec as P

FFT_LEN = 4096
TAPS = 16
CAP = 3
NSPEC = 48


def prototype(tap_count, frame_len):
    span_len = tap_count * frame_len
    points = jnp.arange(span_len, dtype=jnp.float32) + 0.5
    window = 0.5 - 0.5 * jnp.cos(2.0 * math.pi * points / span_len)
    shifted = math.pi * (points - span_len / 2.0) / frame_len
    filt_vals = jnp.sin(shifted) / shifted * window
    filt_vals = filt_vals / jnp.sqrt(jnp.sum(filt_vals * filt_vals))
    return filt_vals.reshape(tap_count, frame_len)


def direct_dft(folded, band_len):
    frame_len = folded.shape[-1]
    positions = jnp.arange(frame_len, dtype=jnp.int32)
    channels = jnp.arange(band_len, dtype=jnp.int32)
    phase = (positions[:, None] * channels[None, :] % frame_len).astype(jnp.float32) * (
        2.0 * math.pi / frame_len
    )
    cosine = jnp.cos(phase)
    sine = jnp.sin(phase)
    table = jnp.concatenate(
        [jnp.concatenate([cosine, -sine], axis=1), jnp.concatenate([sine, cosine], axis=1)], axis=0
    )
    rows_in = folded.reshape(-1, 2 * frame_len)
    result = jnp.dot(
        rows_in, table, precision=lax.Precision.HIGHEST, preferred_element_type=jnp.float32
    )
    return result.reshape(folded.shape[:-2] + (2, band_len))


def body(voltages, station_map, chan_counts):
    stn_count = lax.axis_size("stn")
    band_len = 2 * stn_count
    signal = voltages[:, 0]
    local_rows = signal.shape[0]
    taper_table = prototype(TAPS, FFT_LEN)
    folded = jnp.zeros((local_rows, NSPEC, 2, FFT_LEN), jnp.float32)
    for tap_idx in range(TAPS):
        folded = (
            folded + signal[:, tap_idx : tap_idx + NSPEC].astype(jnp.float32) * taper_table[tap_idx]
        )
    spectra = direct_dft(folded, band_len)
    spectra = spectra.astype(jnp.bfloat16)
    offsets = jnp.cumsum(chan_counts) - chan_counts
    slot_range = jnp.arange(CAP, dtype=jnp.int32)
    pick_index = (
        offsets[:, None] + jnp.minimum(slot_range[None, :], chan_counts[:, None] - 1)
    ).reshape(-1)
    outgoing = jnp.take(spectra, pick_index, axis=3).reshape(local_rows, NSPEC, 2, stn_count, CAP)
    outgoing = outgoing.transpose(3, 4, 2, 0, 1)
    time_len = outgoing.shape[4]
    incoming = lax.all_to_all(
        outgoing.reshape(stn_count, -1), "stn", split_axis=0, concat_axis=0, tiled=True
    )
    incoming = incoming.reshape(stn_count, CAP, 2, local_rows, time_len).transpose(1, 2, 0, 3, 4)
    incoming = incoming.reshape(CAP, 2, stn_count * local_rows, time_len)
    incoming = lax.all_gather(incoming, "blk", axis=3, tiled=True)
    row_count = stn_count * local_rows
    station_total = row_count // 2
    inverse = (
        jnp.zeros((station_total,), jnp.int32)
        .at[station_map]
        .set(jnp.arange(station_total, dtype=jnp.int32))
    )
    true_rows = (2 * inverse[:, None] + jnp.arange(2, dtype=jnp.int32)[None, :]).reshape(-1)
    ordered = jnp.take(incoming, true_rows, axis=2)
    joined = jnp.concatenate([ordered[:, 0], ordered[:, 1]], axis=2)
    turned = jnp.concatenate([ordered[:, 1], -ordered[:, 0]], axis=2)
    groups = lax.axis_size("blk")
    half_rows = row_count // groups
    my_index = lax.axis_index("stn")
    live_count = chan_counts[my_index]
    valid_mask = (slot_range < live_count).astype(jnp.float32)[:, None, None, None]
    samples = ordered.shape[3]
    row_start = lax.axis_index("blk") * half_rows
    near_rows = lax.dynamic_slice_in_dim(joined, row_start, half_rows, 1)
    turn_rows = lax.dynamic_slice_in_dim(turned, row_start, half_rows, 1)
    stacked = jnp.concatenate([near_rows, turn_rows], axis=1)
    visibility = jnp.einsum("kit,kjt->kij", stacked, joined, preferred_element_type=jnp.float32)
    visibility = visibility.reshape(CAP, 2, half_rows, row_count) * (valid_mask / samples)
    return visibility.astype(jnp.bfloat16)[None]


def solution(mesh):
    return jax.shard_map(
        body,
        mesh=mesh,
        in_specs=(P("stn", "blk", None, None, None), P(), P()),
        out_specs=P("stn", None, None, "blk", None),
        check_vma=False,
    )
```

profile of v0, /device:TPU:0, one launch (start us, length us, event | category | flops | bytes accessed | tf_op | source)
XLA Modules:
  0.0 1026.1 jit_solution(3508396548868112700)
XLA Ops:
  6.5 2.4 multiply_reduce_fusion
  8.9 2.9 fusion.23
  11.8 2.7 fusion.25
  14.5 0.7 copy.31
  15.3 0.1 reduce
  15.4 0.7 fusion.32
  16.1 0.7 minimum_add_fusion
  16.7 0.7 compare_and_fusion
  18.0 1.8 broadcast_divide_fusion
  19.8 55.6 %copy.46 = bf16[64,1,63,2,4096]{4,2,3,0,1:T(8,128)(2,1)} copy(bf16[64,1,63,2,4096]{4,3,2,1,0:T(2,128)(2,1)} %param.3) | data formatting | bytes 132120576 | tf_op args[0]
  75.4 392.1 %multiply_add_fusion = f32[64,48,2,4096]{3,1,2,0:T(8,128)} fusion(bf16[64,63,2,4096]{3,1,2,0:T(8,128)(2,1)} %bitcast.38, f32[4096]{0:T(1024)S(1)} %get-tuple-element.10, f32[4096]{0:T(1024)S(1)} %get-tuple-element.11, f32[4096]{0:T(1024)S(1)} %get-tuple-element.12, f32[4096]{0:T(1024)S(1)} %get-tuple-element.13, f32[4096]{0:T(1024)S(1)} %get-tuple-element.14, ...), kind=kLoop, calls=%fused_computation.5 | loop fusion | flops 1182793728 | bytes 906231808 | tf_op jit(solution)/shard_map/add | solution.py:52
  467.6 161.3 %copy.33 = f32[64,48,2,4096]{3,2,1,0:T(2,128)} copy(f32[64,48,2,4096]{3,1,2,0:T(8,128)} %multiply_add_fusion) | data formatting | bytes 201326592 | tf_op jit(solution)/shard_map/add | solution.py:52
  628.9 0.0 copy-start
  628.9 0.0 copy-start.1
  628.9 0.0 copy-start.2
  628.9 125.7 %reshape.242 = f32[64,48,8192,1]{2,1,0,3:T(8,128)} reshape(f32[64,48,2,4096]{3,2,1,0:T(2,128)} %copy.33) | data formatting | bytes 201326592 | tf_op jit(solution)/shard_map/dot_general | solution.py:37
  754.5 0.0 copy-done
  754.5 0.0 copy-done.1
  754.5 0.0 copy-done.2
  754.5 0.1 maximum_maximum_fusion
  754.7 0.0 copy-start.3
  754.7 0.0 copy-start.4
  754.7 0.0 copy-start.5
  754.7 0.0 copy-start.6
  754.7 168.4 %fusion.2 = bf16[64,48,2,32]{1,3,2,0:T(8,128)(2,1)S(1)} fusion(f32[2,32,8192,1]{2,1,0,3:T(8,128)S(1)} %bitcast.40, f32[64,48,8192,1]{2,1,0,3:T(8,128)} %reshape.242), kind=kOutput, calls=%fused_computation.9 | convolution fusion | flops 19327549440 | bytes 103153664 | tf_op jit(solution)/shard_map/dot_general | solution.py:37
  923.2 1.2 copy.34
  924.4 0.0 copy-done.3
  924.4 0.1 add.203
  924.5 0.8 gather_fusion
  925.3 0.1 copy.35
  925.4 0.0 copy-done.4
  925.4 0.2 select_bitcast_fusion.1
  925.6 0.9 copy.36
  926.4 2.0 all_to_all.8
  928.4 0.5 broadcast.167
  929.0 4.2 reduce.2
  933.1 1.2 reshape.250
  934.4 7.4 all-to-all-start
  941.7 0.0 all-gather.2.cloned.1.call-start
  941.8 0.0 copy-done.5
  941.8 2.4 scatter_custom_fusion
  944.3 13.0 %all-to-all-done = bf16[16,2,9216]{2,1,0:T(2,128)(2,1)S(1)} async-done(((bf16[16,2,9216]{2,1,0:T(2,128)(2,1)}), bf16[16,2,9216]{2,1,0:T(2,128)(2,1)S(1)}, u32[]{:S(2)}, u32[]{:S(2)}) %all-to-all-start) | async-done | bytes 589856 | tf_op jit(solution)/shard_map/all_to_all | solution.py:64
  957.3 0.7 reshape.251
  958.0 3.5 reduce.1
  961.6 1.6 reshape.214
  963.2 1.1 copy.43
  964.3 1.5 reshape.245
  965.8 0.0 all-gather.2.cloned.1.call-update
  965.9 0.1 iota_add_fusion.2
  966.0 0.2 add.206
  966.2 0.2 add.179
  966.3 0.0 copy-done.6
  966.3 0.6 dynamic_slice.11
  967.0 0.6 compare_select_fusion.5
  967.6 20.9 %all-gather.2.cloned.1.call-done = bf16[3,2,1024,96]{2,1,0,3:T(2,128)(2,1)} async-done(((bf16[3,2,1024,48]{2,1,0,3:T(2,128)(2,1)}), bf16[3,2,1024,96]{2,1,0,3:T(2,128)(2,1)}) %all-gather.2.cloned.1.call-update) | async-done | bytes 1179664 | tf_op jit(solution)/shard_map/all_gather | solution.py:69
  988.5 4.8 copy.40
  993.4 7.2 gather_fusion.1
  1000.6 2.1 copy.41
  1002.7 0.1 select_bitcast_fusion
  1002.8 0.1 slice_bitcast_fusion.1
  1003.0 0.1 fusion.10
  1003.2 6.4 fusion.5
  1009.6 9.3 multiply_convert_fusion
  (11 shorter events, 0.1 us)
Async XLA Ops:
  628.9 125.7 %copy-start = (f32[4096,32]{0,1:T(8,128)S(1)}, f32[4096,32]{0,1:T(8,128)}, u32[]{:S(2)}) copy-start(f32[4096,32]{0,1:T(8,128)} %get-tuple-element.27) | copy-start | bytes 1572868
  628.9 125.7 %copy-start.1 = (f32[4096,32]{0,1:T(8,128)S(1)}, f32[4096,32]{0,1:T(8,128)}, u32[]{:S(2)}) copy-start(f32[4096,32]{0,1:T(8,128)} %get-tuple-element.28) | copy-start | bytes 1572868
  628.9 125.7 %copy-start.2 = (f32[4096,32]{0,1:T(8,128)S(1)}, f32[4096,32]{0,1:T(8,128)}, u32[]{:S(2)}) copy-start(f32[4096,32]{0,1:T(8,128)} %fusion.25) | copy-start | bytes 1572868
  754.7 169.7 %copy-start.3 = (s32[16,3]{1,0:T(8,128)S(1)}, s32[16,3]{1,0:T(8,128)}, u32[]{:S(2)}) copy-start(s32[16,3]{1,0:T(8,128)} %minimum_add_fusion) | copy-start | bytes 580
  754.7 170.7 %copy-start.4 = (pred[16,3]{1,0:T(8,128)(4,1)S(1)}, pred[16,3]{1,0:T(8,128)(4,1)}, u32[]{:S(2)}) copy-start(pred[16,3]{1,0:T(8,128)(4,1)} %compare_and_fusion) | copy-start | bytes 148
  754.7 187.1 %copy-start.5 = (s32[512]{0:T(512)S(1)}, s32[512]{0:T(512)}, u32[]{:S(2)}) copy-start(s32[512]{0:T(512)} %param.4) | copy-start | bytes 6148
  754.7 211.6 %copy-start.6 = (s32[16]{0:T(128)S(1)}, s32[16]{0:T(128)}, u32[]{:S(2)}) copy-start(s32[16]{0:T(128)} %param.5) | copy-start | bytes 196
  934.4 22.9 %all-to-all-start = ((bf16[16,2,9216]{2,1,0:T(2,128)(2,1)}), bf16[16,2,9216]{2,1,0:T(2,128)(2,1)S(1)}, u32[]{:S(2)}, u32[]{:S(2)}) async-start(bf16[16,2,9216]{2,1,0:T(2,128)(2,1)} %reshape.250), calls=%async_computation | async-start | bytes 1179648 | tf_op jit(solution)/shard_map/all_to_all | solution.py:64
  941.7 46.8 %all-gather.2.cloned.1.call-start = ((), (), s32[]{:S(2)}) async-start(), calls=%async_computation.1 | async-start | bytes 1769472 | tf_op jit(solution)/shard_map/all_gather | solution.py:69
Sparse Core Ops, SparseCore 0:
  966.0 22.5 all-gather.1
where the time goes:
time: 1040 us; the launch traced here: 1030 us
  other arithmetic  422 us (41%)
  local copies, waits for them, and re-layouts  373 us (36%)
  matrix products  175 us (17%)
  waiting for transfers between devices  34 us (3%)
  between operations  14.8 us (1%)
    add x1, other arithmetic, body(): folded + signal[:, tap_idx:tap_idx + NSPEC].astype(jnp.float32) * taper_t...  392 us
    dot_general x1, matrix products, direct_dft(): jnp.dot(rows_in, table, precision=lax.Precision.HIGHEST, preferred_elemen...  168 us
    add x1, local copies, waits for them, and re-layouts, body(): folded + signal[:, tap_idx:tap_idx + NSPEC].astype(jnp.float32) * taper_t...  161 us
    dot_general x1, local copies, waits for them, and re-layouts, direct_dft(): jnp.dot(rows_in, table, precision=lax.Precision.HIGHEST, preferred_elemen...  126 us
    unnamed x17, local copies, waits for them, and re-layouts  57.6 us
    all_gather x1, waiting for transfers between devices, body(): incoming = lax.all_gather(incoming, 'blk', axis=3, tiled=True)  20.9 us
  transfers between devices with their start and end apart: 2, of which 2 were waited for; matrix products, arithmetic and copies ran while one was open for 0% of the time, Pallas kernels for 0%

commit v1 on v0

v1 whole, which is shorter than its diff:
```python
import functools
import math

import jax
import jax.numpy as jnp
import ml_dtypes
import numpy as np
from jax import lax
from jax.experimental import pallas as pl
from jax.experimental.pallas import tpu as pltpu
from jax.sharding import PartitionSpec as P

FFT_LEN = 4096
TAPS = 16
CAP = 3
NSPEC = 48
LANES = 128


def prototype():
    span = TAPS * FFT_LEN
    points = np.arange(span, dtype=np.float64) + 0.5
    window = 0.5 - 0.5 * np.cos(2.0 * math.pi * points / span)
    shifted = math.pi * (points - span / 2.0) / FFT_LEN
    filt = np.sin(shifted) / shifted * window
    return (filt / np.sqrt(np.sum(filt * filt))).reshape(TAPS, FFT_LEN)


def frame_basis(band, count):
    limit = math.pi * (band + 0.1)
    terms = count + int(limit) + 60
    k = np.arange(terms, dtype=np.float64)
    diagonal = k * (k + 1) + (2 * k * (k + 1) - 1) / ((2 * k + 3) * (2 * k - 1)) * limit**2
    m = k[:-2]
    beside = (m + 2) * (m + 1) / ((2 * m + 3) * np.sqrt((2 * m + 1) * (2 * m + 5))) * limit**2
    matrix = np.diag(diagonal) + np.diag(beside, 2) + np.diag(beside, -2)
    _, vectors = np.linalg.eigh(matrix)
    x = (2 * np.arange(FFT_LEN) + 1.0) / FFT_LEN - 1
    legendre = np.zeros((terms, FFT_LEN))
    legendre[0] = 1.0
    legendre[1] = x
    for j in range(2, terms):
        legendre[j] = ((2 * j - 1) * x * legendre[j - 1] - (j - 1) * legendre[j - 2]) / j
    legendre *= np.sqrt((k + 0.5) * 2.0 / FFT_LEN)[:, None]
    return legendre.T @ vectors[:, :count]


@functools.lru_cache(maxsize=4)
def tables(band):
    bf16 = ml_dtypes.bfloat16
    count = -(-(2 * band + 32) // LANES) * LANES
    basis = frame_basis(band, count)
    high = basis.astype(bf16)
    low = (basis - high.astype(np.float64)).astype(bf16)
    held = high.astype(np.float64) + low.astype(np.float64)
    phase = 2.0 * math.pi / FFT_LEN * (np.outer(np.arange(FFT_LEN), np.arange(band)) % FFT_LEN)
    wave = np.concatenate([np.cos(phase), -np.sin(phase)], axis=1)
    gram = held.T @ held
    mixing = [np.linalg.solve(gram, held.T @ (row[:, None] * wave)) for row in prototype()]
    per = max(1, LANES // (2 * band))
    groups = TAPS // per
    order = [b + groups * u for b in range(groups) for u in range(per)]
    mixing = np.concatenate([mixing[t] for t in order], axis=1).astype(bf16)
    return np.concatenate([high, low], axis=1), np.concatenate([mixing, mixing], axis=0)


def channelizer(band, dests, streams, step, counts, v_ref, u_ref, w_ref, out_ref, z, p, x, turned):
    i = pl.program_id(0)
    half = u_ref.shape[1] // 2
    frames = v_ref.shape[2]
    rows = 2 * frames
    per = max(1, LANES // (2 * band))
    groups = TAPS // per
    width = per * 2 * band
    need = 2 * NSPEC + 2 * groups * (per - 1)

    signal = v_ref[...].reshape(step * rows, FFT_LEN)
    coeff = jnp.dot(signal, u_ref[...], preferred_element_type=jnp.float32)
    coeff = coeff[:, :half] + coeff[:, half:]
    high = coeff.astype(jnp.bfloat16)
    low = (coeff - high.astype(jnp.float32)).astype(jnp.bfloat16)
    z[...] = jnp.dot(
        jnp.concatenate([high, low], axis=1), w_ref[...], preferred_element_type=jnp.float32
    )
    for r in range(step):
        total = None
        for b in range(groups):
            term = z[pl.ds(r * rows + 2 * b, need), b * width : (b + 1) * width]
            total = term if total is None else total + term
        if per > 1:
            whole = total[: 2 * NSPEC]
            for u in range(1, per):
                shifted = total[2 * groups * u : 2 * groups * u + 2 * NSPEC]
                whole = whole + jnp.roll(shifted, -2 * band * u, axis=1)
            total = whole
        blocks = range(width // LANES)
        for n in blocks:
            p[n] = total[:, n * LANES : (n + 1) * LANES]
        even = jnp.concatenate([p[n, pl.ds(0, NSPEC, stride=2), :] for n in blocks], axis=1)
        odd = jnp.concatenate([p[n, pl.ds(1, NSPEC, stride=2), :] for n in blocks], axis=1)
        swapped = [-odd[:, band : 2 * band], odd[:, :band]]
        if width > 2 * band:
            swapped.append(jnp.zeros((NSPEC, width - 2 * band), jnp.float32))
        spectrum = even + jnp.concatenate(swapped, axis=1)
        for n in blocks:
            x[n, pl.ds(i * step + r, NSPEC, stride=streams), :] = spectrum[
                :, n * LANES : (n + 1) * LANES
            ]

    @pl.when(i == pl.num_programs(0) - 1)
    def _():
        lane = lax.broadcasted_iota(jnp.int32, (8, width), 1)
        row = lax.broadcasted_iota(jnp.int32, (8, width), 0)
        slot = row // 2
        base = (row % 2) * band
        picks = []
        offset = jnp.int32(0)
        for d in range(dests):
            count = counts[d]
            want = offset + jnp.minimum(slot, count - 1) + base
            picks.append(jnp.where((lane == want) & (row < 2 * CAP), 1.0, 0.0))
            offset = offset + count
        pick = jnp.concatenate(picks, axis=0).astype(jnp.bfloat16)
        spectra = jnp.concatenate([x[n] for n in range(width // LANES)], axis=1)
        out = lax.dot_general(
            pick, spectra.astype(jnp.bfloat16), (((1,), (1,)), ((), ())),
            preferred_element_type=jnp.float32,
        )
        tiles = NSPEC * streams // LANES
        for d in range(dests):
            for t in range(tiles):
                turned[d, pl.ds(t, 2 * CAP, stride=tiles), :] = out[
                    8 * d : 8 * d + 2 * CAP, t * LANES : (t + 1) * LANES
                ]
        out_ref[...] = turned[...].astype(jnp.bfloat16)


def channelize(voltages, chan_counts, dests):
    band = 2 * dests
    streams, frames = voltages.shape[0], voltages.shape[2]
    step = 4 if band <= 64 else 2
    analysis, mixing = tables(band)
    width = max(LANES, 2 * band)
    payload = 2 * CAP * NSPEC * streams // LANES
    rows = step * 2 * frames
    kernel = functools.partial(channelizer, band, dests, streams, step)
    return pl.pallas_call(
        kernel,
        grid_spec=pltpu.PrefetchScalarGridSpec(
            num_scalar_prefetch=1,
            grid=(streams // step,),
            in_specs=[
                pl.BlockSpec((step, 1, frames, 2, FFT_LEN), lambda i, c: (i, 0, 0, 0, 0)),
                pl.BlockSpec(analysis.shape, lambda i, c: (0, 0), pipeline_mode=pl.Buffered(1)),
                pl.BlockSpec(mixing.shape, lambda i, c: (0, 0), pipeline_mode=pl.Buffered(1)),
            ],
            out_specs=pl.BlockSpec((dests, payload, LANES), lambda i, c: (0, 0, 0)),
            scratch_shapes=[
                pltpu.VMEM((rows, mixing.shape[1]), jnp.float32),
                pltpu.VMEM((width // LANES, 2 * NSPEC, LANES), jnp.float32),
                pltpu.VMEM((width // LANES, NSPEC * streams, LANES), jnp.float32),
                pltpu.VMEM((dests, payload, LANES), jnp.float32),
            ],
        ),
        out_shape=jax.ShapeDtypeStruct((dests, payload, LANES), jnp.bfloat16),
        compiler_params=pltpu.CompilerParams(vmem_limit_bytes=60 * 1024 * 1024),
        cost_estimate=pl.CostEstimate(
            flops=2 * streams * 2 * frames * FFT_LEN * analysis.shape[1],
            bytes_accessed=2 * voltages.size, transcendentals=0,
        ),
    )(chan_counts, voltages, jnp.asarray(analysis), jnp.asarray(mixing))


def correlator(direct, counts, where, dest_ref, *refs):
    out_ref, pre, post = refs[-3:]
    k = pl.program_id(0)
    time_len = pre.shape[1]
    total = pre.shape[2]

    @pl.when(k == 0)
    def _():
        if direct:
            own, other = refs[:2]
            sources, payload = own.shape[0], own.shape[1]
            tiles = payload // (2 * CAP)
            lane = lax.broadcasted_iota(jnp.int32, (payload, LANES), 1)
            left = lane < LANES // 2
            for h, ref in enumerate((own, other)):
                for q in range(sources // 2):
                    a = ref[2 * q].astype(jnp.float32)
                    b = ref[2 * q + 1].astype(jnp.float32)
                    first = jnp.where(left, a, jnp.roll(b, LANES // 2, axis=1))
                    second = jnp.where(left, jnp.roll(a, LANES // 2, axis=1), b)
                    for part in range(2 * CAP):
                        rows = slice(part * tiles, (part + 1) * tiles)
                        both = jnp.concatenate([first[rows], second[rows]], axis=0)
                        pre[part, h * NSPEC : (h + 1) * NSPEC, q * LANES : (q + 1) * LANES] = (
                            both.astype(jnp.bfloat16)
                        )
        else:
            pre[...] = refs[0][...]
        spot = lax.broadcasted_iota(jnp.int32, (total, total), 0)
        turn = jnp.where(spot == dest_ref[...], 1.0, 0.0).astype(jnp.bfloat16)
        ordered = lax.dot_general(
            pre[...].reshape(2 * CAP * time_len, total), turn, (((1,), (1,)), ((), ())),
            preferred_element_type=jnp.float32,
        )
        post[...] = ordered.astype(jnp.bfloat16).reshape(CAP, 2 * time_len, total)

    rows = out_ref.shape[3]
    every = post[k]
    near = post[k, :, pl.ds(pl.multiple_of(where[1] * rows, LANES), rows)]
    turned = jnp.concatenate([near[time_len:], -near[:time_len]], axis=0)
    valid = jnp.where(k < counts[where[0]], 1.0, 0.0) / jnp.float32(time_len)
    for part, left in enumerate((near, turned)):
        vis = lax.dot_general(
            left, every, (((0,), (0,)), ((), ())), preferred_element_type=jnp.float32
        )
        out_ref[0, 0, part] = (vis * valid).astype(jnp.bfloat16)


def correlate(own, other, dest, chan_counts, where, streams):
    sources = own.shape[0]
    total = sources * streams
    spread = LANES // streams
    direct = spread == 2
    if direct:
        operands = (own, other)
        specs = [pl.BlockSpec(own.shape, lambda k, c, w: (0, 0, 0))] * 2
    else:
        tiles = NSPEC // spread
        both = jnp.stack([own, other], axis=0).reshape(2, sources, 2 * CAP, tiles, spread, streams)
        both = both.transpose(2, 0, 3, 4, 1, 5).reshape(2 * CAP, 2 * NSPEC, total)
        operands = (both,)
        specs = [pl.BlockSpec(both.shape, lambda k, c, w: (0, 0, 0))]
    rows = total // 2
    return pl.pallas_call(
        functools.partial(correlator, direct),
        grid_spec=pltpu.PrefetchScalarGridSpec(
            num_scalar_prefetch=2,
            grid=(CAP,),
            in_specs=[pl.BlockSpec((1, total), lambda k, c, w: (0, 0))] + specs,
            out_specs=pl.BlockSpec((1, 1, 2, rows, total), lambda k, c, w: (0, k, 0, 0, 0)),
            scratch_shapes=[
                pltpu.VMEM((2 * CAP, 2 * NSPEC, total), jnp.bfloat16),
                pltpu.VMEM((CAP, 4 * NSPEC, total), jnp.bfloat16),
            ],
        ),
        out_shape=jax.ShapeDtypeStruct((1, CAP, 2, rows, total), jnp.bfloat16),
        compiler_params=pltpu.CompilerParams(vmem_limit_bytes=60 * 1024 * 1024),
    )(chan_counts, where, dest, *operands)


def body(voltages, station_map, chan_counts):
    dests = lax.axis_size("stn")
    streams = voltages.shape[0]
    outgoing = channelize(voltages, chan_counts, dests)
    own = lax.all_to_all(outgoing, "stn", split_axis=0, concat_axis=0, tiled=True)
    other = lax.ppermute(own, "blk", [(0, 1), (1, 0)])
    dest = (2 * station_map[:, None] + jnp.arange(2, dtype=jnp.int32)[None, :]).reshape(1, -1)
    where = jnp.stack([lax.axis_index("stn"), lax.axis_index("blk")]).astype(jnp.int32)
    return correlate(own, other, dest, chan_counts, where, streams)


def solution(mesh):
    return jax.shard_map(
        body,
        mesh=mesh,
        in_specs=(P("stn", "blk", None, None, None), P(), P()),
        out_specs=P("stn", None, None, "blk", None),
        check_vma=False,
    )
```

time: 1040 us -> 91.5 us (0.09); the launches traced: 1030 us -> 91.3 us
  other arithmetic: 422 us -> 0.79 us
  local copies, waits for them, and re-layouts: 373 us -> 1.6 us
  matrix products: 175 us -> 0 us
  Pallas kernels: 0 us -> 50.4 us
  blocking collectives: 0 us -> 24.6 us
  waiting for transfers between devices: 34 us -> 12.2 us
  between operations: 14.8 us -> 0.02 us
    add x3 -> x1, other arithmetic: 393 us -> 0.13 us  [body(): 2 * station_map[:, None] + jnp.arange(2, dtype=jnp.int32)[None, :]]
    dot_general x2 -> x0, matrix products: 175 us -> none  [the longest x1 168 us: direct_dft(): jnp.dot(rows_in, table, precision=lax.Precision.HIGHEST, preferred_elemen...]
    add x4 -> x1, local copies, waits for them, and re-layouts: 162 us -> 0.78 us  [body(): 2 * station_map[:, None] + jnp.arange(2, dtype=jnp.int32)[None, :]]
    dot_general x1 -> x0, local copies, waits for them, and re-layouts: 126 us -> none  [direct_dft(): jnp.dot(rows_in, table, precision=lax.Precision.HIGHEST, preferred_elemen...]
    unnamed x17 -> x6, local copies, waits for them, and re-layouts: 57.6 us -> 0.83 us
    pallas_call x0 -> x2, Pallas kernels: none -> 50.4 us  [the longest x1 42.8 us: channelize(): pl.pallas_call(kernel, grid_spec=pltpu.PrefetchScalarGridSpec(num_scalar_...]
    all_to_all x0 -> x1, blocking collectives: none -> 24.6 us  [body(): lax.all_to_all(outgoing, 'stn', split_axis=0, concat_axis=0, tiled=True)]
    all_gather x1 -> x0, waiting for transfers between devices: 20.9 us -> none  [body(): incoming = lax.all_gather(incoming, 'blk', axis=3, tiled=True)]
  transfers between devices with their start and end apart: 2 -> 1, of which waited for: 2 -> 1; matrix products, arithmetic and copies ran while one was open for 0% -> 2% of each run, Pallas kernels for 0% -> 0%
where the time goes in v1:
time: 91.5 us; the launch traced here: 91.3 us
  Pallas kernels  50.4 us (55%)
  blocking collectives  24.6 us (27%)
  waiting for transfers between devices  12.2 us (13%)
  local copies, waits for them, and re-layouts  1.6 us (2%)
  starting transfers between devices  1.52 us (2%)
    pallas_call x1, Pallas kernels, channelize(): pl.pallas_call(kernel, grid_spec=pltpu.PrefetchScalarGridSpec(num_scalar_...  42.8 us
    all_to_all x1, blocking collectives, body(): lax.all_to_all(outgoing, 'stn', split_axis=0, concat_axis=0, tiled=True)  24.6 us
    ppermute x1, waiting for transfers between devices, body(): other = lax.ppermute(own, 'blk', [(0, 1), (1, 0)])  12.2 us
    pallas_call x1, Pallas kernels, correlate(): pl.pallas_call(functools.partial(correlator, direct), grid_spec=pltpu.Pre...  7.63 us
  transfers between devices with their start and end apart: 1, of which 1 were waited for; matrix products, arithmetic and copies ran while one was open for 2% of the time, Pallas kernels for 0%

profile of v1, /device:TPU:0, one launch (start us, length us, event | category | flops | bytes accessed | tf_op | source)
XLA Modules:
  0.0 91.3 jit_solution(9986534856729515478)
XLA Ops:
  0.0 0.0 copy-start.2
  0.0 42.8 %shard_map.55 = bf16[16,144,128]{2,1,0:T(8,128)(2,1)} custom-call(s32[16]{0:T(128)} %counts.3, bf16[64,1,63,2,4096]{4,3,2,1,0:T(2,128)(2,1)} %v_ref.1, bf16[4096,256]{1,0:T(8,128)(2,1)} %constant.14.clone.u_ref, bf16[256,1024]{1,0:T(8,128)(2,1)} %constant.15.clone.w_ref), custom_call_target="tpu_custom_call" | custom-call | flops 16911433728 | bytes 66060288 | tf_op jit(solution)/shard_map/pallas_call | solution.py:147
  42.8 24.6 %all_to_all.5.refs_0_ = bf16[16,144,128]{2,1,0:T(8,128)(2,1)S(1)} all-to-all(bf16[16,144,128]{2,1,0:T(8,128)(2,1)} %shard_map.55), channel_id=1, replica_groups=mesh['stn'=16,'blk'=2] {'stn'}, dimensions={0} | all-to-all | bytes 1179648 | tf_op jit(solution)/shard_map/all_to_all | solution.py:258
  67.5 0.0 copy-start
  67.5 1.5 %collective-permute-start = (bf16[16,144,128]{2,1,0:T(8,128)(2,1)S(1)}, bf16[16,144,128]{2,1,0:T(8,128)(2,1)S(1)}, u32[]{:S(2)}, u32[]{:S(2)}) collective-permute-start(bf16[16,144,128]{2,1,0:T(8,128)(2,1)S(1)} %all_to_all.5.refs_0_), channel_id=1, source_target_pairs={{0,1},{1,0},{2,3},{3,2},{4,5},{5,4},{6,7},{7,6},{8,9},{9,8},{10,11... | collective-permute-start | bytes 1769480 | tf_op jit(solution)/shard_map/ppermute | solution.py:259
  69.0 0.0 copy-done.2
  69.0 0.1 iota_add_fusion
  69.1 0.8 add.26.dest_ref
  69.9 0.7 pad_add_fusion.where
  70.6 12.2 %collective-permute-done.refs_1_ = bf16[16,144,128]{2,1,0:T(8,128)(2,1)S(1)} collective-permute-done((bf16[16,144,128]{2,1,0:T(8,128)(2,1)S(1)}, bf16[16,144,128]{2,1,0:T(8,128)(2,1)S(1)}, u32[]{:S(2)}, u32[]{:S(2)}) %collective-permute-start) | collective-permute-done | bytes 589856 | tf_op jit(solution)/shard_map/ppermute | solution.py:259
  82.8 0.0 copy-done
  82.8 0.0 copy-start.1
  82.8 0.8 copy-done.1
  83.6 7.6 %shard_map.56 = bf16[1,3,2,512,1024]{4,3,2,1,0:T(8,128)(2,1)} custom-call(s32[16]{0:T(128)} %counts.3, s32[2]{0:T(128)} %pad_add_fusion.where, s32[1,1024]{1,0:T(1,128)} %add.26.dest_ref, bf16[16,144,128]{2,1,0:T(8,128)(2,1)} %copy-done, bf16[16,144,128]{2,1,0:T(8,128)(2,1)} %copy-done.1), custom_call_target="tpu_custom_call" | custom-call | tf_op jit(solution)/shard_map/pallas_call | solution.py:237
  (1 shorter events, 0.0 us)
Async XLA Ops:
  0.0 69.0 %copy-start.2 = (s32[512]{0:T(512)S(1)}, s32[512]{0:T(512)}, u32[]{:S(2)}) copy-start(s32[512]{0:T(512)} %param.6) | copy-start | bytes 6148
  67.5 15.4 %copy-start = (bf16[16,144,128]{2,1,0:T(8,128)(2,1)}, bf16[16,144,128]{2,1,0:T(8,128)(2,1)S(1)}, u32[]{:S(2)}) copy-start(bf16[16,144,128]{2,1,0:T(8,128)(2,1)S(1)} %all_to_all.5.refs_0_) | copy-start | bytes 1769476
  67.5 15.3 %collective-permute-start = (bf16[16,144,128]{2,1,0:T(8,128)(2,1)S(1)}, bf16[16,144,128]{2,1,0:T(8,128)(2,1)S(1)}, u32[]{:S(2)}, u32[]{:S(2)}) collective-permute-start(bf16[16,144,128]{2,1,0:T(8,128)(2,1)S(1)} %all_to_all.5.refs_0_), channel_id=1, source_target_pairs={{0,1},{1,0},{2,3},{3,2},{4,5},{5,4},{6,7},{7,6},{8,9},{9,8},{10,11... | collective-permute-start | bytes 1769480 | tf_op jit(solution)/shard_map/ppermute | solution.py:259
  82.8 0.8 copy-start.1

commit v2 on v1

v2 whole, which is shorter than its diff:
```python
import functools
import math

import jax
import jax.numpy as jnp
import ml_dtypes
import numpy as np
from jax import lax
from jax.experimental import pallas as pl
from jax.experimental.pallas import tpu as pltpu
from jax.sharding import PartitionSpec as P

FFT_LEN = 4096
TAPS = 16
CAP = 3
NSPEC = 48
LANES = 128


def prototype():
    span = TAPS * FFT_LEN
    points = np.arange(span, dtype=np.float64) + 0.5
    window = 0.5 - 0.5 * np.cos(2.0 * math.pi * points / span)
    shifted = math.pi * (points - span / 2.0) / FFT_LEN
    filt = np.sin(shifted) / shifted * window
    return (filt / np.sqrt(np.sum(filt * filt))).reshape(TAPS, FFT_LEN)


def frame_basis(band, count):
    limit = math.pi * (band + 0.1)
    terms = count + int(limit) + 60
    k = np.arange(terms, dtype=np.float64)
    diagonal = k * (k + 1) + (2 * k * (k + 1) - 1) / ((2 * k + 3) * (2 * k - 1)) * limit**2
    m = k[:-2]
    beside = (m + 2) * (m + 1) / ((2 * m + 3) * np.sqrt((2 * m + 1) * (2 * m + 5))) * limit**2
    matrix = np.diag(diagonal) + np.diag(beside, 2) + np.diag(beside, -2)
    _, vectors = np.linalg.eigh(matrix)
    x = (2 * np.arange(FFT_LEN) + 1.0) / FFT_LEN - 1
    legendre = np.zeros((terms, FFT_LEN))
    legendre[0] = 1.0
    legendre[1] = x
    for j in range(2, terms):
        legendre[j] = ((2 * j - 1) * x * legendre[j - 1] - (j - 1) * legendre[j - 2]) / j
    legendre *= np.sqrt((k + 0.5) * 2.0 / FFT_LEN)[:, None]
    return legendre.T @ vectors[:, :count]


SHIFTS = 4


def turn_lanes(value, shift):
    shift = shift % LANES
    return pltpu.roll(value, shift, axis=1) if shift else value


def packing(band):
    if 3 * (2 * band + 21) <= 2 * LANES:
        return 2 * band + 21, 2 * LANES, True
    count = -(-(2 * band + 32) // (LANES // 2)) * (LANES // 2)
    return count, -(-2 * count // LANES) * LANES, False


@functools.lru_cache(maxsize=4)
def tables(band):
    bf16 = ml_dtypes.bfloat16
    count, packed, triple = packing(band)
    basis = frame_basis(band, count)
    high = basis.astype(bf16)
    low = (basis - high.astype(np.float64)).astype(bf16)
    held = high.astype(np.float64) + low.astype(np.float64)
    lanes = -(-count // LANES) * LANES
    analysis = np.zeros((FFT_LEN, 2 * lanes), bf16)
    analysis[:, :count] = high
    analysis[:, lanes : lanes + count] = low

    phase = 2.0 * math.pi / FFT_LEN * (np.outer(np.arange(FFT_LEN), np.arange(band)) % FFT_LEN)
    wave = np.concatenate([np.cos(phase), -np.sin(phase)], axis=1)
    gram = held.T @ held
    taper = prototype()
    mixing = np.zeros((TAPS // SHIFTS, 2, packed, SHIFTS, 2 * band), bf16)
    for t in range(TAPS):
        real = np.linalg.solve(gram, held.T @ (taper[t][:, None] * wave))
        imag = np.concatenate([-real[:, band:], real[:, :band]], axis=1)
        for c, full in enumerate((real, imag)):
            part = mixing[t // SHIFTS, c, :, t % SHIFTS]
            top = full.astype(bf16)
            part[:count] = top
            part[count : 2 * count] = top
            if triple:
                part[2 * count : 3 * count] = (full - top.astype(np.float64)).astype(bf16)
    return analysis, mixing.reshape(-1, SHIFTS * 2 * band)


def channelizer(band, dests, streams, step, counts, v_ref, u_ref, w_ref, out_ref, y, p, x, turned):
    i = pl.program_id(0)
    last = pl.num_programs(0) - 1
    count, packed, triple = packing(band)
    lanes = u_ref.shape[1] // 2
    rows = 2 * v_ref.shape[2]
    reach = NSPEC + 8
    wide = max(1, 2 * band // LANES)

    def analyse():
        signal = v_ref[...].reshape(step * rows, FFT_LEN)
        coeff = jnp.dot(signal, u_ref[...], preferred_element_type=jnp.float32)
        coeff = coeff[:, :lanes] + coeff[:, lanes:]
        high = coeff.astype(jnp.bfloat16).astype(jnp.float32)
        low = coeff - high
        if triple:
            lane = lax.broadcasted_iota(jnp.int32, coeff.shape, 1)
            low = turn_lanes(low, count)
            spare = 2 * count - LANES
            y[0, : step * rows] = jnp.where(lane < count, high, low)
            y[1, : step * rows] = jnp.where(lane < spare, low, turn_lanes(high, spare))
        else:
            both = jnp.concatenate([high[:, :count], low[:, :count]], axis=1)
            for n in range(packed // LANES):
                y[n, : step * rows] = both[:, n * LANES : (n + 1) * LANES]

    def mix(block):
        taps = []
        for r in range(step):
            taps.append(jnp.concatenate([
                y[n, pl.ds(r * rows + 2 * SHIFTS * m + c, reach, stride=2), :]
                for m in range(TAPS // SHIFTS) for c in range(2) for n in range(packed // LANES)
            ], axis=1))
        taps = jnp.concatenate(taps, axis=0).astype(jnp.bfloat16)
        mixed = jnp.dot(taps, w_ref[...], preferred_element_type=jnp.float32)
        for n in range(mixed.shape[1] // LANES):
            p[n] = mixed[:, n * LANES : (n + 1) * LANES]
        for r in range(step):
            place = pl.ds(block * step + r, NSPEC, stride=streams)
            if 2 * band >= LANES:
                for n in range(wide):
                    x[n, place, :] = sum(
                        p[wide * h + n, pl.ds(r * reach + h, NSPEC), :] for h in range(SHIFTS)
                    )
            else:
                per = LANES // (2 * band)
                lane = lax.broadcasted_iota(jnp.int32, (NSPEC, LANES), 1)
                total = None
                for u in reversed(range(per)):
                    part = sum(
                        p[b, pl.ds(r * reach + b * per + u, NSPEC), :] for b in range(SHIFTS // per)
                    )
                    total = part if total is None else jnp.where(
                        lane < 2 * band * (u + 1), part, total
                    )
                whole = total
                for u in range(1, per):
                    whole = whole + turn_lanes(total, -2 * band * u)
                x[0, place, :] = whole

    @pl.when(i < last)
    def _():
        mix(jnp.maximum(i - 1, 0))
        analyse()

    @pl.when(i == last)
    def _():
        mix(i - 1)
        lane = lax.broadcasted_iota(jnp.int32, (8, wide * LANES), 1)
        row = lax.broadcasted_iota(jnp.int32, (8, wide * LANES), 0)
        slot = row // 2
        base = (row % 2) * band
        picks = []
        offset = jnp.int32(0)
        for d in range(dests):
            held = counts[d]
            want = offset + jnp.minimum(slot, held - 1) + base
            picks.append(jnp.where((lane == want) & (row < 2 * CAP), 1.0, 0.0))
            offset = offset + held
        pick = jnp.concatenate(picks, axis=0).astype(jnp.bfloat16)
        spectra = jnp.concatenate([x[n] for n in range(wide)], axis=1)
        out = lax.dot_general(
            pick, spectra.astype(jnp.bfloat16), (((1,), (1,)), ((), ())),
            preferred_element_type=jnp.float32,
        )
        tiles = NSPEC * streams // LANES
        for d in range(dests):
            for t in range(tiles):
                turned[d, pl.ds(t, 2 * CAP, stride=tiles), :] = out[
                    8 * d : 8 * d + 2 * CAP, t * LANES : (t + 1) * LANES
                ]
        out_ref[...] = turned[...].astype(jnp.bfloat16)


def channelize(voltages, chan_counts, dests, start, streams):
    band = 2 * dests
    frames = voltages.shape[2]
    step = 4 if band <= 64 else 2
    analysis, mixing = tables(band)
    packed = packing(band)[1]
    payload = 2 * CAP * NSPEC * streams // LANES
    steps = streams // step
    first = start // step
    kernel = functools.partial(channelizer, band, dests, streams, step)
    return pl.pallas_call(
        kernel,
        grid_spec=pltpu.PrefetchScalarGridSpec(
            num_scalar_prefetch=1,
            grid=(steps + 1,),
            in_specs=[
                pl.BlockSpec(
                    (step, 1, frames, 2, FFT_LEN),
                    lambda i, c: (first + jnp.minimum(i, steps - 1), 0, 0, 0, 0),
                ),
                pl.BlockSpec(analysis.shape, lambda i, c: (0, 0), pipeline_mode=pl.Buffered(1)),
                pl.BlockSpec(mixing.shape, lambda i, c: (0, 0), pipeline_mode=pl.Buffered(1)),
            ],
            out_specs=pl.BlockSpec((dests, payload, LANES), lambda i, c: (0, 0, 0)),
            scratch_shapes=[
                pltpu.VMEM((packed // LANES, step * 2 * frames + 16, LANES), jnp.float32),
                pltpu.VMEM((SHIFTS * 2 * band // LANES, step * (NSPEC + 8), LANES), jnp.float32),
                pltpu.VMEM((max(1, 2 * band // LANES), NSPEC * streams, LANES), jnp.float32),
                pltpu.VMEM((dests, payload, LANES), jnp.float32),
            ],
        ),
        out_shape=jax.ShapeDtypeStruct((dests, payload, LANES), jnp.bfloat16),
        compiler_params=pltpu.CompilerParams(vmem_limit_bytes=60 * 1024 * 1024),
        cost_estimate=pl.CostEstimate(
            flops=2 * streams * 2 * frames * FFT_LEN * analysis.shape[1],
            bytes_accessed=2 * 2 * frames * FFT_LEN * streams, transcendentals=0,
        ),
    )(chan_counts, voltages, jnp.asarray(analysis), jnp.asarray(mixing))


def correlator(direct, counts, where, dest_ref, *refs):
    out_ref, pre, post = refs[-3:]
    k = pl.program_id(0)
    time_len = pre.shape[1]
    total = pre.shape[2]

    @pl.when(k == 0)
    def _():
        if direct:
            base = 0
            for c in range(len(refs[:-3]) // 2):
                for h, ref in enumerate(refs[2 * c : 2 * c + 2]):
                    sources, payload = ref.shape[0], ref.shape[1]
                    tiles = payload // (2 * CAP)
                    spread = NSPEC // tiles
                    width = LANES // spread
                    lane = lax.broadcasted_iota(jnp.int32, (payload, LANES), 1)
                    for q in range(sources // spread):
                        parts = [ref[spread * q + a].astype(jnp.float32) for a in range(spread)]
                        groups = []
                        for g in range(spread):
                            group = None
                            for a in range(spread):
                                moved = turn_lanes(parts[a], (a - g) * width)
                                group = moved if a == 0 else jnp.where(
                                    lane < a * width, group, moved
                                )
                            groups.append(group)
                        for part in range(2 * CAP):
                            rows = slice(part * tiles, (part + 1) * tiles)
                            both = jnp.concatenate([group[rows] for group in groups], axis=0)
                            pre[
                                part, h * NSPEC : (h + 1) * NSPEC,
                                base + q * LANES : base + (q + 1) * LANES,
                            ] = both.astype(jnp.bfloat16)
                base = base + sources * width
        else:
            pre[...] = refs[0][...]
        spot = lax.broadcasted_iota(jnp.int32, (total, total), 0)
        turn = jnp.where(spot == dest_ref[...], 1.0, 0.0).astype(jnp.bfloat16)
        ordered = lax.dot_general(
            pre[...].reshape(2 * CAP * time_len, total), turn, (((1,), (1,)), ((), ())),
            preferred_element_type=jnp.float32,
        )
        post[...] = ordered.astype(jnp.bfloat16).reshape(CAP, 2 * time_len, total)

    rows = out_ref.shape[3]
    every = post[k]
    near = post[k, :, pl.ds(pl.multiple_of(where[1] * rows, LANES), rows)]
    turned = jnp.concatenate([near[time_len:], -near[:time_len]], axis=0)
    valid = jnp.where(k < counts[where[0]], 1.0, 0.0) / jnp.float32(time_len)
    for part, left in enumerate((near, turned)):
        vis = lax.dot_general(
            left, every, (((0,), (0,)), ((), ())), preferred_element_type=jnp.float32
        )
        out_ref[0, 0, part] = (vis * valid).astype(jnp.bfloat16)


def correlate(pairs, dest, chan_counts, where, total):
    sources, payload = pairs[0][0].shape[:2]
    spread = 2 * CAP * NSPEC // payload
    direct = spread <= 4
    if direct:
        operands = [half for pair in pairs for half in pair]
    else:
        operands = []
        for pair in pairs:
            both = jnp.stack(pair).reshape(2, sources, 2 * CAP, NSPEC // spread, spread, -1)
            both = both.transpose(2, 0, 3, 4, 1, 5).reshape(2 * CAP, 2 * NSPEC, -1)
            operands.append(both)
        operands = [jnp.concatenate(operands, axis=2)]
    specs = [pl.BlockSpec(a.shape, lambda k, c, w: (0, 0, 0)) for a in operands]
    rows = total // 2
    return pl.pallas_call(
        functools.partial(correlator, direct),
        grid_spec=pltpu.PrefetchScalarGridSpec(
            num_scalar_prefetch=2,
            grid=(CAP,),
            in_specs=[pl.BlockSpec((1, total), lambda k, c, w: (0, 0))] + specs,
            out_specs=pl.BlockSpec((1, 1, 2, rows, total), lambda k, c, w: (0, k, 0, 0, 0)),
            scratch_shapes=[
                pltpu.VMEM((2 * CAP, 2 * NSPEC, total), jnp.bfloat16),
                pltpu.VMEM((CAP, 4 * NSPEC, total), jnp.bfloat16),
            ],
        ),
        out_shape=jax.ShapeDtypeStruct((1, CAP, 2, rows, total), jnp.bfloat16),
        compiler_params=pltpu.CompilerParams(vmem_limit_bytes=60 * 1024 * 1024),
    )(chan_counts, where, dest, *operands)


def body(voltages, station_map, chan_counts):
    dests = lax.axis_size("stn")
    streams = voltages.shape[0]
    sizes = (32, 32) if streams == 64 else (streams,)
    pairs = []
    places = []
    start = 0
    dest = (2 * station_map[:, None] + jnp.arange(2, dtype=jnp.int32)[None, :]).reshape(dests, -1)
    for size in sizes:
        outgoing = channelize(voltages, chan_counts, dests, start, size)
        own = lax.all_to_all(outgoing, "stn", split_axis=0, concat_axis=0, tiled=True)
        other = lax.ppermute(own, "blk", [(0, 1), (1, 0)])
        pairs.append((own, other))
        places.append(dest[:, start : start + size].reshape(1, -1))
        start = start + size
    dest = jnp.concatenate(places, axis=1)
    where = jnp.stack([lax.axis_index("stn"), lax.axis_index("blk")]).astype(jnp.int32)
    return correlate(pairs, dest, chan_counts, where, dests * streams)


def solution(mesh):
    return jax.shard_map(
        body,
        mesh=mesh,
        in_specs=(P("stn", "blk", None, None, None), P(), P()),
        out_specs=P("stn", None, None, "blk", None),
        check_vma=False,
    )
```

time: 91.5 us -> 85.3 us (0.932)
  blocking collectives: 24.6 us -> 0 us
  starting transfers between devices: 1.52 us -> 16.4 us
  waiting for transfers between devices: 12.2 us -> 14.4 us
    all_to_all x1 -> x0, blocking collectives: 24.6 us -> none  [body(): lax.all_to_all(outgoing, 'stn', split_axis=0, concat_axis=0, tiled=True)]
    all_to_all x0 -> x2, starting transfers between devices: none -> 13.4 us  [body(): lax.all_to_all(outgoing, 'stn', split_axis=0, concat_axis=0, tiled=True)]
    all_to_all x0 -> x2, waiting for transfers between devices: none -> 8.66 us  [body(): lax.all_to_all(outgoing, 'stn', split_axis=0, concat_axis=0, tiled=True)]
    ppermute x1 -> x2, waiting for transfers between devices: 12.2 us -> 5.72 us  [body(): other = lax.ppermute(own, 'blk', [(0, 1), (1, 0)])]
    ppermute x1 -> x2, starting transfers between devices: 1.52 us -> 3.05 us  [body(): other = lax.ppermute(own, 'blk', [(0, 1), (1, 0)])]
    pallas_call x1 -> x2, Pallas kernels: 42.8 us -> 42.9 us  [channelize(): pl.pallas_call(kernel, grid_spec=pltpu.PrefetchScalarGridSpec(num_scalar_...]
  transfers between devices with their start and end apart: 1 -> 4, of which waited for: 1 -> 2; matrix products, arithmetic and copies ran while one was open for 2% -> 2% of each run, Pallas kernels for 0% -> 25%
where the time goes in v2:
time: 85.3 us; the launch traced here: 84.5 us
  Pallas kernels  51 us (60%)
  starting transfers between devices  16.4 us (19%)
  waiting for transfers between devices  14.4 us (17%)
  other arithmetic  1.32 us (2%)
  local copies, waits for them, and re-layouts  1.31 us (2%)
    pallas_call x2, Pallas kernels, channelize(): pl.pallas_call(kernel, grid_spec=pltpu.PrefetchScalarGridSpec(num_scalar_...  42.9 us
    all_to_all x2, starting transfers between devices, body(): lax.all_to_all(outgoing, 'stn', split_axis=0, concat_axis=0, tiled=True)  13.4 us
    all_to_all x2, waiting for transfers between devices, body(): lax.all_to_all(outgoing, 'stn', split_axis=0, concat_axis=0, tiled=True)  8.66 us
    pallas_call x1, Pallas kernels, correlate(): pl.pallas_call(functools.partial(correlator, direct), grid_spec=pltpu.Pre...  8.07 us
    ppermute x2, waiting for transfers between devices, body(): other = lax.ppermute(own, 'blk', [(0, 1), (1, 0)])  5.72 us
    ppermute x2, starting transfers between devices, body(): other = lax.ppermute(own, 'blk', [(0, 1), (1, 0)])  3.05 us
  transfers between devices with their start and end apart: 4, of which 2 were waited for; matrix products, arithmetic and copies ran while one was open for 2% of the time, Pallas kernels for 25%

profile of v2, /device:TPU:0, one launch (start us, length us, event | category | flops | bytes accessed | tf_op | source)
XLA Modules:
  0.0 84.5 jit_solution(16446964007002106098)
XLA Ops:
  0.0 21.4 %shard_map.55 = bf16[16,72,128]{2,1,0:T(8,128)(2,1)} custom-call(s32[16]{0:T(128)} %counts.5, bf16[64,1,63,2,4096]{4,3,2,1,0:T(2,128)(2,1)} %v_ref.3, bf16[4096,256]{1,0:T(8,128)(2,1)} %constant.14.clone.u_ref, bf16[2048,256]{1,0:T(8,128)(2,1)} %constant.15.clone.w_ref), custom_call_target="tpu_custom_call" | custom-call | flops 8455716864 | bytes 33030144 | tf_op jit(solution)/shard_map/pallas_call | solution.py:198
  21.4 7.4 %all-to-all-start = ((bf16[16,72,128]{2,1,0:T(8,128)(2,1)}), bf16[16,72,128]{2,1,0:T(8,128)(2,1)S(1)}, u32[]{:S(2)}, u32[]{:S(2)}) async-start(bf16[16,72,128]{2,1,0:T(8,128)(2,1)} %shard_map.55), calls=%async_computation | async-start | bytes 589824 | tf_op jit(solution)/shard_map/all_to_all | solution.py:328
  28.8 0.0 copy-start.4
  28.8 21.5 %shard_map.56 = bf16[16,72,128]{2,1,0:T(8,128)(2,1)} custom-call(s32[16]{0:T(128)} %counts.5, bf16[64,1,63,2,4096]{4,3,2,1,0:T(2,128)(2,1)} %v_ref.3, bf16[4096,256]{1,0:T(8,128)(2,1)} %constant.14.clone.u_ref, bf16[2048,256]{1,0:T(8,128)(2,1)} %constant.15.clone.w_ref), custom_call_target="tpu_custom_call" | custom-call | flops 8455716864 | bytes 33030144 | tf_op jit(solution)/shard_map/pallas_call | solution.py:198
  50.3 0.0 all-to-all-done.refs_0_
  50.3 0.0 copy-start
  50.3 6.0 %all-to-all-start.1 = ((bf16[16,72,128]{2,1,0:T(8,128)(2,1)}), bf16[16,72,128]{2,1,0:T(8,128)(2,1)S(1)}, u32[]{:S(2)}, u32[]{:S(2)}) async-start(bf16[16,72,128]{2,1,0:T(8,128)(2,1)} %shard_map.56), calls=%async_computation.1 | async-start | bytes 589824 | tf_op jit(solution)/shard_map/all_to_all | solution.py:328
  56.3 0.0 copy-done.4
  56.3 0.1 add.22
  56.4 0.1 copy.8
  56.5 0.1 add.26
  56.6 0.1 broadcast_add_fusion
  56.7 1.5 %collective-permute-start = (bf16[16,72,128]{2,1,0:T(8,128)(2,1)S(1)}, bf16[16,72,128]{2,1,0:T(8,128)(2,1)S(1)}, u32[]{:S(2)}, u32[]{:S(2)}) collective-permute-start(bf16[16,72,128]{2,1,0:T(8,128)(2,1)S(1)} %all-to-all-done.refs_0_), channel_id=1, source_target_pairs={{0,1},{1,0},{2,3},{3,2},{4,5},{5,4},{6,7},{7,6},{8,9},{9,8},{10,11... | collective-permute-start | bytes 884744 | tf_op jit(solution)/shard_map/ppermute | solution.py:329
  58.2 8.7 %all-to-all-done.1.refs_2_ = bf16[16,72,128]{2,1,0:T(8,128)(2,1)S(1)} async-done(((bf16[16,72,128]{2,1,0:T(8,128)(2,1)}), bf16[16,72,128]{2,1,0:T(8,128)(2,1)S(1)}, u32[]{:S(2)}, u32[]{:S(2)}) %all-to-all-start.1) | async-done | bytes 294944 | tf_op jit(solution)/shard_map/all_to_all | solution.py:328
  66.9 0.0 copy-start.1
  66.9 1.5 %collective-permute-start.1 = (bf16[16,72,128]{2,1,0:T(8,128)(2,1)S(1)}, bf16[16,72,128]{2,1,0:T(8,128)(2,1)S(1)}, u32[]{:S(2)}, u32[]{:S(2)}) collective-permute-start(bf16[16,72,128]{2,1,0:T(8,128)(2,1)S(1)} %all-to-all-done.1.refs_2_), channel_id=1, source_target_pairs={{0,1},{1,0},{2,3},{3,2},{4,5},{5,4},{6,7},{7,6},{8,9},{9,8},{10,11... | collective-permute-start | bytes 884744 | tf_op jit(solution)/shard_map/ppermute | solution.py:329
  68.4 0.1 copy.9
  68.5 0.1 reshape.13
  68.6 0.1 copy.10
  68.6 0.1 reshape.14
  68.7 0.7 pad_add_fusion.1.where
  69.4 0.6 pad_add_fusion.dest_ref
  70.0 0.0 collective-permute-done.refs_1_
  70.0 0.0 copy-start.2
  70.0 5.7 %collective-permute-done.1.refs_3_ = bf16[16,72,128]{2,1,0:T(8,128)(2,1)S(1)} collective-permute-done((bf16[16,72,128]{2,1,0:T(8,128)(2,1)S(1)}, bf16[16,72,128]{2,1,0:T(8,128)(2,1)S(1)}, u32[]{:S(2)}, u32[]{:S(2)}) %collective-permute-start.1) | collective-permute-done | bytes 294944 | tf_op jit(solution)/shard_map/ppermute | solution.py:329
  75.7 0.0 copy-done
  75.7 0.0 copy-done.1
  75.7 0.0 copy-done.2
  75.7 0.0 copy-start.3
  75.7 0.7 copy-done.3
  76.4 8.1 %shard_map.57 = bf16[1,3,2,512,1024]{4,3,2,1,0:T(8,128)(2,1)} custom-call(s32[16]{0:T(128)} %counts.5, s32[2]{0:T(128)} %pad_add_fusion.1.where, s32[1,1024]{1,0:T(1,128)} %pad_add_fusion.dest_ref, bf16[16,72,128]{2,1,0:T(8,128)(2,1)} %copy-done, bf16[16,72,128]{2,1,0:T(8,128)(2,1)} %copy-done.2, bf16[16,72,128]{2,1,0:T(8,128)(2,1)} %copy-done.1, ...), custom_call_target="tpu_custom_call" | custom-call | tf_op jit(solution)/shard_map/pallas_call | solution.py:301
  (4 shorter events, 0.0 us)
Async XLA Ops:
  21.4 28.9 %all-to-all-start = ((bf16[16,72,128]{2,1,0:T(8,128)(2,1)}), bf16[16,72,128]{2,1,0:T(8,128)(2,1)S(1)}, u32[]{:S(2)}, u32[]{:S(2)}) async-start(bf16[16,72,128]{2,1,0:T(8,128)(2,1)} %shard_map.55), calls=%async_computation | async-start | bytes 589824 | tf_op jit(solution)/shard_map/all_to_all | solution.py:328
  28.8 27.6 %copy-start.4 = (s32[512]{0:T(512)S(1)}, s32[512]{0:T(512)}, u32[]{:S(2)}) copy-start(s32[512]{0:T(512)} %param.6) | copy-start | bytes 6148
  50.3 25.4 %copy-start = (bf16[16,72,128]{2,1,0:T(8,128)(2,1)}, bf16[16,72,128]{2,1,0:T(8,128)(2,1)S(1)}, u32[]{:S(2)}) copy-start(bf16[16,72,128]{2,1,0:T(8,128)(2,1)S(1)} %all-to-all-done.refs_0_) | copy-start | bytes 884740
  50.3 16.6 %all-to-all-start.1 = ((bf16[16,72,128]{2,1,0:T(8,128)(2,1)}), bf16[16,72,128]{2,1,0:T(8,128)(2,1)S(1)}, u32[]{:S(2)}, u32[]{:S(2)}) async-start(bf16[16,72,128]{2,1,0:T(8,128)(2,1)} %shard_map.56), calls=%async_computation.1 | async-start | bytes 589824 | tf_op jit(solution)/shard_map/all_to_all | solution.py:328
  56.7 13.3 %collective-permute-start = (bf16[16,72,128]{2,1,0:T(8,128)(2,1)S(1)}, bf16[16,72,128]{2,1,0:T(8,128)(2,1)S(1)}, u32[]{:S(2)}, u32[]{:S(2)}) collective-permute-start(bf16[16,72,128]{2,1,0:T(8,128)(2,1)S(1)} %all-to-all-done.refs_0_), channel_id=1, source_target_pairs={{0,1},{1,0},{2,3},{3,2},{4,5},{5,4},{6,7},{7,6},{8,9},{9,8},{10,11... | collective-permute-start | bytes 884744 | tf_op jit(solution)/shard_map/ppermute | solution.py:329
  66.9 8.8 %copy-start.1 = (bf16[16,72,128]{2,1,0:T(8,128)(2,1)}, bf16[16,72,128]{2,1,0:T(8,128)(2,1)S(1)}, u32[]{:S(2)}) copy-start(bf16[16,72,128]{2,1,0:T(8,128)(2,1)S(1)} %all-to-all-done.1.refs_2_) | copy-start | bytes 884740
  66.9 8.8 %collective-permute-start.1 = (bf16[16,72,128]{2,1,0:T(8,128)(2,1)S(1)}, bf16[16,72,128]{2,1,0:T(8,128)(2,1)S(1)}, u32[]{:S(2)}, u32[]{:S(2)}) collective-permute-start(bf16[16,72,128]{2,1,0:T(8,128)(2,1)S(1)} %all-to-all-done.1.refs_2_), channel_id=1, source_target_pairs={{0,1},{1,0},{2,3},{3,2},{4,5},{5,4},{6,7},{7,6},{8,9},{9,8},{10,11... | collective-permute-start | bytes 884744 | tf_op jit(solution)/shard_map/ppermute | solution.py:329
  70.0 5.7 %copy-start.2 = (bf16[16,72,128]{2,1,0:T(8,128)(2,1)}, bf16[16,72,128]{2,1,0:T(8,128)(2,1)S(1)}, u32[]{:S(2)}) copy-start(bf16[16,72,128]{2,1,0:T(8,128)(2,1)S(1)} %collective-permute-done.refs_1_) | copy-start | bytes 884740
  75.7 0.7 copy-start.3

commit v3 on v2

--- a/solution.py
+++ b/solution.py
@@ -91,17 +91,33 @@
     return analysis, mixing.reshape(-1, SHIFTS * 2 * band)
 
 
-def channelizer(band, dests, streams, step, counts, v_ref, u_ref, w_ref, out_ref, y, p, x, turned):
+def channelizer(
+    band, dests, first, streams, step, counts, v_ref, u_hbm, w_hbm, out_ref,
+    held, u_ref, w_ref, y, p, x, turned, arrived,
+):
     i = pl.program_id(0)
     last = pl.num_programs(0) - 1
     count, packed, triple = packing(band)
     lanes = u_ref.shape[1] // 2
     rows = 2 * v_ref.shape[2]
+    tables_in = [
+        pltpu.make_async_copy(u_hbm, u_ref, arrived.at[2]),
+        pltpu.make_async_copy(w_hbm, w_ref, arrived.at[3]),
+    ]
+
+    def fetch(block):
+        slot = block % 2
+        return pltpu.make_async_copy(
+            v_ref.at[pl.ds(first + block * step, step), 0],
+            held.at[slot, :, :, :, pl.ds(0, FFT_LEN)],
+            arrived.at[slot],
+        )
+
     reach = NSPEC + 8
     wide = max(1, 2 * band // LANES)
 
     def analyse():
-        signal = v_ref[...].reshape(step * rows, FFT_LEN)
+        signal = held[i % 2].reshape(step * rows, FFT_LEN + LANES)[:, :FFT_LEN]
         coeff = jnp.dot(signal, u_ref[...], preferred_element_type=jnp.float32)
         coeff = coeff[:, :lanes] + coeff[:, lanes:]
         high = coeff.astype(jnp.bfloat16).astype(jnp.float32)
@@ -151,8 +167,24 @@
                     whole = whole + turn_lanes(total, -2 * band * u)
                 x[0, place, :] = whole
 
+    @pl.when(i == 0)
+    def _():
+        fetch(0).start()
+        for copy in tables_in:
+            copy.start()
+
+    @pl.when(i + 1 < last)
+    def _():
+        fetch(i + 1).start()
+
+    @pl.when(i == 0)
+    def _():
+        for copy in tables_in:
+            copy.wait()
+
     @pl.when(i < last)
     def _():
+        fetch(i).wait()
         mix(jnp.maximum(i - 1, 0))
         analyse()
 
@@ -193,27 +225,23 @@
     packed = packing(band)[1]
     payload = 2 * CAP * NSPEC * streams // LANES
     steps = streams // step
-    first = start // step
-    kernel = functools.partial(channelizer, band, dests, streams, step)
+    kernel = functools.partial(channelizer, band, dests, start, streams, step)
     return pl.pallas_call(
         kernel,
         grid_spec=pltpu.PrefetchScalarGridSpec(
             num_scalar_prefetch=1,
             grid=(steps + 1,),
-            in_specs=[
-                pl.BlockSpec(
-                    (step, 1, frames, 2, FFT_LEN),
-                    lambda i, c: (first + jnp.minimum(i, steps - 1), 0, 0, 0, 0),
-                ),
-                pl.BlockSpec(analysis.shape, lambda i, c: (0, 0), pipeline_mode=pl.Buffered(1)),
-                pl.BlockSpec(mixing.shape, lambda i, c: (0, 0), pipeline_mode=pl.Buffered(1)),
-            ],
+            in_specs=[pl.BlockSpec(memory_space=pl.ANY)] * 3,
             out_specs=pl.BlockSpec((dests, payload, LANES), lambda i, c: (0, 0, 0)),
             scratch_shapes=[
+                pltpu.VMEM((2, step, frames, 2, FFT_LEN + LANES), jnp.bfloat16),
+                pltpu.VMEM(analysis.shape, jnp.bfloat16),
+                pltpu.VMEM(mixing.shape, jnp.bfloat16),
                 pltpu.VMEM((packed // LANES, step * 2 * frames + 16, LANES), jnp.float32),
                 pltpu.VMEM((SHIFTS * 2 * band // LANES, step * (NSPEC + 8), LANES), jnp.float32),
                 pltpu.VMEM((max(1, 2 * band // LANES), NSPEC * streams, LANES), jnp.float32),
                 pltpu.VMEM((dests, payload, LANES), jnp.float32),
+                pltpu.SemaphoreType.DMA((4,)),
             ],
         ),
         out_shape=jax.ShapeDtypeStruct((dests, payload, LANES), jnp.bfloat16),

time: 85.3 us -> 84.7 us (level)
  no operation moved by 1% of the time
where the time goes in v3:
time: 84.7 us; the launch traced here: 84 us
  Pallas kernels  50.4 us (60%)
  starting transfers between devices  16.4 us (19%)
  waiting for transfers between devices  14.4 us (17%)
  other arithmetic  1.32 us (2%)
  local copies, waits for them, and re-layouts  1.31 us (2%)
    pallas_call x2, Pallas kernels, channelize(): pl.pallas_call(kernel, grid_spec=pltpu.PrefetchScalarGridSpec(num_scalar_...  42.3 us
    all_to_all x2, starting transfers between devices, body(): lax.all_to_all(outgoing, 'stn', split_axis=0, concat_axis=0, tiled=True)  13.4 us
    all_to_all x2, waiting for transfers between devices, body(): lax.all_to_all(outgoing, 'stn', split_axis=0, concat_axis=0, tiled=True)  8.66 us
    pallas_call x1, Pallas kernels, correlate(): pl.pallas_call(functools.partial(correlator, direct), grid_spec=pltpu.Pre...  8.07 us
    ppermute x2, waiting for transfers between devices, body(): other = lax.ppermute(own, 'blk', [(0, 1), (1, 0)])  5.72 us
    ppermute x2, starting transfers between devices, body(): other = lax.ppermute(own, 'blk', [(0, 1), (1, 0)])  3.05 us
  transfers between devices with their start and end apart: 4, of which 2 were waited for; matrix products, arithmetic and copies ran while one was open for 2% of the time, Pallas kernels for 25%

profile of v3, /device:TPU:0, one launch (start us, length us, event | category | flops | bytes accessed | tf_op | source)
XLA Modules:
  0.0 84.0 jit_solution(6226028979434944092)
XLA Ops:
  0.0 21.1 %shard_map.55 = bf16[16,72,128]{2,1,0:T(8,128)(2,1)} custom-call(s32[16]{0:T(128)} %counts.5, bf16[64,1,63,2,4096]{4,3,2,1,0:T(2,128)(2,1)} %v_ref.3, bf16[4096,256]{1,0:T(8,128)(2,1)} %constant.14.clone.u_hbm, bf16[2048,256]{1,0:T(8,128)(2,1)} %constant.15.clone.w_hbm), custom_call_target="tpu_custom_call" | custom-call | flops 8455716864 | bytes 33030144 | tf_op jit(solution)/shard_map/pallas_call | solution.py:229
  21.1 7.4 %all-to-all-start = ((bf16[16,72,128]{2,1,0:T(8,128)(2,1)}), bf16[16,72,128]{2,1,0:T(8,128)(2,1)S(1)}, u32[]{:S(2)}, u32[]{:S(2)}) async-start(bf16[16,72,128]{2,1,0:T(8,128)(2,1)} %shard_map.55), calls=%async_computation | async-start | bytes 589824 | tf_op jit(solution)/shard_map/all_to_all | solution.py:356
  28.5 0.0 copy-start.4
  28.5 21.2 %shard_map.56 = bf16[16,72,128]{2,1,0:T(8,128)(2,1)} custom-call(s32[16]{0:T(128)} %counts.5, bf16[64,1,63,2,4096]{4,3,2,1,0:T(2,128)(2,1)} %v_ref.3, bf16[4096,256]{1,0:T(8,128)(2,1)} %constant.14.clone.u_hbm, bf16[2048,256]{1,0:T(8,128)(2,1)} %constant.15.clone.w_hbm), custom_call_target="tpu_custom_call" | custom-call | flops 8455716864 | bytes 33030144 | tf_op jit(solution)/shard_map/pallas_call | solution.py:229
  49.7 0.0 all-to-all-done.refs_0_
  49.7 0.0 copy-start
  49.8 6.0 %all-to-all-start.1 = ((bf16[16,72,128]{2,1,0:T(8,128)(2,1)}), bf16[16,72,128]{2,1,0:T(8,128)(2,1)S(1)}, u32[]{:S(2)}, u32[]{:S(2)}) async-start(bf16[16,72,128]{2,1,0:T(8,128)(2,1)} %shard_map.56), calls=%async_computation.1 | async-start | bytes 589824 | tf_op jit(solution)/shard_map/all_to_all | solution.py:356
  55.8 0.0 copy-done.4
  55.8 0.1 add.22
  55.9 0.1 copy.8
  56.0 0.1 add.26
  56.1 0.1 broadcast_add_fusion
  56.2 1.5 %collective-permute-start = (bf16[16,72,128]{2,1,0:T(8,128)(2,1)S(1)}, bf16[16,72,128]{2,1,0:T(8,128)(2,1)S(1)}, u32[]{:S(2)}, u32[]{:S(2)}) collective-permute-start(bf16[16,72,128]{2,1,0:T(8,128)(2,1)S(1)} %all-to-all-done.refs_0_), channel_id=1, source_target_pairs={{0,1},{1,0},{2,3},{3,2},{4,5},{5,4},{6,7},{7,6},{8,9},{9,8},{10,11... | collective-permute-start | bytes 884744 | tf_op jit(solution)/shard_map/ppermute | solution.py:357
  57.7 8.7 %all-to-all-done.1.refs_2_ = bf16[16,72,128]{2,1,0:T(8,128)(2,1)S(1)} async-done(((bf16[16,72,128]{2,1,0:T(8,128)(2,1)}), bf16[16,72,128]{2,1,0:T(8,128)(2,1)S(1)}, u32[]{:S(2)}, u32[]{:S(2)}) %all-to-all-start.1) | async-done | bytes 294944 | tf_op jit(solution)/shard_map/all_to_all | solution.py:356
  66.4 0.0 copy-start.1
  66.4 1.5 %collective-permute-start.1 = (bf16[16,72,128]{2,1,0:T(8,128)(2,1)S(1)}, bf16[16,72,128]{2,1,0:T(8,128)(2,1)S(1)}, u32[]{:S(2)}, u32[]{:S(2)}) collective-permute-start(bf16[16,72,128]{2,1,0:T(8,128)(2,1)S(1)} %all-to-all-done.1.refs_2_), channel_id=1, source_target_pairs={{0,1},{1,0},{2,3},{3,2},{4,5},{5,4},{6,7},{7,6},{8,9},{9,8},{10,11... | collective-permute-start | bytes 884744 | tf_op jit(solution)/shard_map/ppermute | solution.py:357
  67.9 0.1 copy.9
  67.9 0.1 reshape.13
  68.0 0.1 copy.10
  68.1 0.1 reshape.14
  68.2 0.7 pad_add_fusion.1.where
  68.8 0.6 pad_add_fusion.dest_ref
  69.4 0.0 collective-permute-done.refs_1_
  69.4 0.0 copy-start.2
  69.4 5.7 %collective-permute-done.1.refs_3_ = bf16[16,72,128]{2,1,0:T(8,128)(2,1)S(1)} collective-permute-done((bf16[16,72,128]{2,1,0:T(8,128)(2,1)S(1)}, bf16[16,72,128]{2,1,0:T(8,128)(2,1)S(1)}, u32[]{:S(2)}, u32[]{:S(2)}) %collective-permute-start.1) | collective-permute-done | bytes 294944 | tf_op jit(solution)/shard_map/ppermute | solution.py:357
  75.2 0.0 copy-done
  75.2 0.0 copy-done.1
  75.2 0.0 copy-done.2
  75.2 0.0 copy-start.3
  75.2 0.7 copy-done.3
  75.9 8.1 %shard_map.57 = bf16[1,3,2,512,1024]{4,3,2,1,0:T(8,128)(2,1)} custom-call(s32[16]{0:T(128)} %counts.5, s32[2]{0:T(128)} %pad_add_fusion.1.where, s32[1,1024]{1,0:T(1,128)} %pad_add_fusion.dest_ref, bf16[16,72,128]{2,1,0:T(8,128)(2,1)} %copy-done, bf16[16,72,128]{2,1,0:T(8,128)(2,1)} %copy-done.2, bf16[16,72,128]{2,1,0:T(8,128)(2,1)} %copy-done.1, ...), custom_call_target="tpu_custom_call" | custom-call | tf_op jit(solution)/shard_map/pallas_call | solution.py:329
  (4 shorter events, 0.0 us)
Async XLA Ops:
  21.1 28.6 %all-to-all-start = ((bf16[16,72,128]{2,1,0:T(8,128)(2,1)}), bf16[16,72,128]{2,1,0:T(8,128)(2,1)S(1)}, u32[]{:S(2)}, u32[]{:S(2)}) async-start(bf16[16,72,128]{2,1,0:T(8,128)(2,1)} %shard_map.55), calls=%async_computation | async-start | bytes 589824 | tf_op jit(solution)/shard_map/all_to_all | solution.py:356
  28.5 27.3 %copy-start.4 = (s32[512]{0:T(512)S(1)}, s32[512]{0:T(512)}, u32[]{:S(2)}) copy-start(s32[512]{0:T(512)} %param.6) | copy-start | bytes 6148
  49.7 25.4 %copy-start = (bf16[16,72,128]{2,1,0:T(8,128)(2,1)}, bf16[16,72,128]{2,1,0:T(8,128)(2,1)S(1)}, u32[]{:S(2)}) copy-start(bf16[16,72,128]{2,1,0:T(8,128)(2,1)S(1)} %all-to-all-done.refs_0_) | copy-start | bytes 884740
  49.8 16.6 %all-to-all-start.1 = ((bf16[16,72,128]{2,1,0:T(8,128)(2,1)}), bf16[16,72,128]{2,1,0:T(8,128)(2,1)S(1)}, u32[]{:S(2)}, u32[]{:S(2)}) async-start(bf16[16,72,128]{2,1,0:T(8,128)(2,1)} %shard_map.56), calls=%async_computation.1 | async-start | bytes 589824 | tf_op jit(solution)/shard_map/all_to_all | solution.py:356
  56.2 13.3 %collective-permute-start = (bf16[16,72,128]{2,1,0:T(8,128)(2,1)S(1)}, bf16[16,72,128]{2,1,0:T(8,128)(2,1)S(1)}, u32[]{:S(2)}, u32[]{:S(2)}) collective-permute-start(bf16[16,72,128]{2,1,0:T(8,128)(2,1)S(1)} %all-to-all-done.refs_0_), channel_id=1, source_target_pairs={{0,1},{1,0},{2,3},{3,2},{4,5},{5,4},{6,7},{7,6},{8,9},{9,8},{10,11... | collective-permute-start | bytes 884744 | tf_op jit(solution)/shard_map/ppermute | solution.py:357
  66.4 8.8 %copy-start.1 = (bf16[16,72,128]{2,1,0:T(8,128)(2,1)}, bf16[16,72,128]{2,1,0:T(8,128)(2,1)S(1)}, u32[]{:S(2)}) copy-start(bf16[16,72,128]{2,1,0:T(8,128)(2,1)S(1)} %all-to-all-done.1.refs_2_) | copy-start | bytes 884740
  66.4 8.8 %collective-permute-start.1 = (bf16[16,72,128]{2,1,0:T(8,128)(2,1)S(1)}, bf16[16,72,128]{2,1,0:T(8,128)(2,1)S(1)}, u32[]{:S(2)}, u32[]{:S(2)}) collective-permute-start(bf16[16,72,128]{2,1,0:T(8,128)(2,1)S(1)} %all-to-all-done.1.refs_2_), channel_id=1, source_target_pairs={{0,1},{1,0},{2,3},{3,2},{4,5},{5,4},{6,7},{7,6},{8,9},{9,8},{10,11... | collective-permute-start | bytes 884744 | tf_op jit(solution)/shard_map/ppermute | solution.py:357
  69.4 5.7 %copy-start.2 = (bf16[16,72,128]{2,1,0:T(8,128)(2,1)}, bf16[16,72,128]{2,1,0:T(8,128)(2,1)S(1)}, u32[]{:S(2)}) copy-start(bf16[16,72,128]{2,1,0:T(8,128)(2,1)S(1)} %collective-permute-done.refs_1_) | copy-start | bytes 884740
  75.2 0.7 copy-start.3

commit v4 on v3

--- a/solution.py
+++ b/solution.py
@@ -92,7 +92,7 @@
 
 
 def channelizer(
-    band, dests, first, streams, step, counts, v_ref, u_hbm, w_hbm, out_ref,
+    band, dests, first, streams, step, by_tile, counts, v_ref, u_hbm, w_hbm, out_ref,
     held, u_ref, w_ref, y, p, x, turned, arrived,
 ):
     i = pl.program_id(0)
@@ -105,19 +105,30 @@
         pltpu.make_async_copy(w_hbm, w_ref, arrived.at[3]),
     ]
 
+    tiles_in = FFT_LEN // LANES
+
     def fetch(block):
         slot = block % 2
-        return pltpu.make_async_copy(
-            v_ref.at[pl.ds(first + block * step, step), 0],
-            held.at[slot, :, :, :, pl.ds(0, FFT_LEN)],
-            arrived.at[slot],
-        )
+        frames_in = v_ref.at[pl.ds(first + block * step, step), 0]
+        if by_tile:
+            return [
+                pltpu.make_async_copy(
+                    frames_in.at[:, :, :, pl.ds(j * LANES, LANES)], held.at[slot, j], arrived.at[slot]
+                )
+                for j in range(tiles_in)
+            ]
+        return [pltpu.make_async_copy(frames_in, held.at[slot], arrived.at[slot])]
 
     reach = NSPEC + 8
     wide = max(1, 2 * band // LANES)
 
     def analyse():
-        signal = held[i % 2].reshape(step * rows, FFT_LEN + LANES)[:, :FFT_LEN]
+        if by_tile:
+            signal = jnp.concatenate(
+                [held[i % 2, j].reshape(step * rows, LANES) for j in range(tiles_in)], axis=1
+            )
+        else:
+            signal = held[i % 2].reshape(step * rows, FFT_LEN)
         coeff = jnp.dot(signal, u_ref[...], preferred_element_type=jnp.float32)
         coeff = coeff[:, :lanes] + coeff[:, lanes:]
         high = coeff.astype(jnp.bfloat16).astype(jnp.float32)
@@ -169,13 +180,13 @@
 
     @pl.when(i == 0)
     def _():
-        fetch(0).start()
-        for copy in tables_in:
+        for copy in fetch(0) + tables_in:
             copy.start()
 
     @pl.when(i + 1 < last)
     def _():
-        fetch(i + 1).start()
+        for copy in fetch(i + 1):
+            copy.start()
 
     @pl.when(i == 0)
     def _():
@@ -184,7 +195,8 @@
 
     @pl.when(i < last)
     def _():
-        fetch(i).wait()
+        whole = held.at[i % 2]
+        pltpu.make_async_copy(whole, whole, arrived.at[i % 2]).wait()
         mix(jnp.maximum(i - 1, 0))
         analyse()
 
@@ -217,15 +229,15 @@
         out_ref[...] = turned[...].astype(jnp.bfloat16)
 
 
-def channelize(voltages, chan_counts, dests, start, streams):
+def channelize(voltages, chan_counts, dests, start, streams, step, by_tile):
     band = 2 * dests
     frames = voltages.shape[2]
-    step = 4 if band <= 64 else 2
     analysis, mixing = tables(band)
     packed = packing(band)[1]
     payload = 2 * CAP * NSPEC * streams // LANES
     steps = streams // step
-    kernel = functools.partial(channelizer, band, dests, start, streams, step)
+    kernel = functools.partial(channelizer, band, dests, start, streams, step, by_tile)
+    held = (FFT_LEN // LANES, step, frames, 2, LANES) if by_tile else (step, frames, 2, FFT_LEN)
     return pl.pallas_call(
         kernel,
         grid_spec=pltpu.PrefetchScalarGridSpec(
@@ -234,7 +246,7 @@
             in_specs=[pl.BlockSpec(memory_space=pl.ANY)] * 3,
             out_specs=pl.BlockSpec((dests, payload, LANES), lambda i, c: (0, 0, 0)),
             scratch_shapes=[
-                pltpu.VMEM((2, step, frames, 2, FFT_LEN + LANES), jnp.bfloat16),
+                pltpu.VMEM((2,) + held, jnp.bfloat16),
                 pltpu.VMEM(analysis.shape, jnp.bfloat16),
                 pltpu.VMEM(mixing.shape, jnp.bfloat16),
                 pltpu.VMEM((packed // LANES, step * 2 * frames + 16, LANES), jnp.float32),
@@ -253,51 +265,52 @@
     )(chan_counts, voltages, jnp.asarray(analysis), jnp.asarray(mixing))
 
 
-def correlator(direct, counts, where, dest_ref, *refs):
+def in_order(refs, dest_ref, pre, total):
+    if len(refs) == 2:
+        for h, ref in enumerate(refs):
+            sources, payload = ref.shape[0], ref.shape[1]
+            tiles = payload // (2 * CAP)
+            spread = NSPEC // tiles
+            width = LANES // spread
+            lane = lax.broadcasted_iota(jnp.int32, (payload, LANES), 1)
+            for q in range(sources // spread):
+                parts = [ref[spread * q + a].astype(jnp.float32) for a in range(spread)]
+                groups = []
+                for g in range(spread):
+                    group = None
+                    for a in range(spread):
+                        moved = turn_lanes(parts[a], (a - g) * width)
+                        group = moved if a == 0 else jnp.where(lane < a * width, group, moved)
+                    groups.append(group)
+                for part in range(2 * CAP):
+                    rows = slice(part * tiles, (part + 1) * tiles)
+                    both = jnp.concatenate([group[rows] for group in groups], axis=0)
+                    pre[part, h * NSPEC : (h + 1) * NSPEC, q * LANES : (q + 1) * LANES] = (
+                        both.astype(jnp.bfloat16)
+                    )
+    else:
+        pre[...] = refs[0][...]
+    parts, time_len, held = pre.shape
+    spot = lax.broadcasted_iota(jnp.int32, (total, held), 0)
+    turn = jnp.where(spot == dest_ref[...], 1.0, 0.0).astype(jnp.bfloat16)
+    return lax.dot_general(
+        pre[...].reshape(parts * time_len, held), turn, (((1,), (1,)), ((), ())),
+        preferred_element_type=jnp.float32,
+    )
+
+
+def correlator(given, counts, where, dest_ref, *refs):
     out_ref, pre, post = refs[-3:]
+    refs = refs[:-3]
     k = pl.program_id(0)
     time_len = pre.shape[1]
-    total = pre.shape[2]
 
     @pl.when(k == 0)
     def _():
-        if direct:
-            base = 0
-            for c in range(len(refs[:-3]) // 2):
-                for h, ref in enumerate(refs[2 * c : 2 * c + 2]):
-                    sources, payload = ref.shape[0], ref.shape[1]
-                    tiles = payload // (2 * CAP)
-                    spread = NSPEC // tiles
-                    width = LANES // spread
-                    lane = lax.broadcasted_iota(jnp.int32, (payload, LANES), 1)
-                    for q in range(sources // spread):
-                        parts = [ref[spread * q + a].astype(jnp.float32) for a in range(spread)]
-                        groups = []
-                        for g in range(spread):
-                            group = None
-                            for a in range(spread):
-                                moved = turn_lanes(parts[a], (a - g) * width)
-                                group = moved if a == 0 else jnp.where(
-                                    lane < a * width, group, moved
-                                )
-                            groups.append(group)
-                        for part in range(2 * CAP):
-                            rows = slice(part * tiles, (part + 1) * tiles)
-                            both = jnp.concatenate([group[rows] for group in groups], axis=0)
-                            pre[
-                                part, h * NSPEC : (h + 1) * NSPEC,
-                                base + q * LANES : base + (q + 1) * LANES,
-                            ] = both.astype(jnp.bfloat16)
-                base = base + sources * width
-        else:
-            pre[...] = refs[0][...]
-        spot = lax.broadcasted_iota(jnp.int32, (total, total), 0)
-        turn = jnp.where(spot == dest_ref[...], 1.0, 0.0).astype(jnp.bfloat16)
-        ordered = lax.dot_general(
-            pre[...].reshape(2 * CAP * time_len, total), turn, (((1,), (1,)), ((), ())),
-            preferred_element_type=jnp.float32,
-        )
-        post[...] = ordered.astype(jnp.bfloat16).reshape(CAP, 2 * time_len, total)
+        ordered = in_order(refs[:given], dest_ref, pre, post.shape[2])
+        for ref in refs[given:]:
+            ordered = ordered + ref[...].astype(jnp.float32)
+        post[...] = ordered.astype(jnp.bfloat16).reshape(post.shape)
 
     rows = out_ref.shape[3]
     every = post[k]
@@ -311,30 +324,53 @@
         out_ref[0, 0, part] = (vis * valid).astype(jnp.bfloat16)
 
 
-def correlate(pairs, dest, chan_counts, where, total):
-    sources, payload = pairs[0][0].shape[:2]
+def orderer(dest_ref, *refs):
+    out_ref, pre = refs[-2:]
+    out_ref[...] = in_order(refs[:-2], dest_ref, pre, out_ref.shape[1]).astype(jnp.bfloat16)
+
+
+def halves(own, other):
+    sources, payload = own.shape[:2]
     spread = 2 * CAP * NSPEC // payload
-    direct = spread <= 4
-    if direct:
-        operands = [half for pair in pairs for half in pair]
-    else:
-        operands = []
-        for pair in pairs:
-            both = jnp.stack(pair).reshape(2, sources, 2 * CAP, NSPEC // spread, spread, -1)
-            both = both.transpose(2, 0, 3, 4, 1, 5).reshape(2 * CAP, 2 * NSPEC, -1)
-            operands.append(both)
-        operands = [jnp.concatenate(operands, axis=2)]
-    specs = [pl.BlockSpec(a.shape, lambda k, c, w: (0, 0, 0)) for a in operands]
+    held = (2 * CAP, 2 * NSPEC, sources * LANES // spread)
+    if spread <= 4:
+        return [own, other], held
+    both = jnp.stack([own, other]).reshape(2, sources, 2 * CAP, NSPEC // spread, spread, -1)
+    return [both.transpose(2, 0, 3, 4, 1, 5).reshape(held)], held
+
+
+def order(own, other, dest, total):
+    operands, held = halves(own, other)
+    return pl.pallas_call(
+        orderer,
+        out_shape=jax.ShapeDtypeStruct((held[0] * held[1], total), jnp.bfloat16),
+        scratch_shapes=[pltpu.VMEM(held, jnp.bfloat16)],
+        compiler_params=pltpu.CompilerParams(vmem_limit_bytes=60 * 1024 * 1024),
+        cost_estimate=pl.CostEstimate(
+            flops=2 * held[0] * held[1] * held[2] * total, bytes_accessed=4 * own.size,
+            transcendentals=0,
+        ),
+    )(dest, *operands)
+
+
+def correlate(own, other, dest, before, chan_counts, where, total):
+    operands, held = halves(own, other)
+    given = len(operands)
+    operands = operands + before
+    specs = [
+        pl.BlockSpec(a.shape, functools.partial(lambda n, k, c, w: (0,) * n, a.ndim))
+        for a in [dest] + operands
+    ]
     rows = total // 2
     return pl.pallas_call(
-        functools.partial(correlator, direct),
+        functools.partial(correlator, given),
         grid_spec=pltpu.PrefetchScalarGridSpec(
             num_scalar_prefetch=2,
             grid=(CAP,),
-            in_specs=[pl.BlockSpec((1, total), lambda k, c, w: (0, 0))] + specs,
+            in_specs=specs,
             out_specs=pl.BlockSpec((1, 1, 2, rows, total), lambda k, c, w: (0, k, 0, 0, 0)),
             scratch_shapes=[
-                pltpu.VMEM((2 * CAP, 2 * NSPEC, total), jnp.bfloat16),
+                pltpu.VMEM(held, jnp.bfloat16),
                 pltpu.VMEM((CAP, 4 * NSPEC, total), jnp.bfloat16),
             ],
         ),
@@ -346,21 +382,21 @@
 def body(voltages, station_map, chan_counts):
     dests = lax.axis_size("stn")
     streams = voltages.shape[0]
-    sizes = (32, 32) if streams == 64 else (streams,)
-    pairs = []
-    places = []
+    total = dests * streams
+    plan = ((32, 4, True), (32, 8, False)) if streams == 64 else ((streams, 2, False),)
+    dest = (2 * station_map[:, None] + jnp.arange(2, dtype=jnp.int32)[None, :]).reshape(dests, -1)
+    where = jnp.stack([lax.axis_index("stn"), lax.axis_index("blk")]).astype(jnp.int32)
     start = 0
-    dest = (2 * station_map[:, None] + jnp.arange(2, dtype=jnp.int32)[None, :]).reshape(dests, -1)
-    for size in sizes:
-        outgoing = channelize(voltages, chan_counts, dests, start, size)
+    before = []
+    for size, step, by_tile in plan:
+        outgoing = channelize(voltages, chan_counts, dests, start, size, step, by_tile)
         own = lax.all_to_all(outgoing, "stn", split_axis=0, concat_axis=0, tiled=True)
         other = lax.ppermute(own, "blk", [(0, 1), (1, 0)])
-        pairs.append((own, other))
-        places.append(dest[:, start : start + size].reshape(1, -1))
+        place = dest[:, start : start + size].reshape(1, -1)
         start = start + size
-    dest = jnp.concatenate(places, axis=1)
-    where = jnp.stack([lax.axis_index("stn"), lax.axis_index("blk")]).astype(jnp.int32)
-    return correlate(pairs, dest, chan_counts, where, dests * streams)
+        if start < streams:
+            before.append(order(own, other, place, total))
+    return correlate(own, other, place, before, chan_counts, where, total)
 
 
 def solution(mesh):

time: 84.7 us -> 91.7 us (1.083)
  Pallas kernels: 50.4 us -> 57 us
  local copies, waits for them, and re-layouts: 1.31 us -> 3.15 us
    pallas_call x2, Pallas kernels: 42.3 us -> 46.4 us  [channelize(): pl.pallas_call(kernel, grid_spec=pltpu.PrefetchScalarGridSpec(num_scalar_...]
    pallas_call x1 -> x2, Pallas kernels: 8.07 us -> 10.6 us  [the longest x1 7.45 us: correlate(): pl.pallas_call(functools.partial(correlator, given), grid_spec=pltpu.Pref...]
    reshape x2, local copies, waits for them, and re-layouts: 0.16 us -> 1.33 us  [body(): place = dest[:, start:start + size].reshape(1, -1)]
  transfers between devices with their start and end apart: 4 -> 4, of which waited for: 2 -> 2; matrix products, arithmetic and copies ran while one was open for 2% -> 3% of each run, Pallas kernels for 25% -> 31%
where the time goes in v4:
time: 91.7 us; the launch traced here: 91.2 us
  Pallas kernels  57 us (62%)
  starting transfers between devices  16.4 us (18%)
  waiting for transfers between devices  13.9 us (15%)
  local copies, waits for them, and re-layouts  3.15 us (3%)
    pallas_call x2, Pallas kernels, channelize(): pl.pallas_call(kernel, grid_spec=pltpu.PrefetchScalarGridSpec(num_scalar_...  46.4 us
    all_to_all x2, starting transfers between devices, body(): lax.all_to_all(outgoing, 'stn', split_axis=0, concat_axis=0, tiled=True)  13.4 us
    all_to_all x2, waiting for transfers between devices, body(): lax.all_to_all(outgoing, 'stn', split_axis=0, concat_axis=0, tiled=True)  8.66 us
    pallas_call x1, Pallas kernels, correlate(): pl.pallas_call(functools.partial(correlator, given), grid_spec=pltpu.Pref...  7.45 us
    ppermute x2, waiting for transfers between devices, body(): other = lax.ppermute(own, 'blk', [(0, 1), (1, 0)])  5.19 us
    pallas_call x1, Pallas kernels, order(): pl.pallas_call(orderer, out_shape=jax.ShapeDtypeStruct((held[0] * held[1]...  3.17 us
    ppermute x2, starting transfers between devices, body(): other = lax.ppermute(own, 'blk', [(0, 1), (1, 0)])  3.03 us
  transfers between devices with their start and end apart: 4, of which 2 were waited for; matrix products, arithmetic and copies ran while one was open for 3% of the time, Pallas kernels for 31%

profile of v4, /device:TPU:0, one launch (start us, length us, event | category | flops | bytes accessed | tf_op | source)
XLA Modules:
  0.0 91.2 jit_solution(1595248548276543861)
XLA Ops:
  0.0 21.1 %shard_map.55 = bf16[16,72,128]{2,1,0:T(8,128)(2,1)} custom-call(s32[16]{0:T(128)} %counts.5, bf16[64,1,63,2,4096]{4,3,2,1,0:T(2,128)(2,1)} %v_ref.3, bf16[4096,256]{1,0:T(8,128)(2,1)} %constant.14.clone.u_hbm, bf16[2048,256]{1,0:T(8,128)(2,1)} %constant.15.clone.w_hbm), custom_call_target="tpu_custom_call" | custom-call | flops 8455716864 | bytes 33030144 | tf_op jit(solution)/shard_map/pallas_call | solution.py:241
  21.1 7.4 %all-to-all-start = ((bf16[16,72,128]{2,1,0:T(8,128)(2,1)}), bf16[16,72,128]{2,1,0:T(8,128)(2,1)S(1)}, u32[]{:S(2)}, u32[]{:S(2)}) async-start(bf16[16,72,128]{2,1,0:T(8,128)(2,1)} %shard_map.55), calls=%async_computation | async-start | bytes 589824 | tf_op jit(solution)/shard_map/all_to_all | solution.py:393
  28.4 0.0 copy-start.3
  28.5 25.3 %shard_map.56 = bf16[16,72,128]{2,1,0:T(8,128)(2,1)} custom-call(s32[16]{0:T(128)} %counts.5, bf16[64,1,63,2,4096]{4,3,2,1,0:T(2,128)(2,1)} %v_ref.3, bf16[4096,256]{1,0:T(8,128)(2,1)} %constant.14.clone.u_hbm, bf16[2048,256]{1,0:T(8,128)(2,1)} %constant.15.clone.w_hbm), custom_call_target="tpu_custom_call" | custom-call | flops 8455716864 | bytes 33030144 | tf_op jit(solution)/shard_map/pallas_call | solution.py:241
  53.8 0.0 all-to-all-done.refs_0_
  53.8 0.0 copy-start
  53.8 6.0 %all-to-all-start.1 = ((bf16[16,72,128]{2,1,0:T(8,128)(2,1)}), bf16[16,72,128]{2,1,0:T(8,128)(2,1)S(1)}, u32[]{:S(2)}, u32[]{:S(2)}) async-start(bf16[16,72,128]{2,1,0:T(8,128)(2,1)} %shard_map.56), calls=%async_computation.1 | async-start | bytes 589824 | tf_op jit(solution)/shard_map/all_to_all | solution.py:393
  59.8 0.0 copy-done.3
  59.8 0.1 add.22
  59.9 0.1 copy.8
  60.0 0.1 add.26
  60.1 0.1 broadcast_add_fusion
  60.2 1.5 %collective-permute-start = (bf16[16,72,128]{2,1,0:T(8,128)(2,1)S(1)}, bf16[16,72,128]{2,1,0:T(8,128)(2,1)S(1)}, u32[]{:S(2)}, u32[]{:S(2)}) collective-permute-start(bf16[16,72,128]{2,1,0:T(8,128)(2,1)S(1)} %all-to-all-done.refs_0_), channel_id=1, source_target_pairs={{0,1},{1,0},{2,3},{3,2},{4,5},{5,4},{6,7},{7,6},{8,9},{9,8},{10,11... | collective-permute-start | bytes 884744 | tf_op jit(solution)/shard_map/ppermute | solution.py:394
  61.7 8.7 %all-to-all-done.1.refs_0_ = bf16[16,72,128]{2,1,0:T(8,128)(2,1)S(1)} async-done(((bf16[16,72,128]{2,1,0:T(8,128)(2,1)}), bf16[16,72,128]{2,1,0:T(8,128)(2,1)S(1)}, u32[]{:S(2)}, u32[]{:S(2)}) %all-to-all-start.1) | async-done | bytes 294944 | tf_op jit(solution)/shard_map/all_to_all | solution.py:393
  70.4 0.0 copy-start.2
  70.4 1.5 %collective-permute-start.1 = (bf16[16,72,128]{2,1,0:T(8,128)(2,1)S(1)}, bf16[16,72,128]{2,1,0:T(8,128)(2,1)S(1)}, u32[]{:S(2)}, u32[]{:S(2)}) collective-permute-start(bf16[16,72,128]{2,1,0:T(8,128)(2,1)S(1)} %all-to-all-done.1.refs_0_), channel_id=1, source_target_pairs={{0,1},{1,0},{2,3},{3,2},{4,5},{5,4},{6,7},{7,6},{8,9},{9,8},{10,11... | collective-permute-start | bytes 884744 | tf_op jit(solution)/shard_map/ppermute | solution.py:394
  71.9 0.1 copy.10
  72.0 0.7 reshape.14.dest_ref
  72.6 0.1 copy.9
  72.7 0.7 reshape.13.dest_ref
  73.4 0.6 pad_add_fusion.where
  74.0 5.2 %collective-permute-done.1.refs_1_ = bf16[16,72,128]{2,1,0:T(8,128)(2,1)S(1)} collective-permute-done((bf16[16,72,128]{2,1,0:T(8,128)(2,1)S(1)}, bf16[16,72,128]{2,1,0:T(8,128)(2,1)S(1)}, u32[]{:S(2)}, u32[]{:S(2)}) %collective-permute-start.1) | collective-permute-done | bytes 294944 | tf_op jit(solution)/shard_map/ppermute | solution.py:394
  79.2 0.0 copy-done.2
  79.2 0.0 copy-start.4
  79.2 0.7 copy-done.4
  79.9 3.2 %shard_map.57.refs_2_ = bf16[576,1024]{1,0:T(8,128)(2,1)} custom-call(s32[1,512]{1,0:T(1,128)} %reshape.14.dest_ref, bf16[16,72,128]{2,1,0:T(8,128)(2,1)} %copy-done.2, bf16[16,72,128]{2,1,0:T(8,128)(2,1)} %copy-done.4), custom_call_target="tpu_custom_call" | custom-call | flops 603979776 | bytes 589824 | tf_op jit(solution)/shard_map/pallas_call | solution.py:344
  83.1 0.0 collective-permute-done.refs_1_
  83.1 0.0 copy-done
  83.1 0.0 copy-start.1
  83.1 0.7 copy-done.1
  83.8 7.5 %shard_map.58 = bf16[1,3,2,512,1024]{4,3,2,1,0:T(8,128)(2,1)} custom-call(s32[16]{0:T(128)} %counts.5, s32[2]{0:T(128)} %pad_add_fusion.where, s32[1,512]{1,0:T(1,128)} %reshape.13.dest_ref, bf16[16,72,128]{2,1,0:T(8,128)(2,1)} %copy-done, bf16[16,72,128]{2,1,0:T(8,128)(2,1)} %copy-done.1, bf16[576,1024]{1,0:T(8,128)(2,1)} %shard_map.57.refs_2_), custom_call_target="tpu_custom_call" | custom-call | tf_op jit(solution)/shard_map/pallas_call | solution.py:365
  (4 shorter events, 0.0 us)
Async XLA Ops:
  21.1 32.7 %all-to-all-start = ((bf16[16,72,128]{2,1,0:T(8,128)(2,1)}), bf16[16,72,128]{2,1,0:T(8,128)(2,1)S(1)}, u32[]{:S(2)}, u32[]{:S(2)}) async-start(bf16[16,72,128]{2,1,0:T(8,128)(2,1)} %shard_map.55), calls=%async_computation | async-start | bytes 589824 | tf_op jit(solution)/shard_map/all_to_all | solution.py:393
  28.4 31.4 %copy-start.3 = (s32[512]{0:T(512)S(1)}, s32[512]{0:T(512)}, u32[]{:S(2)}) copy-start(s32[512]{0:T(512)} %param.6) | copy-start | bytes 6148
  53.8 29.3 %copy-start = (bf16[16,72,128]{2,1,0:T(8,128)(2,1)}, bf16[16,72,128]{2,1,0:T(8,128)(2,1)S(1)}, u32[]{:S(2)}) copy-start(bf16[16,72,128]{2,1,0:T(8,128)(2,1)S(1)} %all-to-all-done.refs_0_) | copy-start | bytes 884740
  53.8 16.6 %all-to-all-start.1 = ((bf16[16,72,128]{2,1,0:T(8,128)(2,1)}), bf16[16,72,128]{2,1,0:T(8,128)(2,1)S(1)}, u32[]{:S(2)}, u32[]{:S(2)}) async-start(bf16[16,72,128]{2,1,0:T(8,128)(2,1)} %shard_map.56), calls=%async_computation.1 | async-start | bytes 589824 | tf_op jit(solution)/shard_map/all_to_all | solution.py:393
  60.2 22.9 %collective-permute-start = (bf16[16,72,128]{2,1,0:T(8,128)(2,1)S(1)}, bf16[16,72,128]{2,1,0:T(8,128)(2,1)S(1)}, u32[]{:S(2)}, u32[]{:S(2)}) collective-permute-start(bf16[16,72,128]{2,1,0:T(8,128)(2,1)S(1)} %all-to-all-done.refs_0_), channel_id=1, source_target_pairs={{0,1},{1,0},{2,3},{3,2},{4,5},{5,4},{6,7},{7,6},{8,9},{9,8},{10,11... | collective-permute-start | bytes 884744 | tf_op jit(solution)/shard_map/ppermute | solution.py:394
  70.4 8.8 %copy-start.2 = (bf16[16,72,128]{2,1,0:T(8,128)(2,1)}, bf16[16,72,128]{2,1,0:T(8,128)(2,1)S(1)}, u32[]{:S(2)}) copy-start(bf16[16,72,128]{2,1,0:T(8,128)(2,1)S(1)} %all-to-all-done.1.refs_0_) | copy-start | bytes 884740
  70.4 8.8 %collective-permute-start.1 = (bf16[16,72,128]{2,1,0:T(8,128)(2,1)S(1)}, bf16[16,72,128]{2,1,0:T(8,128)(2,1)S(1)}, u32[]{:S(2)}, u32[]{:S(2)}) collective-permute-start(bf16[16,72,128]{2,1,0:T(8,128)(2,1)S(1)} %all-to-all-done.1.refs_0_), channel_id=1, source_target_pairs={{0,1},{1,0},{2,3},{3,2},{4,5},{5,4},{6,7},{7,6},{8,9},{9,8},{10,11... | collective-permute-start | bytes 884744 | tf_op jit(solution)/shard_map/ppermute | solution.py:394
  79.2 0.7 copy-start.4
  83.1 0.7 copy-start.1

commit v5 on v4

--- a/solution.py
+++ b/solution.py
@@ -92,45 +92,42 @@
 
 
 def channelizer(
-    band, dests, first, streams, step, by_tile, counts, v_ref, u_hbm, w_hbm, out_ref,
+    band, dests, first, streams, step, turned_dot, counts, v_ref, u_hbm, w_hbm, out_ref,
     held, u_ref, w_ref, y, p, x, turned, arrived,
 ):
     i = pl.program_id(0)
     last = pl.num_programs(0) - 1
     count, packed, triple = packing(band)
-    lanes = u_ref.shape[1] // 2
+    lanes = u_ref.shape[0 if turned_dot else 1] // 2
     rows = 2 * v_ref.shape[2]
     tables_in = [
         pltpu.make_async_copy(u_hbm, u_ref, arrived.at[2]),
         pltpu.make_async_copy(w_hbm, w_ref, arrived.at[3]),
     ]
 
-    tiles_in = FFT_LEN // LANES
-
     def fetch(block):
         slot = block % 2
         frames_in = v_ref.at[pl.ds(first + block * step, step), 0]
-        if by_tile:
-            return [
-                pltpu.make_async_copy(
-                    frames_in.at[:, :, :, pl.ds(j * LANES, LANES)], held.at[slot, j], arrived.at[slot]
-                )
-                for j in range(tiles_in)
-            ]
         return [pltpu.make_async_copy(frames_in, held.at[slot], arrived.at[slot])]
 
     reach = NSPEC + 8
     wide = max(1, 2 * band // LANES)
 
     def analyse():
-        if by_tile:
-            signal = jnp.concatenate(
-                [held[i % 2, j].reshape(step * rows, LANES) for j in range(tiles_in)], axis=1
+        if turned_dot:
+            signal = held[i % 2].reshape(step * rows, FFT_LEN)
+            coeff = lax.dot_general(
+                u_ref[...], signal, (((1,), (1,)), ((), ())), preferred_element_type=jnp.float32
             )
+            coeff = (coeff[:lanes] + coeff[lanes:]).T
         else:
-            signal = held[i % 2].reshape(step * rows, FFT_LEN)
-        coeff = jnp.dot(signal, u_ref[...], preferred_element_type=jnp.float32)
-        coeff = coeff[:, :lanes] + coeff[:, lanes:]
+            coeff = []
+            for part in range(2):
+                signal = held[i % 2, part * step // 2 : (part + 1) * step // 2]
+                signal = signal.reshape(step * rows // 2, FFT_LEN)
+                coeff.append(jnp.dot(signal, u_ref[...], preferred_element_type=jnp.float32))
+            coeff = jnp.concatenate(coeff, axis=0)
+            coeff = coeff[:, :lanes] + coeff[:, lanes:]
         high = coeff.astype(jnp.bfloat16).astype(jnp.float32)
         low = coeff - high
         if triple:
@@ -229,15 +226,16 @@
         out_ref[...] = turned[...].astype(jnp.bfloat16)
 
 
-def channelize(voltages, chan_counts, dests, start, streams, step, by_tile):
+def channelize(voltages, chan_counts, dests, start, streams, step, turned_dot):
     band = 2 * dests
     frames = voltages.shape[2]
     analysis, mixing = tables(band)
+    if turned_dot:
+        analysis = np.ascontiguousarray(analysis.T)
     packed = packing(band)[1]
     payload = 2 * CAP * NSPEC * streams // LANES
     steps = streams // step
-    kernel = functools.partial(channelizer, band, dests, start, streams, step, by_tile)
-    held = (FFT_LEN // LANES, step, frames, 2, LANES) if by_tile else (step, frames, 2, FFT_LEN)
+    kernel = functools.partial(channelizer, band, dests, start, streams, step, turned_dot)
     return pl.pallas_call(
         kernel,
         grid_spec=pltpu.PrefetchScalarGridSpec(
@@ -246,7 +244,7 @@
             in_specs=[pl.BlockSpec(memory_space=pl.ANY)] * 3,
             out_specs=pl.BlockSpec((dests, payload, LANES), lambda i, c: (0, 0, 0)),
             scratch_shapes=[
-                pltpu.VMEM((2,) + held, jnp.bfloat16),
+                pltpu.VMEM((2, step, frames, 2, FFT_LEN), jnp.bfloat16),
                 pltpu.VMEM(analysis.shape, jnp.bfloat16),
                 pltpu.VMEM(mixing.shape, jnp.bfloat16),
                 pltpu.VMEM((packed // LANES, step * 2 * frames + 16, LANES), jnp.float32),
@@ -259,7 +257,7 @@
         out_shape=jax.ShapeDtypeStruct((dests, payload, LANES), jnp.bfloat16),
         compiler_params=pltpu.CompilerParams(vmem_limit_bytes=60 * 1024 * 1024),
         cost_estimate=pl.CostEstimate(
-            flops=2 * streams * 2 * frames * FFT_LEN * analysis.shape[1],
+            flops=2 * streams * 2 * frames * analysis.size,
             bytes_accessed=2 * 2 * frames * FFT_LEN * streams, transcendentals=0,
         ),
     )(chan_counts, voltages, jnp.asarray(analysis), jnp.asarray(mixing))
@@ -383,13 +381,13 @@
     dests = lax.axis_size("stn")
     streams = voltages.shape[0]
     total = dests * streams
-    plan = ((32, 4, True), (32, 8, False)) if streams == 64 else ((streams, 2, False),)
+    plan = ((32, 4, True), (32, 4, False)) if streams == 64 else ((streams, 2, False),)
     dest = (2 * station_map[:, None] + jnp.arange(2, dtype=jnp.int32)[None, :]).reshape(dests, -1)
     where = jnp.stack([lax.axis_index("stn"), lax.axis_index("blk")]).astype(jnp.int32)
     start = 0
     before = []
-    for size, step, by_tile in plan:
-        outgoing = channelize(voltages, chan_counts, dests, start, size, step, by_tile)
+    for size, step, turned_dot in plan:
+        outgoing = channelize(voltages, chan_counts, dests, start, size, step, turned_dot)
         own = lax.all_to_all(outgoing, "stn", split_axis=0, concat_axis=0, tiled=True)
         other = lax.ppermute(own, "blk", [(0, 1), (1, 0)])
         place = dest[:, start : start + size].reshape(1, -1)

time: 91.7 us -> 89.2 us (0.973)
  Pallas kernels: 57 us -> 54.2 us
    pallas_call x2, Pallas kernels: 46.4 us -> 43.5 us  [channelize(): pl.pallas_call(kernel, grid_spec=pltpu.PrefetchScalarGridSpec(num_scalar_...]
  transfers between devices with their start and end apart: 4 -> 4, of which waited for: 2 -> 2; matrix products, arithmetic and copies ran while one was open for 3% -> 3% of each run, Pallas kernels for 31% -> 29%
where the time goes in v5:
time: 89.2 us; the launch traced here: 88.4 us
  Pallas kernels  54.2 us (61%)
  starting transfers between devices  16.4 us (18%)
  waiting for transfers between devices  13.8 us (15%)
  local copies, waits for them, and re-layouts  3.15 us (4%)
    pallas_call x2, Pallas kernels, channelize(): pl.pallas_call(kernel, grid_spec=pltpu.PrefetchScalarGridSpec(num_scalar_...  43.5 us
    all_to_all x2, starting transfers between devices, body(): lax.all_to_all(outgoing, 'stn', split_axis=0, concat_axis=0, tiled=True)  13.4 us
    all_to_all x2, waiting for transfers between devices, body(): lax.all_to_all(outgoing, 'stn', split_axis=0, concat_axis=0, tiled=True)  8.66 us
    pallas_call x1, Pallas kernels, correlate(): pl.pallas_call(functools.partial(correlator, given), grid_spec=pltpu.Pref...  7.45 us
    ppermute x2, waiting for transfers between devices, body(): other = lax.ppermute(own, 'blk', [(0, 1), (1, 0)])  5.18 us
    pallas_call x1, Pallas kernels, order(): pl.pallas_call(orderer, out_shape=jax.ShapeDtypeStruct((held[0] * held[1]...  3.17 us
    ppermute x2, starting transfers between devices, body(): other = lax.ppermute(own, 'blk', [(0, 1), (1, 0)])  3.05 us
  transfers between devices with their start and end apart: 4, of which 2 were waited for; matrix products, arithmetic and copies ran while one was open for 3% of the time, Pallas kernels for 29%

profile of v5, /device:TPU:0, one launch (start us, length us, event | category | flops | bytes accessed | tf_op | source)
XLA Modules:
  0.0 88.4 jit_solution(8585785740463466601)
XLA Ops:
  0.0 21.4 %shard_map.64 = bf16[16,72,128]{2,1,0:T(8,128)(2,1)} custom-call(s32[16]{0:T(128)} %counts.5, bf16[64,1,63,2,4096]{4,3,2,1,0:T(2,128)(2,1)} %v_ref.3, bf16[4096,256]{1,0:T(8,128)(2,1)} %constant.18.clone.u_hbm, bf16[2048,256]{1,0:T(8,128)(2,1)} %constant.17.clone.w_hbm), custom_call_target="tpu_custom_call" | custom-call | flops 8455716864 | bytes 33030144 | tf_op jit(solution)/shard_map/pallas_call | solution.py:239
  21.4 7.4 %all-to-all-start = ((bf16[16,72,128]{2,1,0:T(8,128)(2,1)}), bf16[16,72,128]{2,1,0:T(8,128)(2,1)S(1)}, u32[]{:S(2)}, u32[]{:S(2)}) async-start(bf16[16,72,128]{2,1,0:T(8,128)(2,1)} %shard_map.64), calls=%async_computation | async-start | bytes 589824 | tf_op jit(solution)/shard_map/all_to_all | solution.py:391
  28.8 0.0 copy-start.3
  28.8 22.2 %shard_map.65 = bf16[16,72,128]{2,1,0:T(8,128)(2,1)} custom-call(s32[16]{0:T(128)} %counts.5, bf16[64,1,63,2,4096]{4,3,2,1,0:T(2,128)(2,1)} %v_ref.3, bf16[256,4096]{1,0:T(8,128)(2,1)} %constant.16.clone.u_hbm, bf16[2048,256]{1,0:T(8,128)(2,1)} %constant.17.clone.w_hbm), custom_call_target="tpu_custom_call" | custom-call | flops 8455716864 | bytes 33030144 | tf_op jit(solution)/shard_map/pallas_call | solution.py:239
  50.9 0.0 all-to-all-done.refs_0_
  51.0 0.0 copy-start
  51.0 6.0 %all-to-all-start.1 = ((bf16[16,72,128]{2,1,0:T(8,128)(2,1)}), bf16[16,72,128]{2,1,0:T(8,128)(2,1)S(1)}, u32[]{:S(2)}, u32[]{:S(2)}) async-start(bf16[16,72,128]{2,1,0:T(8,128)(2,1)} %shard_map.65), calls=%async_computation.1 | async-start | bytes 589824 | tf_op jit(solution)/shard_map/all_to_all | solution.py:391
  57.0 0.0 copy-done.3
  57.0 0.1 add.22
  57.1 0.1 copy.9
  57.2 0.1 add.26
  57.3 0.1 broadcast_add_fusion
  57.4 1.5 %collective-permute-start = (bf16[16,72,128]{2,1,0:T(8,128)(2,1)S(1)}, bf16[16,72,128]{2,1,0:T(8,128)(2,1)S(1)}, u32[]{:S(2)}, u32[]{:S(2)}) collective-permute-start(bf16[16,72,128]{2,1,0:T(8,128)(2,1)S(1)} %all-to-all-done.refs_0_), channel_id=1, source_target_pairs={{0,1},{1,0},{2,3},{3,2},{4,5},{5,4},{6,7},{7,6},{8,9},{9,8},{10,11... | collective-permute-start | bytes 884744 | tf_op jit(solution)/shard_map/ppermute | solution.py:392
  58.9 8.7 %all-to-all-done.1.refs_0_ = bf16[16,72,128]{2,1,0:T(8,128)(2,1)S(1)} async-done(((bf16[16,72,128]{2,1,0:T(8,128)(2,1)}), bf16[16,72,128]{2,1,0:T(8,128)(2,1)S(1)}, u32[]{:S(2)}, u32[]{:S(2)}) %all-to-all-start.1) | async-done | bytes 294944 | tf_op jit(solution)/shard_map/all_to_all | solution.py:391
  67.6 0.0 copy-start.2
  67.6 1.5 %collective-permute-start.1 = (bf16[16,72,128]{2,1,0:T(8,128)(2,1)S(1)}, bf16[16,72,128]{2,1,0:T(8,128)(2,1)S(1)}, u32[]{:S(2)}, u32[]{:S(2)}) collective-permute-start(bf16[16,72,128]{2,1,0:T(8,128)(2,1)S(1)} %all-to-all-done.1.refs_0_), channel_id=1, source_target_pairs={{0,1},{1,0},{2,3},{3,2},{4,5},{5,4},{6,7},{7,6},{8,9},{9,8},{10,11... | collective-permute-start | bytes 884744 | tf_op jit(solution)/shard_map/ppermute | solution.py:392
  69.1 0.1 copy.11
  69.2 0.7 reshape.14.dest_ref
  69.8 0.1 copy.10
  69.9 0.7 reshape.13.dest_ref
  70.6 0.6 pad_add_fusion.where
  71.2 5.2 %collective-permute-done.1.refs_1_ = bf16[16,72,128]{2,1,0:T(8,128)(2,1)S(1)} collective-permute-done((bf16[16,72,128]{2,1,0:T(8,128)(2,1)S(1)}, bf16[16,72,128]{2,1,0:T(8,128)(2,1)S(1)}, u32[]{:S(2)}, u32[]{:S(2)}) %collective-permute-start.1) | collective-permute-done | bytes 294944 | tf_op jit(solution)/shard_map/ppermute | solution.py:392
  76.4 0.0 copy-done.2
  76.4 0.0 copy-start.4
  76.4 0.7 copy-done.4
  77.1 3.2 %shard_map.66.refs_2_ = bf16[576,1024]{1,0:T(8,128)(2,1)} custom-call(s32[1,512]{1,0:T(1,128)} %reshape.14.dest_ref, bf16[16,72,128]{2,1,0:T(8,128)(2,1)} %copy-done.2, bf16[16,72,128]{2,1,0:T(8,128)(2,1)} %copy-done.4), custom_call_target="tpu_custom_call" | custom-call | flops 603979776 | bytes 589824 | tf_op jit(solution)/shard_map/pallas_call | solution.py:342
  80.2 0.0 collective-permute-done.refs_1_
  80.2 0.0 copy-done
  80.2 0.0 copy-start.1
  80.2 0.7 copy-done.1
  80.9 7.5 %shard_map.67 = bf16[1,3,2,512,1024]{4,3,2,1,0:T(8,128)(2,1)} custom-call(s32[16]{0:T(128)} %counts.5, s32[2]{0:T(128)} %pad_add_fusion.where, s32[1,512]{1,0:T(1,128)} %reshape.13.dest_ref, bf16[16,72,128]{2,1,0:T(8,128)(2,1)} %copy-done, bf16[16,72,128]{2,1,0:T(8,128)(2,1)} %copy-done.1, bf16[576,1024]{1,0:T(8,128)(2,1)} %shard_map.66.refs_2_), custom_call_target="tpu_custom_call" | custom-call | tf_op jit(solution)/shard_map/pallas_call | solution.py:363
  (4 shorter events, 0.0 us)
Async XLA Ops:
  21.4 29.6 %all-to-all-start = ((bf16[16,72,128]{2,1,0:T(8,128)(2,1)}), bf16[16,72,128]{2,1,0:T(8,128)(2,1)S(1)}, u32[]{:S(2)}, u32[]{:S(2)}) async-start(bf16[16,72,128]{2,1,0:T(8,128)(2,1)} %shard_map.64), calls=%async_computation | async-start | bytes 589824 | tf_op jit(solution)/shard_map/all_to_all | solution.py:391
  28.8 28.2 %copy-start.3 = (s32[512]{0:T(512)S(1)}, s32[512]{0:T(512)}, u32[]{:S(2)}) copy-start(s32[512]{0:T(512)} %param.7) | copy-start | bytes 6148
  51.0 29.3 %copy-start = (bf16[16,72,128]{2,1,0:T(8,128)(2,1)}, bf16[16,72,128]{2,1,0:T(8,128)(2,1)S(1)}, u32[]{:S(2)}) copy-start(bf16[16,72,128]{2,1,0:T(8,128)(2,1)S(1)} %all-to-all-done.refs_0_) | copy-start | bytes 884740
  51.0 16.6 %all-to-all-start.1 = ((bf16[16,72,128]{2,1,0:T(8,128)(2,1)}), bf16[16,72,128]{2,1,0:T(8,128)(2,1)S(1)}, u32[]{:S(2)}, u32[]{:S(2)}) async-start(bf16[16,72,128]{2,1,0:T(8,128)(2,1)} %shard_map.65), calls=%async_computation.1 | async-start | bytes 589824 | tf_op jit(solution)/shard_map/all_to_all | solution.py:391
  57.4 22.9 %collective-permute-start = (bf16[16,72,128]{2,1,0:T(8,128)(2,1)S(1)}, bf16[16,72,128]{2,1,0:T(8,128)(2,1)S(1)}, u32[]{:S(2)}, u32[]{:S(2)}) collective-permute-start(bf16[16,72,128]{2,1,0:T(8,128)(2,1)S(1)} %all-to-all-done.refs_0_), channel_id=1, source_target_pairs={{0,1},{1,0},{2,3},{3,2},{4,5},{5,4},{6,7},{7,6},{8,9},{9,8},{10,11... | collective-permute-start | bytes 884744 | tf_op jit(solution)/shard_map/ppermute | solution.py:392
  67.6 8.8 %copy-start.2 = (bf16[16,72,128]{2,1,0:T(8,128)(2,1)}, bf16[16,72,128]{2,1,0:T(8,128)(2,1)S(1)}, u32[]{:S(2)}) copy-start(bf16[16,72,128]{2,1,0:T(8,128)(2,1)S(1)} %all-to-all-done.1.refs_0_) | copy-start | bytes 884740
  67.6 8.8 %collective-permute-start.1 = (bf16[16,72,128]{2,1,0:T(8,128)(2,1)S(1)}, bf16[16,72,128]{2,1,0:T(8,128)(2,1)S(1)}, u32[]{:S(2)}, u32[]{:S(2)}) collective-permute-start(bf16[16,72,128]{2,1,0:T(8,128)(2,1)S(1)} %all-to-all-done.1.refs_0_), channel_id=1, source_target_pairs={{0,1},{1,0},{2,3},{3,2},{4,5},{5,4},{6,7},{7,6},{8,9},{9,8},{10,11... | collective-permute-start | bytes 884744 | tf_op jit(solution)/shard_map/ppermute | solution.py:392
  76.4 0.7 copy-start.4
  80.2 0.7 copy-start.1

commit v6 on v4

--- a/solution.py
+++ b/solution.py
@@ -92,43 +92,37 @@
 
 
 def channelizer(
-    band, dests, first, streams, step, by_tile, counts, v_ref, u_hbm, w_hbm, out_ref,
+    band, dests, first, streams, step, queues, counts, v_ref, u_hbm, w_hbm, out_ref,
     held, u_ref, w_ref, y, p, x, turned, arrived,
 ):
     i = pl.program_id(0)
+    ahead = held.shape[0]
     last = pl.num_programs(0) - 1
     count, packed, triple = packing(band)
     lanes = u_ref.shape[1] // 2
     rows = 2 * v_ref.shape[2]
-    tables_in = [
-        pltpu.make_async_copy(u_hbm, u_ref, arrived.at[2]),
-        pltpu.make_async_copy(w_hbm, w_ref, arrived.at[3]),
-    ]
-
-    tiles_in = FFT_LEN // LANES
-
-    def fetch(block):
-        slot = block % 2
-        frames_in = v_ref.at[pl.ds(first + block * step, step), 0]
-        if by_tile:
-            return [
-                pltpu.make_async_copy(
-                    frames_in.at[:, :, :, pl.ds(j * LANES, LANES)], held.at[slot, j], arrived.at[slot]
-                )
-                for j in range(tiles_in)
-            ]
-        return [pltpu.make_async_copy(frames_in, held.at[slot], arrived.at[slot])]
-
     reach = NSPEC + 8
     wide = max(1, 2 * band // LANES)
+    tables_in = [
+        pltpu.make_async_copy(u_hbm, u_ref, arrived.at[ahead, 0]),
+        pltpu.make_async_copy(w_hbm, w_ref, arrived.at[ahead, 1]),
+    ]
+
+    def fetch(block):
+        slot = block % ahead
+        return [
+            pltpu.make_async_copy(
+                v_ref.at[first + block * step + r, 0], held.at[slot, r], arrived.at[slot, r]
+            )
+            for r in range(step)
+        ]
+
+    def begin(block):
+        for r, copy in enumerate(fetch(block)):
+            copy.start(priority=r % queues)
 
     def analyse():
-        if by_tile:
-            signal = jnp.concatenate(
-                [held[i % 2, j].reshape(step * rows, LANES) for j in range(tiles_in)], axis=1
-            )
-        else:
-            signal = held[i % 2].reshape(step * rows, FFT_LEN)
+        signal = held[i % ahead].reshape(step * rows, FFT_LEN)
         coeff = jnp.dot(signal, u_ref[...], preferred_element_type=jnp.float32)
         coeff = coeff[:, :lanes] + coeff[:, lanes:]
         high = coeff.astype(jnp.bfloat16).astype(jnp.float32)
@@ -180,13 +174,15 @@
 
     @pl.when(i == 0)
     def _():
-        for copy in fetch(0) + tables_in:
+        begin(0)
+        for copy in tables_in:
             copy.start()
-
-    @pl.when(i + 1 < last)
-    def _():
-        for copy in fetch(i + 1):
-            copy.start()
+        for block in range(1, min(ahead - 1, streams // step)):
+            begin(block)
+
+    @pl.when(i + ahead - 1 < last)
+    def _():
+        begin(i + ahead - 1)
 
     @pl.when(i == 0)
     def _():
@@ -195,8 +191,8 @@
 
     @pl.when(i < last)
     def _():
-        whole = held.at[i % 2]
-        pltpu.make_async_copy(whole, whole, arrived.at[i % 2]).wait()
+        for copy in fetch(i):
+            copy.wait()
         mix(jnp.maximum(i - 1, 0))
         analyse()
 
@@ -229,15 +225,15 @@
         out_ref[...] = turned[...].astype(jnp.bfloat16)
 
 
-def channelize(voltages, chan_counts, dests, start, streams, step, by_tile):
+def channelize(voltages, chan_counts, dests, start, streams, step, queues):
     band = 2 * dests
     frames = voltages.shape[2]
     analysis, mixing = tables(band)
     packed = packing(band)[1]
+    ahead = 4 if band <= 64 else 2
     payload = 2 * CAP * NSPEC * streams // LANES
     steps = streams // step
-    kernel = functools.partial(channelizer, band, dests, start, streams, step, by_tile)
-    held = (FFT_LEN // LANES, step, frames, 2, LANES) if by_tile else (step, frames, 2, FFT_LEN)
+    kernel = functools.partial(channelizer, band, dests, start, streams, step, queues)
     return pl.pallas_call(
         kernel,
         grid_spec=pltpu.PrefetchScalarGridSpec(
@@ -246,20 +242,20 @@
             in_specs=[pl.BlockSpec(memory_space=pl.ANY)] * 3,
             out_specs=pl.BlockSpec((dests, payload, LANES), lambda i, c: (0, 0, 0)),
             scratch_shapes=[
-                pltpu.VMEM((2,) + held, jnp.bfloat16),
+                pltpu.VMEM((ahead, step, frames, 2, FFT_LEN), jnp.bfloat16),
                 pltpu.VMEM(analysis.shape, jnp.bfloat16),
                 pltpu.VMEM(mixing.shape, jnp.bfloat16),
                 pltpu.VMEM((packed // LANES, step * 2 * frames + 16, LANES), jnp.float32),
                 pltpu.VMEM((SHIFTS * 2 * band // LANES, step * (NSPEC + 8), LANES), jnp.float32),
                 pltpu.VMEM((max(1, 2 * band // LANES), NSPEC * streams, LANES), jnp.float32),
                 pltpu.VMEM((dests, payload, LANES), jnp.float32),
-                pltpu.SemaphoreType.DMA((4,)),
+                pltpu.SemaphoreType.DMA((ahead + 1, step)),
             ],
         ),
         out_shape=jax.ShapeDtypeStruct((dests, payload, LANES), jnp.bfloat16),
         compiler_params=pltpu.CompilerParams(vmem_limit_bytes=60 * 1024 * 1024),
         cost_estimate=pl.CostEstimate(
-            flops=2 * streams * 2 * frames * FFT_LEN * analysis.shape[1],
+            flops=2 * streams * 2 * frames * analysis.size,
             bytes_accessed=2 * 2 * frames * FFT_LEN * streams, transcendentals=0,
         ),
     )(chan_counts, voltages, jnp.asarray(analysis), jnp.asarray(mixing))
@@ -383,13 +379,13 @@
     dests = lax.axis_size("stn")
     streams = voltages.shape[0]
     total = dests * streams
-    plan = ((32, 4, True), (32, 8, False)) if streams == 64 else ((streams, 2, False),)
+    plan = ((32, 4, 1), (32, 4, 2)) if streams == 64 else ((streams, 2, 1),)
     dest = (2 * station_map[:, None] + jnp.arange(2, dtype=jnp.int32)[None, :]).reshape(dests, -1)
     where = jnp.stack([lax.axis_index("stn"), lax.axis_index("blk")]).astype(jnp.int32)
     start = 0
     before = []
-    for size, step, by_tile in plan:
-        outgoing = channelize(voltages, chan_counts, dests, start, size, step, by_tile)
+    for size, step, queues in plan:
+        outgoing = channelize(voltages, chan_counts, dests, start, size, step, queues)
         own = lax.all_to_all(outgoing, "stn", split_axis=0, concat_axis=0, tiled=True)
         other = lax.ppermute(own, "blk", [(0, 1), (1, 0)])
         place = dest[:, start : start + size].reshape(1, -1)

time: 91.7 us -> 88.5 us (0.965)
  Pallas kernels: 57 us -> 53.9 us
    pallas_call x2, Pallas kernels: 46.4 us -> 43.3 us  [channelize(): pl.pallas_call(kernel, grid_spec=pltpu.PrefetchScalarGridSpec(num_scalar_...]
  transfers between devices with their start and end apart: 4 -> 4, of which waited for: 2 -> 2; matrix products, arithmetic and copies ran while one was open for 3% -> 3% of each run, Pallas kernels for 31% -> 27%
where the time goes in v6:
time: 88.5 us; the launch traced here: 88.1 us
  Pallas kernels  53.9 us (61%)
  starting transfers between devices  16.4 us (19%)
  waiting for transfers between devices  13.8 us (16%)
  local copies, waits for them, and re-layouts  3.15 us (4%)
    pallas_call x2, Pallas kernels, channelize(): pl.pallas_call(kernel, grid_spec=pltpu.PrefetchScalarGridSpec(num_scalar_...  43.3 us
    all_to_all x2, starting transfers between devices, body(): lax.all_to_all(outgoing, 'stn', split_axis=0, concat_axis=0, tiled=True)  13.4 us
    all_to_all x2, waiting for transfers between devices, body(): lax.all_to_all(outgoing, 'stn', split_axis=0, concat_axis=0, tiled=True)  8.66 us
    pallas_call x1, Pallas kernels, correlate(): pl.pallas_call(functools.partial(correlator, given), grid_spec=pltpu.Pref...  7.45 us
    ppermute x2, waiting for transfers between devices, body(): other = lax.ppermute(own, 'blk', [(0, 1), (1, 0)])  5.18 us
    pallas_call x1, Pallas kernels, order(): pl.pallas_call(orderer, out_shape=jax.ShapeDtypeStruct((held[0] * held[1]...  3.16 us
    ppermute x2, starting transfers between devices, body(): other = lax.ppermute(own, 'blk', [(0, 1), (1, 0)])  3.05 us
  transfers between devices with their start and end apart: 4, of which 2 were waited for; matrix products, arithmetic and copies ran while one was open for 3% of the time, Pallas kernels for 27%

profile of v6, /device:TPU:0, one launch (start us, length us, event | category | flops | bytes accessed | tf_op | source)
XLA Modules:
  0.0 88.1 jit_solution(9870426045888039619)
XLA Ops:
  0.0 22.4 %shard_map.55 = bf16[16,72,128]{2,1,0:T(8,128)(2,1)} custom-call(s32[16]{0:T(128)} %counts.5, bf16[64,1,63,2,4096]{4,3,2,1,0:T(2,128)(2,1)} %v_ref.3, bf16[4096,256]{1,0:T(8,128)(2,1)} %constant.14.clone.u_hbm, bf16[2048,256]{1,0:T(8,128)(2,1)} %constant.15.clone.w_hbm), custom_call_target="tpu_custom_call" | custom-call | flops 8455716864 | bytes 33030144 | tf_op jit(solution)/shard_map/pallas_call | solution.py:237
  22.4 7.4 %all-to-all-start = ((bf16[16,72,128]{2,1,0:T(8,128)(2,1)}), bf16[16,72,128]{2,1,0:T(8,128)(2,1)S(1)}, u32[]{:S(2)}, u32[]{:S(2)}) async-start(bf16[16,72,128]{2,1,0:T(8,128)(2,1)} %shard_map.55), calls=%async_computation | async-start | bytes 589824 | tf_op jit(solution)/shard_map/all_to_all | solution.py:389
  29.8 0.0 copy-start.3
  29.8 20.8 %shard_map.56 = bf16[16,72,128]{2,1,0:T(8,128)(2,1)} custom-call(s32[16]{0:T(128)} %counts.5, bf16[64,1,63,2,4096]{4,3,2,1,0:T(2,128)(2,1)} %v_ref.3, bf16[4096,256]{1,0:T(8,128)(2,1)} %constant.14.clone.u_hbm, bf16[2048,256]{1,0:T(8,128)(2,1)} %constant.15.clone.w_hbm), custom_call_target="tpu_custom_call" | custom-call | flops 8455716864 | bytes 33030144 | tf_op jit(solution)/shard_map/pallas_call | solution.py:237
  50.7 0.0 all-to-all-done.refs_0_
  50.7 0.0 copy-start
  50.7 6.0 %all-to-all-start.1 = ((bf16[16,72,128]{2,1,0:T(8,128)(2,1)}), bf16[16,72,128]{2,1,0:T(8,128)(2,1)S(1)}, u32[]{:S(2)}, u32[]{:S(2)}) async-start(bf16[16,72,128]{2,1,0:T(8,128)(2,1)} %shard_map.56), calls=%async_computation.1 | async-start | bytes 589824 | tf_op jit(solution)/shard_map/all_to_all | solution.py:389
  56.7 0.0 copy-done.3
  56.7 0.1 add.22
  56.8 0.1 copy.8
  56.9 0.1 add.26
  57.0 0.1 broadcast_add_fusion
  57.1 1.5 %collective-permute-start = (bf16[16,72,128]{2,1,0:T(8,128)(2,1)S(1)}, bf16[16,72,128]{2,1,0:T(8,128)(2,1)S(1)}, u32[]{:S(2)}, u32[]{:S(2)}) collective-permute-start(bf16[16,72,128]{2,1,0:T(8,128)(2,1)S(1)} %all-to-all-done.refs_0_), channel_id=1, source_target_pairs={{0,1},{1,0},{2,3},{3,2},{4,5},{5,4},{6,7},{7,6},{8,9},{9,8},{10,11... | collective-permute-start | bytes 884744 | tf_op jit(solution)/shard_map/ppermute | solution.py:390
  58.6 8.7 %all-to-all-done.1.refs_0_ = bf16[16,72,128]{2,1,0:T(8,128)(2,1)S(1)} async-done(((bf16[16,72,128]{2,1,0:T(8,128)(2,1)}), bf16[16,72,128]{2,1,0:T(8,128)(2,1)S(1)}, u32[]{:S(2)}, u32[]{:S(2)}) %all-to-all-start.1) | async-done | bytes 294944 | tf_op jit(solution)/shard_map/all_to_all | solution.py:389
  67.3 0.0 copy-start.2
  67.3 1.5 %collective-permute-start.1 = (bf16[16,72,128]{2,1,0:T(8,128)(2,1)S(1)}, bf16[16,72,128]{2,1,0:T(8,128)(2,1)S(1)}, u32[]{:S(2)}, u32[]{:S(2)}) collective-permute-start(bf16[16,72,128]{2,1,0:T(8,128)(2,1)S(1)} %all-to-all-done.1.refs_0_), channel_id=1, source_target_pairs={{0,1},{1,0},{2,3},{3,2},{4,5},{5,4},{6,7},{7,6},{8,9},{9,8},{10,11... | collective-permute-start | bytes 884744 | tf_op jit(solution)/shard_map/ppermute | solution.py:390
  68.8 0.1 copy.10
  68.9 0.7 reshape.14.dest_ref
  69.5 0.1 copy.9
  69.6 0.7 reshape.13.dest_ref
  70.3 0.6 pad_add_fusion.where
  70.9 5.2 %collective-permute-done.1.refs_1_ = bf16[16,72,128]{2,1,0:T(8,128)(2,1)S(1)} collective-permute-done((bf16[16,72,128]{2,1,0:T(8,128)(2,1)S(1)}, bf16[16,72,128]{2,1,0:T(8,128)(2,1)S(1)}, u32[]{:S(2)}, u32[]{:S(2)}) %collective-permute-start.1) | collective-permute-done | bytes 294944 | tf_op jit(solution)/shard_map/ppermute | solution.py:390
  76.1 0.0 copy-done.2
  76.1 0.0 copy-start.4
  76.1 0.7 copy-done.4
  76.8 3.2 %shard_map.57.refs_2_ = bf16[576,1024]{1,0:T(8,128)(2,1)} custom-call(s32[1,512]{1,0:T(1,128)} %reshape.14.dest_ref, bf16[16,72,128]{2,1,0:T(8,128)(2,1)} %copy-done.2, bf16[16,72,128]{2,1,0:T(8,128)(2,1)} %copy-done.4), custom_call_target="tpu_custom_call" | custom-call | flops 603979776 | bytes 589824 | tf_op jit(solution)/shard_map/pallas_call | solution.py:340
  79.9 0.0 collective-permute-done.refs_1_
  79.9 0.0 copy-done
  79.9 0.0 copy-start.1
  80.0 0.7 copy-done.1
  80.6 7.5 %shard_map.58 = bf16[1,3,2,512,1024]{4,3,2,1,0:T(8,128)(2,1)} custom-call(s32[16]{0:T(128)} %counts.5, s32[2]{0:T(128)} %pad_add_fusion.where, s32[1,512]{1,0:T(1,128)} %reshape.13.dest_ref, bf16[16,72,128]{2,1,0:T(8,128)(2,1)} %copy-done, bf16[16,72,128]{2,1,0:T(8,128)(2,1)} %copy-done.1, bf16[576,1024]{1,0:T(8,128)(2,1)} %shard_map.57.refs_2_), custom_call_target="tpu_custom_call" | custom-call | tf_op jit(solution)/shard_map/pallas_call | solution.py:361
  (4 shorter events, 0.0 us)
Async XLA Ops:
  22.4 28.2 %all-to-all-start = ((bf16[16,72,128]{2,1,0:T(8,128)(2,1)}), bf16[16,72,128]{2,1,0:T(8,128)(2,1)S(1)}, u32[]{:S(2)}, u32[]{:S(2)}) async-start(bf16[16,72,128]{2,1,0:T(8,128)(2,1)} %shard_map.55), calls=%async_computation | async-start | bytes 589824 | tf_op jit(solution)/shard_map/all_to_all | solution.py:389
  29.8 26.9 %copy-start.3 = (s32[512]{0:T(512)S(1)}, s32[512]{0:T(512)}, u32[]{:S(2)}) copy-start(s32[512]{0:T(512)} %param.6) | copy-start | bytes 6148
  50.7 29.3 %copy-start = (bf16[16,72,128]{2,1,0:T(8,128)(2,1)}, bf16[16,72,128]{2,1,0:T(8,128)(2,1)S(1)}, u32[]{:S(2)}) copy-start(bf16[16,72,128]{2,1,0:T(8,128)(2,1)S(1)} %all-to-all-done.refs_0_) | copy-start | bytes 884740
  50.7 16.6 %all-to-all-start.1 = ((bf16[16,72,128]{2,1,0:T(8,128)(2,1)}), bf16[16,72,128]{2,1,0:T(8,128)(2,1)S(1)}, u32[]{:S(2)}, u32[]{:S(2)}) async-start(bf16[16,72,128]{2,1,0:T(8,128)(2,1)} %shard_map.56), calls=%async_computation.1 | async-start | bytes 589824 | tf_op jit(solution)/shard_map/all_to_all | solution.py:389
  57.1 22.8 %collective-permute-start = (bf16[16,72,128]{2,1,0:T(8,128)(2,1)S(1)}, bf16[16,72,128]{2,1,0:T(8,128)(2,1)S(1)}, u32[]{:S(2)}, u32[]{:S(2)}) collective-permute-start(bf16[16,72,128]{2,1,0:T(8,128)(2,1)S(1)} %all-to-all-done.refs_0_), channel_id=1, source_target_pairs={{0,1},{1,0},{2,3},{3,2},{4,5},{5,4},{6,7},{7,6},{8,9},{9,8},{10,11... | collective-permute-start | bytes 884744 | tf_op jit(solution)/shard_map/ppermute | solution.py:390
  67.3 8.8 %copy-start.2 = (bf16[16,72,128]{2,1,0:T(8,128)(2,1)}, bf16[16,72,128]{2,1,0:T(8,128)(2,1)S(1)}, u32[]{:S(2)}) copy-start(bf16[16,72,128]{2,1,0:T(8,128)(2,1)S(1)} %all-to-all-done.1.refs_0_) | copy-start | bytes 884740
  67.3 8.8 %collective-permute-start.1 = (bf16[16,72,128]{2,1,0:T(8,128)(2,1)S(1)}, bf16[16,72,128]{2,1,0:T(8,128)(2,1)S(1)}, u32[]{:S(2)}, u32[]{:S(2)}) collective-permute-start(bf16[16,72,128]{2,1,0:T(8,128)(2,1)S(1)} %all-to-all-done.1.refs_0_), channel_id=1, source_target_pairs={{0,1},{1,0},{2,3},{3,2},{4,5},{5,4},{6,7},{7,6},{8,9},{9,8},{10,11... | collective-permute-start | bytes 884744 | tf_op jit(solution)/shard_map/ppermute | solution.py:390
  76.1 0.7 copy-start.4
  79.9 0.7 copy-start.1

commit v7 on v6

--- a/solution.py
+++ b/solution.py
@@ -45,61 +45,54 @@
     return legendre.T @ vectors[:, :count]
 
 
-SHIFTS = 4
-
-
 def turn_lanes(value, shift):
     shift = shift % LANES
     return pltpu.roll(value, shift, axis=1) if shift else value
 
 
 def packing(band):
-    if 3 * (2 * band + 21) <= 2 * LANES:
-        return 2 * band + 21, 2 * LANES, True
+    if 3 * (2 * band + 16) <= 2 * LANES:
+        return 2 * band + 16, 2 * LANES, True
     count = -(-(2 * band + 32) // (LANES // 2)) * (LANES // 2)
     return count, -(-2 * count // LANES) * LANES, False
 
 
 @functools.lru_cache(maxsize=4)
-def tables(band):
+def tables(band, shifts):
     bf16 = ml_dtypes.bfloat16
     count, packed, triple = packing(band)
     basis = frame_basis(band, count)
     high = basis.astype(bf16)
     low = (basis - high.astype(np.float64)).astype(bf16)
     held = high.astype(np.float64) + low.astype(np.float64)
-    lanes = -(-count // LANES) * LANES
-    analysis = np.zeros((FFT_LEN, 2 * lanes), bf16)
-    analysis[:, :count] = high
-    analysis[:, lanes : lanes + count] = low
+    analysis = np.ascontiguousarray(np.concatenate([high, low], axis=1).T)
 
     phase = 2.0 * math.pi / FFT_LEN * (np.outer(np.arange(FFT_LEN), np.arange(band)) % FFT_LEN)
     wave = np.concatenate([np.cos(phase), -np.sin(phase)], axis=1)
     gram = held.T @ held
     taper = prototype()
-    mixing = np.zeros((TAPS // SHIFTS, 2, packed, SHIFTS, 2 * band), bf16)
+    mixing = np.zeros((TAPS // shifts, 2, packed, shifts, 2 * band), bf16)
     for t in range(TAPS):
         real = np.linalg.solve(gram, held.T @ (taper[t][:, None] * wave))
         imag = np.concatenate([-real[:, band:], real[:, :band]], axis=1)
         for c, full in enumerate((real, imag)):
-            part = mixing[t // SHIFTS, c, :, t % SHIFTS]
+            part = mixing[t // shifts, c, :, t % shifts]
             top = full.astype(bf16)
             part[:count] = top
             part[count : 2 * count] = top
             if triple:
                 part[2 * count : 3 * count] = (full - top.astype(np.float64)).astype(bf16)
-    return analysis, mixing.reshape(-1, SHIFTS * 2 * band)
+    return analysis, mixing.reshape(-1, shifts * 2 * band)
 
 
 def channelizer(
-    band, dests, first, streams, step, queues, counts, v_ref, u_hbm, w_hbm, out_ref,
+    band, dests, first, streams, step, shifts, counts, v_ref, u_hbm, w_hbm, out_ref,
     held, u_ref, w_ref, y, p, x, turned, arrived,
 ):
     i = pl.program_id(0)
     ahead = held.shape[0]
     last = pl.num_programs(0) - 1
     count, packed, triple = packing(band)
-    lanes = u_ref.shape[1] // 2
     rows = 2 * v_ref.shape[2]
     reach = NSPEC + 8
     wide = max(1, 2 * band // LANES)
@@ -119,12 +112,19 @@
 
     def begin(block):
         for r, copy in enumerate(fetch(block)):
-            copy.start(priority=r % queues)
+            copy.start(priority=r % 2)
 
     def analyse():
         signal = held[i % ahead].reshape(step * rows, FFT_LEN)
-        coeff = jnp.dot(signal, u_ref[...], preferred_element_type=jnp.float32)
-        coeff = coeff[:, :lanes] + coeff[:, lanes:]
+        coeff = lax.dot_general(
+            u_ref[...], signal, (((1,), (1,)), ((), ())), preferred_element_type=jnp.float32
+        )
+        coeff = coeff[:count] + coeff[count:]
+        if triple:
+            coeff = jnp.concatenate(
+                [coeff, jnp.zeros((LANES - count, step * rows), jnp.float32)], axis=0
+            )
+        coeff = coeff.T
         high = coeff.astype(jnp.bfloat16).astype(jnp.float32)
         low = coeff - high
         if triple:
@@ -134,7 +134,7 @@
             y[0, : step * rows] = jnp.where(lane < count, high, low)
             y[1, : step * rows] = jnp.where(lane < spare, low, turn_lanes(high, spare))
         else:
-            both = jnp.concatenate([high[:, :count], low[:, :count]], axis=1)
+            both = jnp.concatenate([high, low], axis=1)
             for n in range(packed // LANES):
                 y[n, : step * rows] = both[:, n * LANES : (n + 1) * LANES]
 
@@ -142,8 +142,8 @@
         taps = []
         for r in range(step):
             taps.append(jnp.concatenate([
-                y[n, pl.ds(r * rows + 2 * SHIFTS * m + c, reach, stride=2), :]
-                for m in range(TAPS // SHIFTS) for c in range(2) for n in range(packed // LANES)
+                y[n, pl.ds(r * rows + 2 * shifts * m + c, reach, stride=2), :]
+                for m in range(TAPS // shifts) for c in range(2) for n in range(packed // LANES)
             ], axis=1))
         taps = jnp.concatenate(taps, axis=0).astype(jnp.bfloat16)
         mixed = jnp.dot(taps, w_ref[...], preferred_element_type=jnp.float32)
@@ -154,7 +154,7 @@
             if 2 * band >= LANES:
                 for n in range(wide):
                     x[n, place, :] = sum(
-                        p[wide * h + n, pl.ds(r * reach + h, NSPEC), :] for h in range(SHIFTS)
+                        p[wide * h + n, pl.ds(r * reach + h, NSPEC), :] for h in range(shifts)
                     )
             else:
                 per = LANES // (2 * band)
@@ -162,7 +162,7 @@
                 total = None
                 for u in reversed(range(per)):
                     part = sum(
-                        p[b, pl.ds(r * reach + b * per + u, NSPEC), :] for b in range(SHIFTS // per)
+                        p[b, pl.ds(r * reach + b * per + u, NSPEC), :] for b in range(shifts // per)
                     )
                     total = part if total is None else jnp.where(
                         lane < 2 * band * (u + 1), part, total
@@ -177,6 +177,16 @@
         begin(0)
         for copy in tables_in:
             copy.start()
+        for copy in tables_in:
+            copy.wait()
+
+    @pl.when(i < last)
+    def _():
+        for copy in fetch(i):
+            copy.wait()
+
+    @pl.when(i == 0)
+    def _():
         for block in range(1, min(ahead - 1, streams // step)):
             begin(block)
 
@@ -184,15 +194,8 @@
     def _():
         begin(i + ahead - 1)
 
-    @pl.when(i == 0)
-    def _():
-        for copy in tables_in:
-            copy.wait()
-
     @pl.when(i < last)
     def _():
-        for copy in fetch(i):
-            copy.wait()
         mix(jnp.maximum(i - 1, 0))
         analyse()
 
@@ -225,15 +228,15 @@
         out_ref[...] = turned[...].astype(jnp.bfloat16)
 
 
-def channelize(voltages, chan_counts, dests, start, streams, step, queues):
+def channelize(voltages, chan_counts, dests, start, streams, step, shifts):
     band = 2 * dests
     frames = voltages.shape[2]
-    analysis, mixing = tables(band)
+    analysis, mixing = tables(band, shifts)
     packed = packing(band)[1]
     ahead = 4 if band <= 64 else 2
     payload = 2 * CAP * NSPEC * streams // LANES
     steps = streams // step
-    kernel = functools.partial(channelizer, band, dests, start, streams, step, queues)
+    kernel = functools.partial(channelizer, band, dests, start, streams, step, shifts)
     return pl.pallas_call(
         kernel,
         grid_spec=pltpu.PrefetchScalarGridSpec(
@@ -246,7 +249,7 @@
                 pltpu.VMEM(analysis.shape, jnp.bfloat16),
                 pltpu.VMEM(mixing.shape, jnp.bfloat16),
                 pltpu.VMEM((packed // LANES, step * 2 * frames + 16, LANES), jnp.float32),
-                pltpu.VMEM((SHIFTS * 2 * band // LANES, step * (NSPEC + 8), LANES), jnp.float32),
+                pltpu.VMEM((shifts * 2 * band // LANES, step * (NSPEC + 8), LANES), jnp.float32),
                 pltpu.VMEM((max(1, 2 * band // LANES), NSPEC * streams, LANES), jnp.float32),
                 pltpu.VMEM((dests, payload, LANES), jnp.float32),
                 pltpu.SemaphoreType.DMA((ahead + 1, step)),
@@ -379,13 +382,13 @@
     dests = lax.axis_size("stn")
     streams = voltages.shape[0]
     total = dests * streams
-    plan = ((32, 4, 1), (32, 4, 2)) if streams == 64 else ((streams, 2, 1),)
+    plan = ((32, 4, 4), (32, 4, 8)) if streams == 64 else ((streams, 2, 4),)
     dest = (2 * station_map[:, None] + jnp.arange(2, dtype=jnp.int32)[None, :]).reshape(dests, -1)
     where = jnp.stack([lax.axis_index("stn"), lax.axis_index("blk")]).astype(jnp.int32)
     start = 0
     before = []
-    for size, step, queues in plan:
-        outgoing = channelize(voltages, chan_counts, dests, start, size, step, queues)
+    for size, step, shifts in plan:
+        outgoing = channelize(voltages, chan_counts, dests, start, size, step, shifts)
         own = lax.all_to_all(outgoing, "stn", split_axis=0, concat_axis=0, tiled=True)
         other = lax.ppermute(own, "blk", [(0, 1), (1, 0)])
         place = dest[:, start : start + size].reshape(1, -1)

time: 88.5 us -> 95.7 us (1.081)
  Pallas kernels: 53.9 us -> 61.1 us
    pallas_call x2, Pallas kernels: 43.3 us -> 50.5 us  [channelize(): pl.pallas_call(kernel, grid_spec=pltpu.PrefetchScalarGridSpec(num_scalar_...]
  transfers between devices with their start and end apart: 4 -> 4, of which waited for: 2 -> 2; matrix products, arithmetic and copies ran while one was open for 3% -> 3% of each run, Pallas kernels for 27% -> 29%
where the time goes in v7:
time: 95.7 us; the launch traced here: 95.3 us
  Pallas kernels  61.1 us (64%)
  starting transfers between devices  16.4 us (17%)
  waiting for transfers between devices  13.8 us (14%)
  local copies, waits for them, and re-layouts  3.15 us (3%)
    pallas_call x2, Pallas kernels, channelize(): pl.pallas_call(kernel, grid_spec=pltpu.PrefetchScalarGridSpec(num_scalar_...  50.5 us
    all_to_all x2, starting transfers between devices, body(): lax.all_to_all(outgoing, 'stn', split_axis=0, concat_axis=0, tiled=True)  13.4 us
    all_to_all x2, waiting for transfers between devices, body(): lax.all_to_all(outgoing, 'stn', split_axis=0, concat_axis=0, tiled=True)  8.65 us
    pallas_call x1, Pallas kernels, correlate(): pl.pallas_call(functools.partial(correlator, given), grid_spec=pltpu.Pref...  7.45 us
    ppermute x2, waiting for transfers between devices, body(): other = lax.ppermute(own, 'blk', [(0, 1), (1, 0)])  5.18 us
    pallas_call x1, Pallas kernels, order(): pl.pallas_call(orderer, out_shape=jax.ShapeDtypeStruct((held[0] * held[1]...  3.17 us
    ppermute x2, starting transfers between devices, body(): other = lax.ppermute(own, 'blk', [(0, 1), (1, 0)])  3.06 us
  transfers between devices with their start and end apart: 4, of which 2 were waited for; matrix products, arithmetic and copies ran while one was open for 3% of the time, Pallas kernels for 29%

profile of v7, /device:TPU:0, one launch (start us, length us, event | category | flops | bytes accessed | tf_op | source)
XLA Modules:
  0.0 95.3 jit_solution(11518412668002994108)
XLA Ops:
  0.0 26.4 %shard_map.73 = bf16[16,72,128]{2,1,0:T(8,128)(2,1)} custom-call(s32[16]{0:T(128)} %counts.5, bf16[64,1,63,2,4096]{4,3,2,1,0:T(2,128)(2,1)} %v_ref.3, bf16[160,4096]{1,0:T(8,128)(2,1)} %constant.16.clone.u_hbm, bf16[1024,512]{1,0:T(8,128)(2,1)} %constant.18.clone.w_hbm), custom_call_target="tpu_custom_call" | custom-call | flops 5284823040 | bytes 33030144 | tf_op jit(solution)/shard_map/pallas_call | solution.py:240
  26.4 7.4 %all-to-all-start = ((bf16[16,72,128]{2,1,0:T(8,128)(2,1)}), bf16[16,72,128]{2,1,0:T(8,128)(2,1)S(1)}, u32[]{:S(2)}, u32[]{:S(2)}) async-start(bf16[16,72,128]{2,1,0:T(8,128)(2,1)} %shard_map.73), calls=%async_computation | async-start | bytes 589824 | tf_op jit(solution)/shard_map/all_to_all | solution.py:392
  33.7 0.0 copy-start.3
  33.8 24.1 %shard_map.74 = bf16[16,72,128]{2,1,0:T(8,128)(2,1)} custom-call(s32[16]{0:T(128)} %counts.5, bf16[64,1,63,2,4096]{4,3,2,1,0:T(2,128)(2,1)} %v_ref.3, bf16[160,4096]{1,0:T(8,128)(2,1)} %constant.16.clone.u_hbm, bf16[2048,256]{1,0:T(8,128)(2,1)} %constant.17.clone.w_hbm), custom_call_target="tpu_custom_call" | custom-call | flops 5284823040 | bytes 33030144 | tf_op jit(solution)/shard_map/pallas_call | solution.py:240
  57.9 0.0 all-to-all-done.refs_0_
  57.9 0.0 copy-start
  57.9 6.0 %all-to-all-start.1 = ((bf16[16,72,128]{2,1,0:T(8,128)(2,1)}), bf16[16,72,128]{2,1,0:T(8,128)(2,1)S(1)}, u32[]{:S(2)}, u32[]{:S(2)}) async-start(bf16[16,72,128]{2,1,0:T(8,128)(2,1)} %shard_map.74), calls=%async_computation.1 | async-start | bytes 589824 | tf_op jit(solution)/shard_map/all_to_all | solution.py:392
  63.9 0.0 copy-done.3
  63.9 0.1 add.22
  64.0 0.1 copy.10
  64.1 0.1 add.26
  64.2 0.1 broadcast_add_fusion
  64.3 1.5 %collective-permute-start = (bf16[16,72,128]{2,1,0:T(8,128)(2,1)S(1)}, bf16[16,72,128]{2,1,0:T(8,128)(2,1)S(1)}, u32[]{:S(2)}, u32[]{:S(2)}) collective-permute-start(bf16[16,72,128]{2,1,0:T(8,128)(2,1)S(1)} %all-to-all-done.refs_0_), channel_id=1, source_target_pairs={{0,1},{1,0},{2,3},{3,2},{4,5},{5,4},{6,7},{7,6},{8,9},{9,8},{10,11... | collective-permute-start | bytes 884744 | tf_op jit(solution)/shard_map/ppermute | solution.py:393
  65.8 8.6 %all-to-all-done.1.refs_0_ = bf16[16,72,128]{2,1,0:T(8,128)(2,1)S(1)} async-done(((bf16[16,72,128]{2,1,0:T(8,128)(2,1)}), bf16[16,72,128]{2,1,0:T(8,128)(2,1)S(1)}, u32[]{:S(2)}, u32[]{:S(2)}) %all-to-all-start.1) | async-done | bytes 294944 | tf_op jit(solution)/shard_map/all_to_all | solution.py:392
  74.5 0.0 copy-start.2
  74.5 1.5 %collective-permute-start.1 = (bf16[16,72,128]{2,1,0:T(8,128)(2,1)S(1)}, bf16[16,72,128]{2,1,0:T(8,128)(2,1)S(1)}, u32[]{:S(2)}, u32[]{:S(2)}) collective-permute-start(bf16[16,72,128]{2,1,0:T(8,128)(2,1)S(1)} %all-to-all-done.1.refs_0_), channel_id=1, source_target_pairs={{0,1},{1,0},{2,3},{3,2},{4,5},{5,4},{6,7},{7,6},{8,9},{9,8},{10,11... | collective-permute-start | bytes 884744 | tf_op jit(solution)/shard_map/ppermute | solution.py:393
  76.0 0.1 copy.12
  76.1 0.7 reshape.14.dest_ref
  76.7 0.1 copy.11
  76.8 0.7 reshape.13.dest_ref
  77.5 0.6 pad_add_fusion.where
  78.1 5.2 %collective-permute-done.1.refs_1_ = bf16[16,72,128]{2,1,0:T(8,128)(2,1)S(1)} collective-permute-done((bf16[16,72,128]{2,1,0:T(8,128)(2,1)S(1)}, bf16[16,72,128]{2,1,0:T(8,128)(2,1)S(1)}, u32[]{:S(2)}, u32[]{:S(2)}) %collective-permute-start.1) | collective-permute-done | bytes 294944 | tf_op jit(solution)/shard_map/ppermute | solution.py:393
  83.3 0.0 copy-done.2
  83.3 0.0 copy-start.4
  83.3 0.7 copy-done.4
  84.0 3.2 %shard_map.75.refs_2_ = bf16[576,1024]{1,0:T(8,128)(2,1)} custom-call(s32[1,512]{1,0:T(1,128)} %reshape.14.dest_ref, bf16[16,72,128]{2,1,0:T(8,128)(2,1)} %copy-done.2, bf16[16,72,128]{2,1,0:T(8,128)(2,1)} %copy-done.4), custom_call_target="tpu_custom_call" | custom-call | flops 603979776 | bytes 589824 | tf_op jit(solution)/shard_map/pallas_call | solution.py:343
  87.1 0.0 collective-permute-done.refs_1_
  87.1 0.0 copy-done
  87.1 0.0 copy-start.1
  87.2 0.7 copy-done.1
  87.8 7.5 %shard_map.76 = bf16[1,3,2,512,1024]{4,3,2,1,0:T(8,128)(2,1)} custom-call(s32[16]{0:T(128)} %counts.5, s32[2]{0:T(128)} %pad_add_fusion.where, s32[1,512]{1,0:T(1,128)} %reshape.13.dest_ref, bf16[16,72,128]{2,1,0:T(8,128)(2,1)} %copy-done, bf16[16,72,128]{2,1,0:T(8,128)(2,1)} %copy-done.1, bf16[576,1024]{1,0:T(8,128)(2,1)} %shard_map.75.refs_2_), custom_call_target="tpu_custom_call" | custom-call | tf_op jit(solution)/shard_map/pallas_call | solution.py:364
  (4 shorter events, 0.0 us)
Async XLA Ops:
  26.4 31.5 %all-to-all-start = ((bf16[16,72,128]{2,1,0:T(8,128)(2,1)}), bf16[16,72,128]{2,1,0:T(8,128)(2,1)S(1)}, u32[]{:S(2)}, u32[]{:S(2)}) async-start(bf16[16,72,128]{2,1,0:T(8,128)(2,1)} %shard_map.73), calls=%async_computation | async-start | bytes 589824 | tf_op jit(solution)/shard_map/all_to_all | solution.py:392
  33.7 30.2 %copy-start.3 = (s32[512]{0:T(512)S(1)}, s32[512]{0:T(512)}, u32[]{:S(2)}) copy-start(s32[512]{0:T(512)} %param.8) | copy-start | bytes 6148
  57.9 29.3 %copy-start = (bf16[16,72,128]{2,1,0:T(8,128)(2,1)}, bf16[16,72,128]{2,1,0:T(8,128)(2,1)S(1)}, u32[]{:S(2)}) copy-start(bf16[16,72,128]{2,1,0:T(8,128)(2,1)S(1)} %all-to-all-done.refs_0_) | copy-start | bytes 884740
  57.9 16.6 %all-to-all-start.1 = ((bf16[16,72,128]{2,1,0:T(8,128)(2,1)}), bf16[16,72,128]{2,1,0:T(8,128)(2,1)S(1)}, u32[]{:S(2)}, u32[]{:S(2)}) async-start(bf16[16,72,128]{2,1,0:T(8,128)(2,1)} %shard_map.74), calls=%async_computation.1 | async-start | bytes 589824 | tf_op jit(solution)/shard_map/all_to_all | solution.py:392
  64.3 22.9 %collective-permute-start = (bf16[16,72,128]{2,1,0:T(8,128)(2,1)S(1)}, bf16[16,72,128]{2,1,0:T(8,128)(2,1)S(1)}, u32[]{:S(2)}, u32[]{:S(2)}) collective-permute-start(bf16[16,72,128]{2,1,0:T(8,128)(2,1)S(1)} %all-to-all-done.refs_0_), channel_id=1, source_target_pairs={{0,1},{1,0},{2,3},{3,2},{4,5},{5,4},{6,7},{7,6},{8,9},{9,8},{10,11... | collective-permute-start | bytes 884744 | tf_op jit(solution)/shard_map/ppermute | solution.py:393
  74.5 8.8 %copy-start.2 = (bf16[16,72,128]{2,1,0:T(8,128)(2,1)}, bf16[16,72,128]{2,1,0:T(8,128)(2,1)S(1)}, u32[]{:S(2)}) copy-start(bf16[16,72,128]{2,1,0:T(8,128)(2,1)S(1)} %all-to-all-done.1.refs_0_) | copy-start | bytes 884740
  74.5 8.8 %collective-permute-start.1 = (bf16[16,72,128]{2,1,0:T(8,128)(2,1)S(1)}, bf16[16,72,128]{2,1,0:T(8,128)(2,1)S(1)}, u32[]{:S(2)}, u32[]{:S(2)}) collective-permute-start(bf16[16,72,128]{2,1,0:T(8,128)(2,1)S(1)} %all-to-all-done.1.refs_0_), channel_id=1, source_target_pairs={{0,1},{1,0},{2,3},{3,2},{4,5},{5,4},{6,7},{7,6},{8,9},{9,8},{10,11... | collective-permute-start | bytes 884744 | tf_op jit(solution)/shard_map/ppermute | solution.py:393
  83.3 0.7 copy-start.4
  87.1 0.7 copy-start.1

commit v8 on v6

--- a/solution.py
+++ b/solution.py
@@ -45,7 +45,8 @@
     return legendre.T @ vectors[:, :count]
 
 
-SHIFTS = 4
+def shifts_of(band):
+    return 8 if band <= 64 else 4
 
 
 def turn_lanes(value, shift):
@@ -54,8 +55,8 @@
 
 
 def packing(band):
-    if 3 * (2 * band + 21) <= 2 * LANES:
-        return 2 * band + 21, 2 * LANES, True
+    if 3 * (2 * band + 16) <= 2 * LANES:
+        return 2 * band + 16, 2 * LANES, True
     count = -(-(2 * band + 32) // (LANES // 2)) * (LANES // 2)
     return count, -(-2 * count // LANES) * LANES, False
 
@@ -64,6 +65,7 @@
 def tables(band):
     bf16 = ml_dtypes.bfloat16
     count, packed, triple = packing(band)
+    shifts = shifts_of(band)
     basis = frame_basis(band, count)
     high = basis.astype(bf16)
     low = (basis - high.astype(np.float64)).astype(bf16)
@@ -77,26 +79,27 @@
     wave = np.concatenate([np.cos(phase), -np.sin(phase)], axis=1)
     gram = held.T @ held
     taper = prototype()
-    mixing = np.zeros((TAPS // SHIFTS, 2, packed, SHIFTS, 2 * band), bf16)
+    mixing = np.zeros((TAPS // shifts, 2, packed, shifts, 2 * band), bf16)
     for t in range(TAPS):
         real = np.linalg.solve(gram, held.T @ (taper[t][:, None] * wave))
         imag = np.concatenate([-real[:, band:], real[:, :band]], axis=1)
         for c, full in enumerate((real, imag)):
-            part = mixing[t // SHIFTS, c, :, t % SHIFTS]
+            part = mixing[t // shifts, c, :, t % shifts]
             top = full.astype(bf16)
             part[:count] = top
             part[count : 2 * count] = top
             if triple:
                 part[2 * count : 3 * count] = (full - top.astype(np.float64)).astype(bf16)
-    return analysis, mixing.reshape(-1, SHIFTS * 2 * band)
+    return analysis, mixing.reshape(-1, shifts * 2 * band)
 
 
 def channelizer(
-    band, dests, first, streams, step, queues, counts, v_ref, u_hbm, w_hbm, out_ref,
+    band, dests, first, streams, step, unit, counts, v_ref, u_hbm, w_hbm, out_ref,
     held, u_ref, w_ref, y, p, x, turned, arrived,
 ):
     i = pl.program_id(0)
     ahead = held.shape[0]
+    shifts = shifts_of(band)
     last = pl.num_programs(0) - 1
     count, packed, triple = packing(band)
     lanes = u_ref.shape[1] // 2
@@ -119,7 +122,7 @@
 
     def begin(block):
         for r, copy in enumerate(fetch(block)):
-            copy.start(priority=r % queues)
+            copy.start(priority=r % 2)
 
     def analyse():
         signal = held[i % ahead].reshape(step * rows, FFT_LEN)
@@ -142,19 +145,20 @@
         taps = []
         for r in range(step):
             taps.append(jnp.concatenate([
-                y[n, pl.ds(r * rows + 2 * SHIFTS * m + c, reach, stride=2), :]
-                for m in range(TAPS // SHIFTS) for c in range(2) for n in range(packed // LANES)
+                y[n, pl.ds(r * rows + 2 * shifts * m + c, reach, stride=2), :]
+                for m in range(TAPS // shifts) for c in range(2) for n in range(packed // LANES)
             ], axis=1))
         taps = jnp.concatenate(taps, axis=0).astype(jnp.bfloat16)
         mixed = jnp.dot(taps, w_ref[...], preferred_element_type=jnp.float32)
         for n in range(mixed.shape[1] // LANES):
             p[n] = mixed[:, n * LANES : (n + 1) * LANES]
         for r in range(step):
-            place = pl.ds(block * step + r, NSPEC, stride=streams)
+            stream = block * step + r
+            place = pl.ds(stream // unit * (NSPEC * unit) + stream % unit, NSPEC, stride=unit)
             if 2 * band >= LANES:
                 for n in range(wide):
                     x[n, place, :] = sum(
-                        p[wide * h + n, pl.ds(r * reach + h, NSPEC), :] for h in range(SHIFTS)
+                        p[wide * h + n, pl.ds(r * reach + h, NSPEC), :] for h in range(shifts)
                     )
             else:
                 per = LANES // (2 * band)
@@ -162,7 +166,7 @@
                 total = None
                 for u in reversed(range(per)):
                     part = sum(
-                        p[b, pl.ds(r * reach + b * per + u, NSPEC), :] for b in range(SHIFTS // per)
+                        p[b, pl.ds(r * reach + b * per + u, NSPEC), :] for b in range(shifts // per)
                     )
                     total = part if total is None else jnp.where(
                         lane < 2 * band * (u + 1), part, total
@@ -216,24 +220,26 @@
             pick, spectra.astype(jnp.bfloat16), (((1,), (1,)), ((), ())),
             preferred_element_type=jnp.float32,
         )
-        tiles = NSPEC * streams // LANES
+        tiles = NSPEC * unit // LANES
         for d in range(dests):
-            for t in range(tiles):
-                turned[d, pl.ds(t, 2 * CAP, stride=tiles), :] = out[
+            for t in range(streams // unit * tiles):
+                row = t // tiles * (2 * CAP * tiles) + t % tiles
+                turned[d, pl.ds(row, 2 * CAP, stride=tiles), :] = out[
                     8 * d : 8 * d + 2 * CAP, t * LANES : (t + 1) * LANES
                 ]
         out_ref[...] = turned[...].astype(jnp.bfloat16)
 
 
-def channelize(voltages, chan_counts, dests, start, streams, step, queues):
+def channelize(voltages, chan_counts, dests, start, streams, step, unit):
     band = 2 * dests
     frames = voltages.shape[2]
     analysis, mixing = tables(band)
     packed = packing(band)[1]
+    shifts = shifts_of(band)
     ahead = 4 if band <= 64 else 2
     payload = 2 * CAP * NSPEC * streams // LANES
     steps = streams // step
-    kernel = functools.partial(channelizer, band, dests, start, streams, step, queues)
+    kernel = functools.partial(channelizer, band, dests, start, streams, step, unit)
     return pl.pallas_call(
         kernel,
         grid_spec=pltpu.PrefetchScalarGridSpec(
@@ -246,7 +252,7 @@
                 pltpu.VMEM(analysis.shape, jnp.bfloat16),
                 pltpu.VMEM(mixing.shape, jnp.bfloat16),
                 pltpu.VMEM((packed // LANES, step * 2 * frames + 16, LANES), jnp.float32),
-                pltpu.VMEM((SHIFTS * 2 * band // LANES, step * (NSPEC + 8), LANES), jnp.float32),
+                pltpu.VMEM((shifts * 2 * band // LANES, step * (NSPEC + 8), LANES), jnp.float32),
                 pltpu.VMEM((max(1, 2 * band // LANES), NSPEC * streams, LANES), jnp.float32),
                 pltpu.VMEM((dests, payload, LANES), jnp.float32),
                 pltpu.SemaphoreType.DMA((ahead + 1, step)),
@@ -261,51 +267,55 @@
     )(chan_counts, voltages, jnp.asarray(analysis), jnp.asarray(mixing))
 
 
-def in_order(refs, dest_ref, pre, total):
-    if len(refs) == 2:
-        for h, ref in enumerate(refs):
-            sources, payload = ref.shape[0], ref.shape[1]
-            tiles = payload // (2 * CAP)
-            spread = NSPEC // tiles
-            width = LANES // spread
-            lane = lax.broadcasted_iota(jnp.int32, (payload, LANES), 1)
-            for q in range(sources // spread):
+def gather_streams(refs, apart, pre, unit):
+    spread = LANES // unit
+    tiles = NSPEC // spread
+    base = 0
+    for own, other in zip(refs[::2], refs[1::2]):
+        sources, payload = own.shape[:2]
+        units = payload // (2 * CAP * tiles)
+        lane = lax.broadcasted_iota(jnp.int32, (payload, LANES), 1) // unit
+        for q in range(sources // spread):
+            for h, ref in enumerate((own, other)):
                 parts = [ref[spread * q + a].astype(jnp.float32) for a in range(spread)]
-                groups = []
+                bit = 1
+                while bit < spread:
+                    even = lane // bit % 2 == 0
+                    mixed = []
+                    for a in range(spread):
+                        twin = parts[a ^ bit]
+                        if a & bit:
+                            mixed.append(jnp.where(even, turn_lanes(twin, -unit * bit), parts[a]))
+                        else:
+                            mixed.append(jnp.where(even, parts[a], turn_lanes(twin, unit * bit)))
+                    parts = mixed
+                    bit = 2 * bit
                 for g in range(spread):
-                    group = None
-                    for a in range(spread):
-                        moved = turn_lanes(parts[a], (a - g) * width)
-                        group = moved if a == 0 else jnp.where(lane < a * width, group, moved)
-                    groups.append(group)
-                for part in range(2 * CAP):
-                    rows = slice(part * tiles, (part + 1) * tiles)
-                    both = jnp.concatenate([group[rows] for group in groups], axis=0)
-                    pre[part, h * NSPEC : (h + 1) * NSPEC, q * LANES : (q + 1) * LANES] = (
-                        both.astype(jnp.bfloat16)
-                    )
-    else:
-        pre[...] = refs[0][...]
-    parts, time_len, held = pre.shape
-    spot = lax.broadcasted_iota(jnp.int32, (total, held), 0)
-    turn = jnp.where(spot == dest_ref[...], 1.0, 0.0).astype(jnp.bfloat16)
-    return lax.dot_general(
-        pre[...].reshape(parts * time_len, held), turn, (((1,), (1,)), ((), ())),
-        preferred_element_type=jnp.float32,
-    )
-
-
-def correlator(given, counts, where, dest_ref, *refs):
-    out_ref, pre, post = refs[-3:]
-    refs = refs[:-3]
+                    apart[h, pl.ds(g, payload, stride=spread), :] = parts[g]
+                for u in range(units):
+                    place = base + (u * (sources // spread) + q) * LANES
+                    for part in range(2 * CAP):
+                        row = (u * 2 * CAP + part) * NSPEC
+                        pre[part, h * NSPEC : (h + 1) * NSPEC, place : place + LANES] = apart[
+                            h, row : row + NSPEC
+                        ].astype(jnp.bfloat16)
+        base = base + units * sources * unit
+
+
+def correlator(unit, counts, where, dest_ref, *refs):
+    out_ref, apart, pre, post = refs[-4:]
     k = pl.program_id(0)
-    time_len = pre.shape[1]
+    time_len, total = pre.shape[1:]
 
     @pl.when(k == 0)
     def _():
-        ordered = in_order(refs[:given], dest_ref, pre, post.shape[2])
-        for ref in refs[given:]:
-            ordered = ordered + ref[...].astype(jnp.float32)
+        gather_streams(refs[:-4], apart, pre, unit)
+        spot = lax.broadcasted_iota(jnp.int32, (total, total), 0)
+        turn = jnp.where(spot == dest_ref[...], 1.0, 0.0).astype(jnp.bfloat16)
+        ordered = lax.dot_general(
+            pre[...].reshape(2 * CAP * time_len, total), turn, (((1,), (1,)), ((), ())),
+            preferred_element_type=jnp.float32,
+        )
         post[...] = ordered.astype(jnp.bfloat16).reshape(post.shape)
 
     rows = out_ref.shape[3]
@@ -320,53 +330,24 @@
         out_ref[0, 0, part] = (vis * valid).astype(jnp.bfloat16)
 
 
-def orderer(dest_ref, *refs):
-    out_ref, pre = refs[-2:]
-    out_ref[...] = in_order(refs[:-2], dest_ref, pre, out_ref.shape[1]).astype(jnp.bfloat16)
-
-
-def halves(own, other):
-    sources, payload = own.shape[:2]
-    spread = 2 * CAP * NSPEC // payload
-    held = (2 * CAP, 2 * NSPEC, sources * LANES // spread)
-    if spread <= 4:
-        return [own, other], held
-    both = jnp.stack([own, other]).reshape(2, sources, 2 * CAP, NSPEC // spread, spread, -1)
-    return [both.transpose(2, 0, 3, 4, 1, 5).reshape(held)], held
-
-
-def order(own, other, dest, total):
-    operands, held = halves(own, other)
-    return pl.pallas_call(
-        orderer,
-        out_shape=jax.ShapeDtypeStruct((held[0] * held[1], total), jnp.bfloat16),
-        scratch_shapes=[pltpu.VMEM(held, jnp.bfloat16)],
-        compiler_params=pltpu.CompilerParams(vmem_limit_bytes=60 * 1024 * 1024),
-        cost_estimate=pl.CostEstimate(
-            flops=2 * held[0] * held[1] * held[2] * total, bytes_accessed=4 * own.size,
-            transcendentals=0,
-        ),
-    )(dest, *operands)
-
-
-def correlate(own, other, dest, before, chan_counts, where, total):
-    operands, held = halves(own, other)
-    given = len(operands)
-    operands = operands + before
+def correlate(operands, dest, chan_counts, where, unit):
+    total = dest.shape[1]
+    most = max(a.shape[1] for a in operands)
     specs = [
         pl.BlockSpec(a.shape, functools.partial(lambda n, k, c, w: (0,) * n, a.ndim))
         for a in [dest] + operands
     ]
     rows = total // 2
     return pl.pallas_call(
-        functools.partial(correlator, given),
+        functools.partial(correlator, unit),
         grid_spec=pltpu.PrefetchScalarGridSpec(
             num_scalar_prefetch=2,
             grid=(CAP,),
             in_specs=specs,
             out_specs=pl.BlockSpec((1, 1, 2, rows, total), lambda k, c, w: (0, k, 0, 0, 0)),
             scratch_shapes=[
-                pltpu.VMEM(held, jnp.bfloat16),
+                pltpu.VMEM((2, most * LANES // unit, LANES), jnp.float32),
+                pltpu.VMEM((2 * CAP, 2 * NSPEC, total), jnp.bfloat16),
                 pltpu.VMEM((CAP, 4 * NSPEC, total), jnp.bfloat16),
             ],
         ),
@@ -378,21 +359,20 @@
 def body(voltages, station_map, chan_counts):
     dests = lax.axis_size("stn")
     streams = voltages.shape[0]
-    total = dests * streams
-    plan = ((32, 4, 1), (32, 4, 2)) if streams == 64 else ((streams, 2, 1),)
-    dest = (2 * station_map[:, None] + jnp.arange(2, dtype=jnp.int32)[None, :]).reshape(dests, -1)
-    where = jnp.stack([lax.axis_index("stn"), lax.axis_index("blk")]).astype(jnp.int32)
+    unit = min(streams, 16)
+    plan = ((48, 4), (16, 4)) if streams == 64 else ((streams, 2),)
+    operands = []
     start = 0
-    before = []
-    for size, step, queues in plan:
-        outgoing = channelize(voltages, chan_counts, dests, start, size, step, queues)
+    for size, step in plan:
+        outgoing = channelize(voltages, chan_counts, dests, start, size, step, unit)
         own = lax.all_to_all(outgoing, "stn", split_axis=0, concat_axis=0, tiled=True)
         other = lax.ppermute(own, "blk", [(0, 1), (1, 0)])
-        place = dest[:, start : start + size].reshape(1, -1)
+        operands += [own, other]
         start = start + size
-        if start < streams:
-            before.append(order(own, other, place, total))
-    return correlate(own, other, place, before, chan_counts, where, total)
+    dest = (2 * station_map[:, None] + jnp.arange(2, dtype=jnp.int32)[None, :]).reshape(-1)
+    dest = dest.reshape(dests, streams // unit, unit).transpose(1, 0, 2).reshape(1, -1)
+    where = jnp.stack([lax.axis_index("stn"), lax.axis_index("blk")]).astype(jnp.int32)
+    return correlate(operands, dest, chan_counts, where, unit)
 
 
 def solution(mesh):

time: 88.5 us -> 83.5 us (0.944)
  waiting for transfers between devices: 13.8 us -> 11.5 us
  Pallas kernels: 53.9 us -> 51.9 us
    all_to_all x2, waiting for transfers between devices: 8.66 us -> 6.6 us  [body(): lax.all_to_all(outgoing, 'stn', split_axis=0, concat_axis=0, tiled=True)]
    pallas_call x2 -> x1, Pallas kernels: 10.6 us -> 9.4 us  [correlate(): pl.pallas_call(functools.partial(correlator, unit), grid_spec=pltpu.Prefe...]
  transfers between devices with their start and end apart: 4 -> 4, of which waited for: 2 -> 2; matrix products, arithmetic and copies ran while one was open for 3% -> 2% of each run, Pallas kernels for 27% -> 17%
where the time goes in v8:
time: 83.5 us; the launch traced here: 83.1 us
  Pallas kernels  51.9 us (62%)
  starting transfers between devices  16.5 us (20%)
  waiting for transfers between devices  11.5 us (14%)
  local copies, waits for them, and re-layouts  2.46 us (3%)
    pallas_call x2, Pallas kernels, channelize(): pl.pallas_call(kernel, grid_spec=pltpu.PrefetchScalarGridSpec(num_scalar_...  42.5 us
    all_to_all x2, starting transfers between devices, body(): lax.all_to_all(outgoing, 'stn', split_axis=0, concat_axis=0, tiled=True)  13.4 us
    pallas_call x1, Pallas kernels, correlate(): pl.pallas_call(functools.partial(correlator, unit), grid_spec=pltpu.Prefe...  9.4 us
    all_to_all x2, waiting for transfers between devices, body(): lax.all_to_all(outgoing, 'stn', split_axis=0, concat_axis=0, tiled=True)  6.6 us
    ppermute x2, waiting for transfers between devices, body(): other = lax.ppermute(own, 'blk', [(0, 1), (1, 0)])  4.91 us
    ppermute x2, starting transfers between devices, body(): other = lax.ppermute(own, 'blk', [(0, 1), (1, 0)])  3.11 us
  transfers between devices with their start and end apart: 4, of which 2 were waited for; matrix products, arithmetic and copies ran while one was open for 2% of the time, Pallas kernels for 17%

profile of v8, /device:TPU:0, one launch (start us, length us, event | category | flops | bytes accessed | tf_op | source)
XLA Modules:
  0.0 83.1 jit_solution(10300876997073254023)
XLA Ops:
  0.0 28.3 %shard_map.55 = bf16[16,108,128]{2,1,0:T(8,128)(2,1)} custom-call(s32[16]{0:T(128)} %counts.5, bf16[64,1,63,2,4096]{4,3,2,1,0:T(2,128)(2,1)} %v_ref.3, bf16[4096,256]{1,0:T(8,128)(2,1)} %constant.14.clone.u_hbm, bf16[1024,512]{1,0:T(8,128)(2,1)} %constant.15.clone.w_hbm), custom_call_target="tpu_custom_call" | custom-call | flops 12683575296 | bytes 49545216 | tf_op jit(solution)/shard_map/pallas_call | solution.py:243
  28.3 7.3 %all-to-all-start = ((bf16[16,108,128]{2,1,0:T(8,128)(2,1)}), bf16[16,108,128]{2,1,0:T(8,128)(2,1)S(1)}, u32[]{:S(2)}, u32[]{:S(2)}) async-start(bf16[16,108,128]{2,1,0:T(8,128)(2,1)} %shard_map.55), calls=%async_computation | async-start | bytes 917504 | tf_op jit(solution)/shard_map/all_to_all | solution.py:368
  35.7 0.0 copy-start.4
  35.7 14.2 %shard_map.56 = bf16[16,36,128]{2,1,0:T(8,128)(2,1)} custom-call(s32[16]{0:T(128)} %counts.5, bf16[64,1,63,2,4096]{4,3,2,1,0:T(2,128)(2,1)} %v_ref.3, bf16[4096,256]{1,0:T(8,128)(2,1)} %constant.14.clone.u_hbm, bf16[1024,512]{1,0:T(8,128)(2,1)} %constant.15.clone.w_hbm), custom_call_target="tpu_custom_call" | custom-call | flops 4227858432 | bytes 16515072 | tf_op jit(solution)/shard_map/pallas_call | solution.py:243
  49.9 0.0 all-to-all-done.refs_0_
  49.9 0.0 copy-start
  49.9 6.0 %all-to-all-start.1 = ((bf16[16,36,128]{2,1,0:T(8,128)(2,1)}), bf16[16,36,128]{2,1,0:T(8,128)(2,1)S(1)}, u32[]{:S(2)}, u32[]{:S(2)}) async-start(bf16[16,36,128]{2,1,0:T(8,128)(2,1)} %shard_map.56), calls=%async_computation.1 | async-start | bytes 327680 | tf_op jit(solution)/shard_map/all_to_all | solution.py:368
  55.9 1.6 %collective-permute-start = (bf16[16,108,128]{2,1,0:T(8,128)(2,1)S(1)}, bf16[16,108,128]{2,1,0:T(8,128)(2,1)S(1)}, u32[]{:S(2)}, u32[]{:S(2)}) collective-permute-start(bf16[16,108,128]{2,1,0:T(8,128)(2,1)S(1)} %all-to-all-done.refs_0_), channel_id=1, source_target_pairs={{0,1},{1,0},{2,3},{3,2},{4,5},{5,4},{6,7},{7,6},{8,9},{9,8},{10,11... | collective-permute-start | bytes 1327112 | tf_op jit(solution)/shard_map/ppermute | solution.py:369
  57.5 0.0 copy-done.4
  57.5 0.1 add.26
  57.6 0.1 add.22
  57.7 0.1 copy.6
  57.8 6.6 %all-to-all-done.1.refs_2_ = bf16[16,36,128]{2,1,0:T(8,128)(2,1)S(1)} async-done(((bf16[16,36,128]{2,1,0:T(8,128)(2,1)}), bf16[16,36,128]{2,1,0:T(8,128)(2,1)S(1)}, u32[]{:S(2)}, u32[]{:S(2)}) %all-to-all-start.1) | async-done | bytes 147488 | tf_op jit(solution)/shard_map/all_to_all | solution.py:368
  64.4 0.0 copy-start.1
  64.4 1.5 %collective-permute-start.1 = (bf16[16,36,128]{2,1,0:T(8,128)(2,1)S(1)}, bf16[16,36,128]{2,1,0:T(8,128)(2,1)S(1)}, u32[]{:S(2)}, u32[]{:S(2)}) collective-permute-start(bf16[16,36,128]{2,1,0:T(8,128)(2,1)S(1)} %all-to-all-done.1.refs_2_), channel_id=1, source_target_pairs={{0,1},{1,0},{2,3},{3,2},{4,5},{5,4},{6,7},{7,6},{8,9},{9,8},{10,11... | collective-permute-start | bytes 442376 | tf_op jit(solution)/shard_map/ppermute | solution.py:369
  65.9 0.1 add_bitcast_fusion
  66.0 0.1 copy.7
  66.1 0.7 reshape.9.dest_ref
  66.7 0.6 pad_add_fusion.where
  67.3 4.9 %collective-permute-done.1.refs_3_ = bf16[16,36,128]{2,1,0:T(8,128)(2,1)S(1)} collective-permute-done((bf16[16,36,128]{2,1,0:T(8,128)(2,1)S(1)}, bf16[16,36,128]{2,1,0:T(8,128)(2,1)S(1)}, u32[]{:S(2)}, u32[]{:S(2)}) %collective-permute-start.1) | collective-permute-done | bytes 147488 | tf_op jit(solution)/shard_map/ppermute | solution.py:369
  72.3 0.0 copy-start.3
  72.3 0.0 collective-permute-done.refs_1_
  72.3 0.0 copy-done
  72.3 0.0 copy-done.1
  72.3 0.6 copy-done.3
  72.9 0.0 copy-start.2
  72.9 0.8 copy-done.2
  73.7 9.4 %shard_map.57 = bf16[1,3,2,512,1024]{4,3,2,1,0:T(8,128)(2,1)} custom-call(s32[16]{0:T(128)} %counts.5, s32[2]{0:T(128)} %pad_add_fusion.where, s32[1,1024]{1,0:T(1,128)} %reshape.9.dest_ref, bf16[16,108,128]{2,1,0:T(8,128)(2,1)} %copy-done, bf16[16,108,128]{2,1,0:T(8,128)(2,1)} %copy-done.2, bf16[16,36,128]{2,1,0:T(8,128)(2,1)} %copy-done.1, ...), custom_call_target="tpu_custom_call" | custom-call | tf_op jit(solution)/shard_map/pallas_call | solution.py:341
  (3 shorter events, 0.0 us)
Async XLA Ops:
  28.3 21.6 %all-to-all-start = ((bf16[16,108,128]{2,1,0:T(8,128)(2,1)}), bf16[16,108,128]{2,1,0:T(8,128)(2,1)S(1)}, u32[]{:S(2)}, u32[]{:S(2)}) async-start(bf16[16,108,128]{2,1,0:T(8,128)(2,1)} %shard_map.55), calls=%async_computation | async-start | bytes 917504 | tf_op jit(solution)/shard_map/all_to_all | solution.py:368
  35.7 21.8 %copy-start.4 = (s32[512]{0:T(512)S(1)}, s32[512]{0:T(512)}, u32[]{:S(2)}) copy-start(s32[512]{0:T(512)} %param.6) | copy-start | bytes 6148
  49.9 22.4 %copy-start = (bf16[16,108,128]{2,1,0:T(8,128)(2,1)}, bf16[16,108,128]{2,1,0:T(8,128)(2,1)S(1)}, u32[]{:S(2)}) copy-start(bf16[16,108,128]{2,1,0:T(8,128)(2,1)S(1)} %all-to-all-done.refs_0_) | copy-start | bytes 1327108
  49.9 14.5 %all-to-all-start.1 = ((bf16[16,36,128]{2,1,0:T(8,128)(2,1)}), bf16[16,36,128]{2,1,0:T(8,128)(2,1)S(1)}, u32[]{:S(2)}, u32[]{:S(2)}) async-start(bf16[16,36,128]{2,1,0:T(8,128)(2,1)} %shard_map.56), calls=%async_computation.1 | async-start | bytes 327680 | tf_op jit(solution)/shard_map/all_to_all | solution.py:368
  55.9 16.4 %collective-permute-start = (bf16[16,108,128]{2,1,0:T(8,128)(2,1)S(1)}, bf16[16,108,128]{2,1,0:T(8,128)(2,1)S(1)}, u32[]{:S(2)}, u32[]{:S(2)}) collective-permute-start(bf16[16,108,128]{2,1,0:T(8,128)(2,1)S(1)} %all-to-all-done.refs_0_), channel_id=1, source_target_pairs={{0,1},{1,0},{2,3},{3,2},{4,5},{5,4},{6,7},{7,6},{8,9},{9,8},{10,11... | collective-permute-start | bytes 1327112 | tf_op jit(solution)/shard_map/ppermute | solution.py:369
  64.4 7.9 %copy-start.1 = (bf16[16,36,128]{2,1,0:T(8,128)(2,1)}, bf16[16,36,128]{2,1,0:T(8,128)(2,1)S(1)}, u32[]{:S(2)}) copy-start(bf16[16,36,128]{2,1,0:T(8,128)(2,1)S(1)} %all-to-all-done.1.refs_2_) | copy-start | bytes 442372
  64.4 7.9 %collective-permute-start.1 = (bf16[16,36,128]{2,1,0:T(8,128)(2,1)S(1)}, bf16[16,36,128]{2,1,0:T(8,128)(2,1)S(1)}, u32[]{:S(2)}, u32[]{:S(2)}) collective-permute-start(bf16[16,36,128]{2,1,0:T(8,128)(2,1)S(1)} %all-to-all-done.1.refs_2_), channel_id=1, source_target_pairs={{0,1},{1,0},{2,3},{3,2},{4,5},{5,4},{6,7},{7,6},{8,9},{9,8},{10,11... | collective-permute-start | bytes 442376 | tf_op jit(solution)/shard_map/ppermute | solution.py:369
  72.3 0.7 copy-start.3
  72.9 0.8 copy-start.2

commit v9 on v8

--- a/solution.py
+++ b/solution.py
@@ -181,6 +181,7 @@
         begin(0)
         for copy in tables_in:
             copy.start()
+        turned[...] = jnp.zeros(turned.shape, jnp.float32)
         for block in range(1, min(ahead - 1, streams // step)):
             begin(block)
 
@@ -237,7 +238,7 @@
     packed = packing(band)[1]
     shifts = shifts_of(band)
     ahead = 4 if band <= 64 else 2
-    payload = 2 * CAP * NSPEC * streams // LANES
+    payload = payload_rows(streams // unit, unit)
     steps = streams // step
     kernel = functools.partial(channelizer, band, dests, start, streams, step, unit)
     return pl.pallas_call(
@@ -259,7 +260,9 @@
             ],
         ),
         out_shape=jax.ShapeDtypeStruct((dests, payload, LANES), jnp.bfloat16),
-        compiler_params=pltpu.CompilerParams(vmem_limit_bytes=60 * 1024 * 1024),
+        compiler_params=pltpu.CompilerParams(
+            vmem_limit_bytes=(32 if band <= 64 else 60) * 1024 * 1024
+        ),
         cost_estimate=pl.CostEstimate(
             flops=2 * streams * 2 * frames * analysis.size,
             bytes_accessed=2 * 2 * frames * FFT_LEN * streams, transcendentals=0,
@@ -267,112 +270,192 @@
     )(chan_counts, voltages, jnp.asarray(analysis), jnp.asarray(mixing))
 
 
-def gather_streams(refs, apart, pre, unit):
+def payload_rows(units, unit):
+    return -(-units * 2 * CAP * NSPEC * unit // (16 * LANES)) * 16
+
+
+def streams_in(part, unit):
+    return part.shape[0] * unit * (part.shape[1] * LANES // (2 * CAP * NSPEC * unit))
+
+
+def regroup(ref, apart, pre, unit, base):
     spread = LANES // unit
-    tiles = NSPEC // spread
-    base = 0
-    for own, other in zip(refs[::2], refs[1::2]):
-        sources, payload = own.shape[:2]
-        units = payload // (2 * CAP * tiles)
-        lane = lax.broadcasted_iota(jnp.int32, (payload, LANES), 1) // unit
-        for q in range(sources // spread):
-            for h, ref in enumerate((own, other)):
-                parts = [ref[spread * q + a].astype(jnp.float32) for a in range(spread)]
-                bit = 1
-                while bit < spread:
-                    even = lane // bit % 2 == 0
-                    mixed = []
-                    for a in range(spread):
-                        twin = parts[a ^ bit]
-                        if a & bit:
-                            mixed.append(jnp.where(even, turn_lanes(twin, -unit * bit), parts[a]))
-                        else:
-                            mixed.append(jnp.where(even, parts[a], turn_lanes(twin, unit * bit)))
-                    parts = mixed
-                    bit = 2 * bit
-                for g in range(spread):
-                    apart[h, pl.ds(g, payload, stride=spread), :] = parts[g]
-                for u in range(units):
-                    place = base + (u * (sources // spread) + q) * LANES
-                    for part in range(2 * CAP):
-                        row = (u * 2 * CAP + part) * NSPEC
-                        pre[part, h * NSPEC : (h + 1) * NSPEC, place : place + LANES] = apart[
-                            h, row : row + NSPEC
-                        ].astype(jnp.bfloat16)
-        base = base + units * sources * unit
-
-
-def correlator(unit, counts, where, dest_ref, *refs):
-    out_ref, apart, pre, post = refs[-4:]
+    sources, payload = ref.shape[:2]
+    units = streams_in(ref, unit) // (sources * unit)
+    lane = lax.broadcasted_iota(jnp.int32, (payload, LANES), 1) // unit
+    for q in range(sources // spread):
+        parts = [ref[spread * q + a].astype(jnp.float32) for a in range(spread)]
+        bit = 1
+        while bit < spread:
+            even = lane // bit % 2 == 0
+            mixed = []
+            for a in range(spread):
+                twin = parts[a ^ bit]
+                if a & bit:
+                    mixed.append(jnp.where(even, turn_lanes(twin, -unit * bit), parts[a]))
+                else:
+                    mixed.append(jnp.where(even, parts[a], turn_lanes(twin, unit * bit)))
+            parts = mixed
+            bit = 2 * bit
+        slot = q % 2
+        for g in range(spread):
+            apart[slot, pl.ds(g, payload, stride=spread), :] = parts[g]
+        rows = 2 * CAP * NSPEC
+        for u in range(units):
+            place = base + (u * (sources // spread) + q) * LANES
+            pre[:, place : place + LANES] = apart[slot, u * rows : (u + 1) * rows].astype(jnp.bfloat16)
+
+
+def one_hot(dest, total):
+    spot = lax.broadcasted_iota(jnp.int32, (total, dest.shape[1]), 0)
+    return jnp.where(spot == dest, 1.0, 0.0).astype(jnp.bfloat16)
+
+
+def permute(rows, turn):
+    return lax.dot_general(
+        rows, turn, (((1,), (1,)), ((), ())), preferred_element_type=jnp.float32
+    )
+
+
+def settler(unit, dest_ref, part_hbm, out_ref, part, apart, pre, arrived):
+    copy = pltpu.make_async_copy(part_hbm, part, arrived)
+    copy.start()
+    turn = one_hot(dest_ref[...], out_ref.shape[1])
+    copy.wait()
+    regroup(part, apart, pre, unit, 0)
+    out_ref[...] = permute(pre[...], turn).astype(jnp.bfloat16)
+
+
+def settle(part, dest, total, unit):
+    rows = 2 * CAP * NSPEC
+    return pl.pallas_call(
+        functools.partial(settler, unit),
+        in_specs=[pl.BlockSpec(memory_space=pltpu.VMEM), pl.BlockSpec(memory_space=pl.ANY)],
+        out_specs=pl.BlockSpec(memory_space=pltpu.VMEM),
+        out_shape=jax.ShapeDtypeStruct((rows, total), jnp.bfloat16),
+        scratch_shapes=[
+            pltpu.VMEM(part.shape, jnp.bfloat16),
+            pltpu.VMEM((2, part.shape[1] * LANES // unit, LANES), jnp.float32),
+            pltpu.VMEM((rows, dest.shape[1]), jnp.bfloat16),
+            pltpu.SemaphoreType.DMA,
+        ],
+        compiler_params=pltpu.CompilerParams(vmem_limit_bytes=32 * 1024 * 1024),
+        cost_estimate=pl.CostEstimate(
+            flops=2 * rows * dest.shape[1] * total, bytes_accessed=2 * part.size + 2 * rows * total,
+            transcendentals=0,
+        ),
+    )(dest, part)
+
+
+def correlator(unit, own_count, counts, where, dest_ref, *refs):
+    given = (len(refs) - 6) // 2
+    sources, out_ref, held = refs[:given], refs[given], refs[given + 1 : 2 * given + 1]
+    apart, pre, post, near, arrived = refs[2 * given + 1 :]
     k = pl.program_id(0)
-    time_len, total = pre.shape[1:]
-
-    @pl.when(k == 0)
-    def _():
-        gather_streams(refs[:-4], apart, pre, unit)
-        spot = lax.broadcasted_iota(jnp.int32, (total, total), 0)
-        turn = jnp.where(spot == dest_ref[...], 1.0, 0.0).astype(jnp.bfloat16)
-        ordered = lax.dot_general(
-            pre[...].reshape(2 * CAP * time_len, total), turn, (((1,), (1,)), ((), ())),
-            preferred_element_type=jnp.float32,
-        )
-        post[...] = ordered.astype(jnp.bfloat16).reshape(post.shape)
-
+    part = pl.program_id(1)
+    total = post.shape[2]
     rows = out_ref.shape[3]
-    every = post[k]
-    near = post[k, :, pl.ds(pl.multiple_of(where[1] * rows, LANES), rows)]
-    turned = jnp.concatenate([near[time_len:], -near[:time_len]], axis=0)
+    time_len = 2 * NSPEC
+
+    @pl.when((k == 0) & (part == 0))
+    def _():
+        copies = [
+            pltpu.make_async_copy(a, b, arrived.at[n]) for n, (a, b) in enumerate(zip(sources, held))
+        ]
+        for copy in copies:
+            copy.start()
+        turn = one_hot(dest_ref[...], total)
+        for copy in copies:
+            copy.wait()
+        other = held[:-own_count]
+        ours = held[len(held) - own_count :]
+        base = 0
+        for ref in other:
+            regroup(ref, apart, pre, unit, base)
+            base += streams_in(ref, unit)
+        halves = [permute(pre[...], turn)]
+        fresh = ours[0]
+        width = streams_in(fresh, unit)
+        regroup(fresh, apart, pre, unit, total - width)
+        mine = permute(pre[:, total - width :], turn[:, total - width :])
+        for ref in ours[1:]:
+            mine = mine + ref[...].astype(jnp.float32)
+        halves.append(mine)
+        for n in range(2 * CAP):
+            for h, half in enumerate(halves):
+                first = n % 2 * time_len + h * NSPEC
+                post[n // 2, first : first + NSPEC] = half[n * NSPEC : (n + 1) * NSPEC].astype(
+                    jnp.bfloat16
+                )
+
+    @pl.when(part == 0)
+    def _():
+        mine = post[k, :, pl.ds(pl.multiple_of(where[1] * rows, LANES), rows)]
+        near[...] = mine.T
+
     valid = jnp.where(k < counts[where[0]], 1.0, 0.0) / jnp.float32(time_len)
-    for part, left in enumerate((near, turned)):
-        vis = lax.dot_general(
-            left, every, (((0,), (0,)), ((), ())), preferred_element_type=jnp.float32
-        )
-        out_ref[0, 0, part] = (vis * valid).astype(jnp.bfloat16)
-
-
-def correlate(operands, dest, chan_counts, where, unit):
+
+    def put(right):
+        vis = jnp.dot(near[...], right, preferred_element_type=jnp.float32)
+        out_ref[0, 0, 0] = (vis * valid).astype(jnp.bfloat16)
+
+    @pl.when(part == 0)
+    def _():
+        put(post[k])
+
+    @pl.when(part == 1)
+    def _():
+        put(jnp.concatenate([-post[k, time_len:], post[k, :time_len]], axis=0))
+
+
+def correlate(others, ours, dest, chan_counts, where, unit):
     total = dest.shape[1]
-    most = max(a.shape[1] for a in operands)
-    specs = [
-        pl.BlockSpec(a.shape, functools.partial(lambda n, k, c, w: (0,) * n, a.ndim))
-        for a in [dest] + operands
-    ]
+    operands = others + ours
+    most = max(a.shape[1] for a in operands if a.ndim == 3)
     rows = total // 2
     return pl.pallas_call(
-        functools.partial(correlator, unit),
+        functools.partial(correlator, unit, len(ours)),
         grid_spec=pltpu.PrefetchScalarGridSpec(
             num_scalar_prefetch=2,
-            grid=(CAP,),
-            in_specs=specs,
-            out_specs=pl.BlockSpec((1, 1, 2, rows, total), lambda k, c, w: (0, k, 0, 0, 0)),
-            scratch_shapes=[
+            grid=(CAP, 2),
+            in_specs=[pl.BlockSpec((1, total), lambda k, p, c, w: (0, 0))]
+            + [pl.BlockSpec(memory_space=pl.ANY)] * len(operands),
+            out_specs=pl.BlockSpec((1, 1, 1, rows, total), lambda k, p, c, w: (0, k, p, 0, 0)),
+            scratch_shapes=[pltpu.VMEM(a.shape, jnp.bfloat16) for a in operands]
+            + [
                 pltpu.VMEM((2, most * LANES // unit, LANES), jnp.float32),
-                pltpu.VMEM((2 * CAP, 2 * NSPEC, total), jnp.bfloat16),
+                pltpu.VMEM((2 * CAP * NSPEC, total), jnp.bfloat16),
                 pltpu.VMEM((CAP, 4 * NSPEC, total), jnp.bfloat16),
+                pltpu.VMEM((rows, 4 * NSPEC), jnp.bfloat16),
+                pltpu.SemaphoreType.DMA((len(operands),)),
             ],
         ),
         out_shape=jax.ShapeDtypeStruct((1, CAP, 2, rows, total), jnp.bfloat16),
-        compiler_params=pltpu.CompilerParams(vmem_limit_bytes=60 * 1024 * 1024),
+        compiler_params=pltpu.CompilerParams(vmem_limit_bytes=32 * 1024 * 1024),
     )(chan_counts, where, dest, *operands)
 
 
 def body(voltages, station_map, chan_counts):
     dests = lax.axis_size("stn")
     streams = voltages.shape[0]
+    total = dests * streams
     unit = min(streams, 16)
-    plan = ((48, 4), (16, 4)) if streams == 64 else ((streams, 2),)
-    operands = []
-    start = 0
-    for size, step in plan:
-        outgoing = channelize(voltages, chan_counts, dests, start, size, step, unit)
-        own = lax.all_to_all(outgoing, "stn", split_axis=0, concat_axis=0, tiled=True)
-        other = lax.ppermute(own, "blk", [(0, 1), (1, 0)])
-        operands += [own, other]
-        start = start + size
+    plan = (48, 16) if streams == 64 else (streams,)
     dest = (2 * station_map[:, None] + jnp.arange(2, dtype=jnp.int32)[None, :]).reshape(-1)
     dest = dest.reshape(dests, streams // unit, unit).transpose(1, 0, 2).reshape(1, -1)
     where = jnp.stack([lax.axis_index("stn"), lax.axis_index("blk")]).astype(jnp.int32)
-    return correlate(operands, dest, chan_counts, where, unit)
+    others, settled = [], []
+    start = 0
+    for size in plan:
+        outgoing = channelize(voltages, chan_counts, dests, start, size, 2, unit)
+        chan_counts, outgoing = lax.optimization_barrier((chan_counts, outgoing))
+        own = lax.all_to_all(outgoing, "stn", split_axis=0, concat_axis=0, tiled=True)
+        others.append(lax.ppermute(own, "blk", [(0, 1), (1, 0)]))
+        if start + size < streams:
+            spots = dest[:, start * dests : (start + size) * dests]
+            settled.append(settle(own, spots, total, unit))
+        start = start + size
+    return correlate(others, [own] + settled, dest, chan_counts, where, unit)
 
 
 def solution(mesh):

time: 83.5 us -> 85.8 us (1.028)
  local copies, waits for them, and re-layouts: 2.46 us -> 4.69 us
    unnamed x10 -> x16, local copies, waits for them, and re-layouts: 1.43 us -> 4.25 us
    pallas_call x1 -> x2, Pallas kernels: 9.4 us -> 11.4 us  [the longest x1 9.11 us: correlate(): pl.pallas_call(functools.partial(correlator, unit, len(ours)), grid_spec=...]
    all_to_all x2, waiting for transfers between devices: 6.6 us -> 7.8 us  [body(): lax.all_to_all(outgoing, 'stn', split_axis=0, concat_axis=0, tiled=True)]
    pallas_call x2, Pallas kernels: 42.5 us -> 41.3 us  [channelize(): pl.pallas_call(kernel, grid_spec=pltpu.PrefetchScalarGridSpec(num_scalar_...]
  transfers between devices with their start and end apart: 4 -> 4, of which waited for: 2 -> 3; matrix products, arithmetic and copies ran while one was open for 2% -> 1% of each run, Pallas kernels for 17% -> 17%
where the time goes in v9:
time: 85.8 us; the launch traced here: 85.4 us
  Pallas kernels  52.6 us (61%)
  starting transfers between devices  15.8 us (18%)
  waiting for transfers between devices  11.9 us (14%)
  local copies, waits for them, and re-layouts  4.69 us (5%)
    pallas_call x2, Pallas kernels, channelize(): pl.pallas_call(kernel, grid_spec=pltpu.PrefetchScalarGridSpec(num_scalar_...  41.3 us
    all_to_all x2, starting transfers between devices, body(): lax.all_to_all(outgoing, 'stn', split_axis=0, concat_axis=0, tiled=True)  12.7 us
    pallas_call x1, Pallas kernels, correlate(): pl.pallas_call(functools.partial(correlator, unit, len(ours)), grid_spec=...  9.11 us
    all_to_all x2, waiting for transfers between devices, body(): lax.all_to_all(outgoing, 'stn', split_axis=0, concat_axis=0, tiled=True)  7.8 us
    unnamed x16, local copies, waits for them, and re-layouts  4.25 us
    ppermute x2, waiting for transfers between devices, body(): others.append(lax.ppermute(own, 'blk', [(0, 1), (1, 0)]))  4.14 us
    ppermute x2, starting transfers between devices, body(): others.append(lax.ppermute(own, 'blk', [(0, 1), (1, 0)]))  3.12 us
    pallas_call x1, Pallas kernels, settle(): pl.pallas_call(functools.partial(settler, unit), in_specs=[pl.BlockSpec(m...  2.25 us
  transfers between devices with their start and end apart: 4, of which 3 were waited for; matrix products, arithmetic and copies ran while one was open for 1% of the time, Pallas kernels for 17%

profile of v9, /device:TPU:0, one launch (start us, length us, event | category | flops | bytes accessed | tf_op | source)
XLA Modules:
  0.0 85.4 jit_solution(4355009866336794644)
XLA Ops:
  0.0 0.0 copy-start
  0.0 1.6 %copy-done = bf16[4096,256]{1,0:T(8,128)(2,1)S(1)} copy-done((bf16[4096,256]{1,0:T(8,128)(2,1)S(1)}, bf16[4096,256]{1,0:T(8,128)(2,1)}, u32[]{:S(2)}) %copy-start) | copy-done | bytes 2097176
  1.6 0.0 copy-start.2
  1.6 1.2 %copy-done.2 = bf16[1024,512]{1,0:T(8,128)(2,1)S(1)} copy-done((bf16[1024,512]{1,0:T(8,128)(2,1)S(1)}, bf16[1024,512]{1,0:T(8,128)(2,1)}, u32[]{:S(2)}) %copy-start.2) | copy-done | bytes 1048600
  2.8 0.0 copy-start.5
  2.8 0.7 copy-done.5
  3.5 0.0 copy-start.1
  3.5 0.0 copy-start.3
  3.5 0.0 copy-start.6
  3.5 28.7 %shard_map.55 = bf16[16,112,128]{2,1,0:T(8,128)(2,1)S(1)} custom-call(s32[16]{0:T(128)S(1)} %copy-done.5, bf16[64,1,63,2,4096]{4,3,2,1,0:T(2,128)(2,1)} %v_ref.3, bf16[4096,256]{1,0:T(8,128)(2,1)S(1)} %copy-done, bf16[1024,512]{1,0:T(8,128)(2,1)S(1)} %copy-done.2), custom_call_target="tpu_custom_call" | custom-call | flops 12683575296 | bytes 49545216 | tf_op jit(solution)/shard_map/pallas_call | solution.py:244
  32.2 0.0 copy-start.4
  32.2 0.8 copy-done.4
  32.9 7.4 %all-to-all-start = ((bf16[16,112,128]{2,1,0:T(8,128)(2,1)}), bf16[16,112,128]{2,1,0:T(8,128)(2,1)}, u32[]{:S(2)}, u32[]{:S(2)}) async-start(bf16[16,112,128]{2,1,0:T(8,128)(2,1)} %copy-done.4), calls=%async_computation | async-start | bytes 917504 | tf_op jit(solution)/shard_map/all_to_all | solution.py:452
  40.4 0.0 copy-done.1
  40.4 0.0 copy-done.3
  40.4 0.0 copy-done.6
  40.4 0.0 copy-start.7
  40.4 12.6 %shard_map.56 = bf16[16,48,128]{2,1,0:T(8,128)(2,1)} custom-call(s32[16]{0:T(128)S(1)} %copy-done.6, bf16[64,1,63,2,4096]{4,3,2,1,0:T(2,128)(2,1)} %v_ref.3, bf16[4096,256]{1,0:T(8,128)(2,1)S(1)} %copy-done.1, bf16[1024,512]{1,0:T(8,128)(2,1)S(1)} %copy-done.3), custom_call_target="tpu_custom_call" | custom-call | flops 4227858432 | bytes 16515072 | tf_op jit(solution)/shard_map/pallas_call | solution.py:244
  53.0 0.7 all-to-all-done.part_hbm
  53.7 5.3 %all-to-all-start.1 = ((bf16[16,48,128]{2,1,0:T(8,128)(2,1)}), bf16[16,48,128]{2,1,0:T(8,128)(2,1)S(1)}, u32[]{:S(2)}, u32[]{:S(2)}) async-start(bf16[16,48,128]{2,1,0:T(8,128)(2,1)} %shard_map.56), calls=%async_computation.1 | async-start | bytes 393216 | tf_op jit(solution)/shard_map/all_to_all | solution.py:452
  59.0 1.6 %collective-permute-start = (bf16[16,112,128]{2,1,0:T(8,128)(2,1)}, bf16[16,112,128]{2,1,0:T(8,128)(2,1)S(1)}, u32[]{:S(2)}, u32[]{:S(2)}) collective-permute-start(bf16[16,112,128]{2,1,0:T(8,128)(2,1)} %all-to-all-done.part_hbm), channel_id=1, source_target_pairs={{0,1},{1,0},{2,3},{3,2},{4,5},{5,4},{6,7},{7,6},{8,9},{9,8},{10,11... | collective-permute-start | bytes 1376264 | tf_op jit(solution)/shard_map/ppermute | solution.py:453
  60.6 0.0 copy-done.7
  60.6 0.1 add.26
  60.7 0.1 add.22
  60.8 0.1 copy.6
  60.9 7.1 %all-to-all-done.1.refs_2_ = bf16[16,48,128]{2,1,0:T(8,128)(2,1)S(1)} async-done(((bf16[16,48,128]{2,1,0:T(8,128)(2,1)}), bf16[16,48,128]{2,1,0:T(8,128)(2,1)S(1)}, u32[]{:S(2)}, u32[]{:S(2)}) %all-to-all-start.1) | async-done | bytes 196640 | tf_op jit(solution)/shard_map/all_to_all | solution.py:452
  68.0 1.5 %collective-permute-start.1 = (bf16[16,48,128]{2,1,0:T(8,128)(2,1)S(1)}, bf16[16,48,128]{2,1,0:T(8,128)(2,1)S(1)}, u32[]{:S(2)}, u32[]{:S(2)}) collective-permute-start(bf16[16,48,128]{2,1,0:T(8,128)(2,1)S(1)} %all-to-all-done.1.refs_2_), channel_id=1, source_target_pairs={{0,1},{1,0},{2,3},{3,2},{4,5},{5,4},{6,7},{7,6},{8,9},{9,8},{10,11... | collective-permute-start | bytes 589832 | tf_op jit(solution)/shard_map/ppermute | solution.py:453
  69.5 0.1 add_bitcast_fusion
  69.6 0.1 copy.7
  69.7 0.1 reshape.9.dest_ref
  69.8 0.1 pad_add_fusion.where
  69.8 2.3 %shard_map.57.refs_3_ = bf16[288,1024]{1,0:T(8,128)(2,1)S(1)} custom-call(s32[1,768]{1,0:T(1,128)S(1)} %slice.4.dest_ref, bf16[16,112,128]{2,1,0:T(8,128)(2,1)} %all-to-all-done.part_hbm), custom_call_target="tpu_custom_call" | custom-call | flops 452984832 | bytes 1048576 | tf_op jit(solution)/shard_map/pallas_call | solution.py:331
  72.1 4.1 %collective-permute-done.1.refs_1_ = bf16[16,48,128]{2,1,0:T(8,128)(2,1)S(1)} collective-permute-done((bf16[16,48,128]{2,1,0:T(8,128)(2,1)S(1)}, bf16[16,48,128]{2,1,0:T(8,128)(2,1)S(1)}, u32[]{:S(2)}, u32[]{:S(2)}) %collective-permute-start.1) | collective-permute-done | bytes 196640 | tf_op jit(solution)/shard_map/ppermute | solution.py:453
  76.3 0.0 collective-permute-done.refs_0_
  76.3 9.1 %shard_map.58 = bf16[1,3,2,512,1024]{4,3,2,1,0:T(8,128)(2,1)} custom-call(s32[16]{0:T(128)S(1)} %copy-done.6, s32[2]{0:T(128)S(1)} %pad_add_fusion.where, s32[1,1024]{1,0:T(1,128)S(1)} %reshape.9.dest_ref, bf16[16,112,128]{2,1,0:T(8,128)(2,1)S(1)} %collective-permute-done.refs_0_, bf16[16,48,128]{2,1,0:T(8,128)(2,1)S(1)} %collective-permute-done.1.refs_1_, ...), custom_call_target="tpu_custom_call" | custom-call | tf_op jit(solution)/shard_map/pallas_call | solution.py:416
  (4 shorter events, 0.0 us)
Async XLA Ops:
  0.0 1.6 %copy-start = (bf16[4096,256]{1,0:T(8,128)(2,1)S(1)}, bf16[4096,256]{1,0:T(8,128)(2,1)}, u32[]{:S(2)}) copy-start(bf16[4096,256]{1,0:T(8,128)(2,1)} %constant.14.clone.u_hbm) | copy-start | bytes 6291460
  1.6 1.2 %copy-start.2 = (bf16[1024,512]{1,0:T(8,128)(2,1)S(1)}, bf16[1024,512]{1,0:T(8,128)(2,1)}, u32[]{:S(2)}) copy-start(bf16[1024,512]{1,0:T(8,128)(2,1)} %constant.15.clone.w_hbm) | copy-start | bytes 3145732
  2.8 0.7 copy-start.5
  3.5 36.9 %copy-start.1 = (bf16[4096,256]{1,0:T(8,128)(2,1)S(1)}, bf16[4096,256]{1,0:T(8,128)(2,1)}, u32[]{:S(2)}) copy-start(bf16[4096,256]{1,0:T(8,128)(2,1)} %constant.14.clone.u_hbm) | copy-start | bytes 6291460
  3.5 36.9 %copy-start.3 = (bf16[1024,512]{1,0:T(8,128)(2,1)S(1)}, bf16[1024,512]{1,0:T(8,128)(2,1)}, u32[]{:S(2)}) copy-start(bf16[1024,512]{1,0:T(8,128)(2,1)} %constant.15.clone.w_hbm) | copy-start | bytes 3145732
  3.5 36.9 %copy-start.6 = (s32[16]{0:T(128)S(1)}, s32[16]{0:T(128)}, u32[]{:S(2)}) copy-start(s32[16]{0:T(128)} %counts.3) | copy-start | bytes 196
  32.2 0.8 copy-start.4
  32.9 20.7 %all-to-all-start = ((bf16[16,112,128]{2,1,0:T(8,128)(2,1)}), bf16[16,112,128]{2,1,0:T(8,128)(2,1)}, u32[]{:S(2)}, u32[]{:S(2)}) async-start(bf16[16,112,128]{2,1,0:T(8,128)(2,1)} %copy-done.4), calls=%async_computation | async-start | bytes 917504 | tf_op jit(solution)/shard_map/all_to_all | solution.py:452
  40.4 20.2 %copy-start.7 = (s32[512]{0:T(512)S(1)}, s32[512]{0:T(512)}, u32[]{:S(2)}) copy-start(s32[512]{0:T(512)} %param.6) | copy-start | bytes 6148
  53.7 14.3 %all-to-all-start.1 = ((bf16[16,48,128]{2,1,0:T(8,128)(2,1)}), bf16[16,48,128]{2,1,0:T(8,128)(2,1)S(1)}, u32[]{:S(2)}, u32[]{:S(2)}) async-start(bf16[16,48,128]{2,1,0:T(8,128)(2,1)} %shard_map.56), calls=%async_computation.1 | async-start | bytes 393216 | tf_op jit(solution)/shard_map/all_to_all | solution.py:452
  59.0 17.3 %collective-permute-start = (bf16[16,112,128]{2,1,0:T(8,128)(2,1)}, bf16[16,112,128]{2,1,0:T(8,128)(2,1)S(1)}, u32[]{:S(2)}, u32[]{:S(2)}) collective-permute-start(bf16[16,112,128]{2,1,0:T(8,128)(2,1)} %all-to-all-done.part_hbm), channel_id=1, source_target_pairs={{0,1},{1,0},{2,3},{3,2},{4,5},{5,4},{6,7},{7,6},{8,9},{9,8},{10,11... | collective-permute-start | bytes 1376264 | tf_op jit(solution)/shard_map/ppermute | solution.py:453
  68.0 8.3 %collective-permute-start.1 = (bf16[16,48,128]{2,1,0:T(8,128)(2,1)S(1)}, bf16[16,48,128]{2,1,0:T(8,128)(2,1)S(1)}, u32[]{:S(2)}, u32[]{:S(2)}) collective-permute-start(bf16[16,48,128]{2,1,0:T(8,128)(2,1)S(1)} %all-to-all-done.1.refs_2_), channel_id=1, source_target_pairs={{0,1},{1,0},{2,3},{3,2},{4,5},{5,4},{6,7},{7,6},{8,9},{9,8},{10,11... | collective-permute-start | bytes 589832 | tf_op jit(solution)/shard_map/ppermute | solution.py:453

commit v10 on v9

--- a/solution.py
+++ b/solution.py
@@ -182,10 +182,10 @@
         for copy in tables_in:
             copy.start()
         turned[...] = jnp.zeros(turned.shape, jnp.float32)
-        for block in range(1, min(ahead - 1, streams // step)):
-            begin(block)
-
-    @pl.when(i + ahead - 1 < last)
+        if streams // step > 1:
+            begin(1)
+
+    @pl.when((i > 0) & (i + ahead - 1 < last))
     def _():
         begin(i + ahead - 1)
 
@@ -198,6 +198,14 @@
     def _():
         for copy in fetch(i):
             copy.wait()
+
+    @pl.when(i == 0)
+    def _():
+        for block in range(2, min(ahead, streams // step)):
+            begin(block)
+
+    @pl.when(i < last)
+    def _():
         mix(jnp.maximum(i - 1, 0))
         analyse()
 
@@ -231,7 +239,7 @@
         out_ref[...] = turned[...].astype(jnp.bfloat16)
 
 
-def channelize(voltages, chan_counts, dests, start, streams, step, unit):
+def channelize(voltages, chan_counts, dests, start, streams, step, unit, room):
     band = 2 * dests
     frames = voltages.shape[2]
     analysis, mixing = tables(band)
@@ -261,7 +269,7 @@
         ),
         out_shape=jax.ShapeDtypeStruct((dests, payload, LANES), jnp.bfloat16),
         compiler_params=pltpu.CompilerParams(
-            vmem_limit_bytes=(32 if band <= 64 else 60) * 1024 * 1024
+            vmem_limit_bytes=room * 1024 * 1024
         ),
         cost_estimate=pl.CostEstimate(
             flops=2 * streams * 2 * frames * analysis.size,
@@ -435,27 +443,48 @@
     )(chan_counts, where, dest, *operands)
 
 
+def two_stages(outgoing, inner):
+    dests = outgoing.shape[0]
+    outer = dests // inner
+    far = [[o * inner + i for o in range(outer)] for i in range(inner)]
+    near = [[o * inner + i for i in range(inner)] for o in range(outer)]
+    half = lax.all_to_all(
+        outgoing, "stn", split_axis=0, concat_axis=0, axis_index_groups=far, tiled=True
+    )
+    half = half.reshape((outer, inner) + outgoing.shape[1:]).swapaxes(0, 1).reshape(outgoing.shape)
+    return lax.all_to_all(
+        half, "stn", split_axis=0, concat_axis=0, axis_index_groups=near, tiled=True
+    )
+
+
 def body(voltages, station_map, chan_counts):
     dests = lax.axis_size("stn")
     streams = voltages.shape[0]
     total = dests * streams
     unit = min(streams, 16)
-    plan = (48, 16) if streams == 64 else (streams,)
+    inner = 4
+    plan = ((48, 4, 60), (16, 2, 32)) if streams == 64 else ((streams, 2, 60),)
     dest = (2 * station_map[:, None] + jnp.arange(2, dtype=jnp.int32)[None, :]).reshape(-1)
-    dest = dest.reshape(dests, streams // unit, unit).transpose(1, 0, 2).reshape(1, -1)
+    dest = dest.reshape(dests, streams // unit, unit).transpose(1, 0, 2)
     where = jnp.stack([lax.axis_index("stn"), lax.axis_index("blk")]).astype(jnp.int32)
-    others, settled = [], []
+    others, settled, spots = [], [], []
     start = 0
-    for size in plan:
-        outgoing = channelize(voltages, chan_counts, dests, start, size, 2, unit)
+    for size, step, room in plan:
+        outgoing = channelize(voltages, chan_counts, dests, start, size, step, unit, room)
         chan_counts, outgoing = lax.optimization_barrier((chan_counts, outgoing))
-        own = lax.all_to_all(outgoing, "stn", split_axis=0, concat_axis=0, tiled=True)
+        spot = dest[start // unit : (start + size) // unit]
+        if start + size < streams:
+            own = lax.all_to_all(outgoing, "stn", split_axis=0, concat_axis=0, tiled=True)
+            spots.append(spot.reshape(1, -1))
+            settled.append(settle(own, spots[-1], total, unit))
+        else:
+            own = two_stages(outgoing, inner)
+            spot = spot.reshape(-1, dests // inner, inner, unit).swapaxes(1, 2)
+            spots.append(spot.reshape(1, -1))
         others.append(lax.ppermute(own, "blk", [(0, 1), (1, 0)]))
-        if start + size < streams:
-            spots = dest[:, start * dests : (start + size) * dests]
-            settled.append(settle(own, spots, total, unit))
         start = start + size
-    return correlate(others, [own] + settled, dest, chan_counts, where, unit)
+    spots = jnp.concatenate(spots, axis=1)
+    return correlate(others, [own] + settled, spots, chan_counts, where, unit)
 
 
 def solution(mesh):

time: 85.8 us -> 99.3 us (1.16)
  blocking collectives: 0 us -> 13.6 us
  waiting for transfers between devices: 11.9 us -> 23.9 us
  starting transfers between devices: 15.8 us -> 10.2 us
  local copies, waits for them, and re-layouts: 4.69 us -> 1.31 us
  Pallas kernels: 52.6 us -> 49.7 us
    all_to_all x0 -> x1, blocking collectives: none -> 13.6 us  [two_stages(): lax.all_to_all(outgoing, 'stn', split_axis=0, concat_axis=0, axis_index_g...]
    all_to_all x2 -> x1, starting transfers between devices: 12.7 us -> 3.76 us  [body(): lax.all_to_all(outgoing, 'stn', split_axis=0, concat_axis=0, tiled=True)]
    all_to_all x2 -> x1, waiting for transfers between devices: 7.8 us -> 12.3 us  [body(): lax.all_to_all(outgoing, 'stn', split_axis=0, concat_axis=0, tiled=True)]
    unnamed x16 -> x8, local copies, waits for them, and re-layouts: 4.25 us -> 0.02 us
    ppermute x2, waiting for transfers between devices: 4.14 us -> 7.98 us  [body(): others.append(lax.ppermute(own, 'blk', [(0, 1), (1, 0)]))]
    all_to_all x0 -> x1, waiting for transfers between devices: none -> 3.64 us  [two_stages(): lax.all_to_all(half, 'stn', split_axis=0, concat_axis=0, axis_index_group...]
    all_to_all x0 -> x1, starting transfers between devices: none -> 3.36 us  [two_stages(): lax.all_to_all(half, 'stn', split_axis=0, concat_axis=0, axis_index_group...]
    pallas_call x2, Pallas kernels: 41.3 us -> 38.7 us  [channelize(): pl.pallas_call(kernel, grid_spec=pltpu.PrefetchScalarGridSpec(num_scalar_...]
  transfers between devices with their start and end apart: 4 -> 4, of which waited for: 3 -> 3; matrix products, arithmetic and copies ran while one was open for 1% -> 1% of each run, Pallas kernels for 17% -> 2%
where the time goes in v10:
time: 99.3 us; the launch traced here: 99 us
  Pallas kernels  49.7 us (50%)
  waiting for transfers between devices  23.9 us (24%)
  blocking collectives  13.6 us (14%)
  starting transfers between devices  10.2 us (10%)
  local copies, waits for them, and re-layouts  1.31 us (1%)
    pallas_call x2, Pallas kernels, channelize(): pl.pallas_call(kernel, grid_spec=pltpu.PrefetchScalarGridSpec(num_scalar_...  38.7 us
    all_to_all x1, blocking collectives, two_stages(): lax.all_to_all(outgoing, 'stn', split_axis=0, concat_axis=0, axis_index_g...  13.6 us
    all_to_all x1, waiting for transfers between devices, body(): lax.all_to_all(outgoing, 'stn', split_axis=0, concat_axis=0, tiled=True)  12.3 us
    pallas_call x1, Pallas kernels, correlate(): pl.pallas_call(functools.partial(correlator, unit, len(ours)), grid_spec=...  9.11 us
    ppermute x2, waiting for transfers between devices, body(): others.append(lax.ppermute(own, 'blk', [(0, 1), (1, 0)]))  7.98 us
    all_to_all x1, starting transfers between devices, body(): lax.all_to_all(outgoing, 'stn', split_axis=0, concat_axis=0, tiled=True)  3.76 us
    all_to_all x1, waiting for transfers between devices, two_stages(): lax.all_to_all(half, 'stn', split_axis=0, concat_axis=0, axis_index_group...  3.64 us
    all_to_all x1, starting transfers between devices, two_stages(): lax.all_to_all(half, 'stn', split_axis=0, concat_axis=0, axis_index_group...  3.36 us
  transfers between devices with their start and end apart: 4, of which 3 were waited for; matrix products, arithmetic and copies ran while one was open for 1% of the time, Pallas kernels for 2%

profile of v10, /device:TPU:0, one launch (start us, length us, event | category | flops | bytes accessed | tf_op | source)
XLA Modules:
  0.0 99.0 jit_solution(550605615936529561)
XLA Ops:
  0.0 0.0 copy-start
  0.0 0.0 copy-start.1
  0.0 0.0 copy-start.2
  0.0 27.4 %shard_map.55 = bf16[16,112,128]{2,1,0:T(8,128)(2,1)} custom-call(s32[16]{0:T(128)} %counts.3, bf16[64,1,63,2,4096]{4,3,2,1,0:T(2,128)(2,1)} %v_ref.3, bf16[4096,256]{1,0:T(8,128)(2,1)} %constant.14.clone.u_hbm, bf16[1024,512]{1,0:T(8,128)(2,1)} %constant.15.clone.w_hbm), custom_call_target="tpu_custom_call" | custom-call | flops 12683575296 | bytes 49545216 | tf_op jit(solution)/shard_map/pallas_call | solution.py:252
  27.4 0.0 copy-done
  27.4 0.0 copy-done.1
  27.4 0.0 copy-done.2
  27.4 0.0 copy-start.3
  27.4 11.3 %shard_map.56 = bf16[16,48,128]{2,1,0:T(8,128)(2,1)S(1)} custom-call(s32[16]{0:T(128)S(1)} %copy-done.2, bf16[64,1,63,2,4096]{4,3,2,1,0:T(2,128)(2,1)} %v_ref.3, bf16[4096,256]{1,0:T(8,128)(2,1)S(1)} %copy-done, bf16[1024,512]{1,0:T(8,128)(2,1)S(1)} %copy-done.1), custom_call_target="tpu_custom_call" | custom-call | flops 4227858432 | bytes 16515072 | tf_op jit(solution)/shard_map/pallas_call | solution.py:252
  38.8 13.6 %all_to_all.15 = bf16[16,48,128]{2,1,0:T(8,128)(2,1)S(1)} all-to-all(bf16[16,48,128]{2,1,0:T(8,128)(2,1)S(1)} %shard_map.56), channel_id=1, replica_groups={{0,8,16,24},{2,10,18,26},{4,12,20,28},{6,14,22,30},{1,9,17,25},{3,11,19..., dimensions={0} | all-to-all | bytes 393216 | tf_op jit(solution)/shard_map/all_to_all | solution.py:451
  52.4 3.8 %all-to-all-start = ((bf16[16,112,128]{2,1,0:T(8,128)(2,1)}), bf16[16,112,128]{2,1,0:T(8,128)(2,1)S(1)}, u32[]{:S(2)}, u32[]{:S(2)}) async-start(bf16[16,112,128]{2,1,0:T(8,128)(2,1)} %shard_map.55), calls=%async_computation | async-start | bytes 917504 | tf_op jit(solution)/shard_map/all_to_all | solution.py:477
  56.1 0.1 add.26
  56.2 0.0 copy-done.3
  56.2 0.1 add.22
  56.3 0.1 copy.7
  56.4 0.7 copy.11
  57.1 12.3 %all-to-all-done.part_hbm = bf16[16,112,128]{2,1,0:T(8,128)(2,1)S(1)} async-done(((bf16[16,112,128]{2,1,0:T(8,128)(2,1)}), bf16[16,112,128]{2,1,0:T(8,128)(2,1)S(1)}, u32[]{:S(2)}, u32[]{:S(2)}) %all-to-all-start) | async-done | bytes 458784 | tf_op jit(solution)/shard_map/all_to_all | solution.py:477
  69.4 3.4 %all-to-all-start.2 = ((bf16[16,48,128]{2,1,0:T(8,128)(2,1)}), bf16[16,48,128]{2,1,0:T(8,128)(2,1)S(1)}, u32[]{:S(2)}, u32[]{:S(2)}) async-start(bf16[16,48,128]{2,1,0:T(8,128)(2,1)} %bitcast.8), calls=%async_computation.2 | async-start | bytes 393216 | tf_op jit(solution)/shard_map/all_to_all | solution.py:455
  72.8 1.6 %collective-permute-start = (bf16[16,112,128]{2,1,0:T(8,128)(2,1)S(1)}, bf16[16,112,128]{2,1,0:T(8,128)(2,1)S(1)}, u32[]{:S(2)}, u32[]{:S(2)}) collective-permute-start(bf16[16,112,128]{2,1,0:T(8,128)(2,1)S(1)} %all-to-all-done.part_hbm), channel_id=1, source_target_pairs={{0,1},{1,0},{2,3},{3,2},{4,5},{5,4},{6,7},{7,6},{8,9},{9,8},{10,11... | collective-permute-start | bytes 1376264 | tf_op jit(solution)/shard_map/ppermute | solution.py:484
  74.3 0.1 add_bitcast_fusion
  74.4 3.6 %all-to-all-done.2.refs_2_ = bf16[16,48,128]{2,1,0:T(8,128)(2,1)S(1)} async-done(((bf16[16,48,128]{2,1,0:T(8,128)(2,1)}), bf16[16,48,128]{2,1,0:T(8,128)(2,1)S(1)}, u32[]{:S(2)}, u32[]{:S(2)}) %all-to-all-start.2) | async-done | bytes 196640 | tf_op jit(solution)/shard_map/all_to_all | solution.py:455
  78.1 1.5 %collective-permute-start.1 = (bf16[16,48,128]{2,1,0:T(8,128)(2,1)S(1)}, bf16[16,48,128]{2,1,0:T(8,128)(2,1)S(1)}, u32[]{:S(2)}, u32[]{:S(2)}) collective-permute-start(bf16[16,48,128]{2,1,0:T(8,128)(2,1)S(1)} %all-to-all-done.2.refs_2_), channel_id=1, source_target_pairs={{0,1},{1,0},{2,3},{3,2},{4,5},{5,4},{6,7},{7,6},{8,9},{9,8},{10,11... | collective-permute-start | bytes 589832 | tf_op jit(solution)/shard_map/ppermute | solution.py:484
  79.6 0.1 pad_add_fusion.1.where
  79.6 0.1 copy.8
  79.7 0.1 reshape.21.dest_ref
  79.8 0.1 copy.9
  79.9 0.1 reshape.23
  80.0 1.9 %shard_map.57.refs_3_ = bf16[288,1024]{1,0:T(8,128)(2,1)S(1)} custom-call(s32[1,768]{1,0:T(1,128)S(1)} %reshape.21.dest_ref, bf16[16,112,128]{2,1,0:T(8,128)(2,1)S(1)} %all-to-all-done.part_hbm), custom_call_target="tpu_custom_call" | custom-call | flops 452984832 | bytes 1048576 | tf_op jit(solution)/shard_map/pallas_call | solution.py:339
  81.9 8.0 %collective-permute-done.1.refs_1_ = bf16[16,48,128]{2,1,0:T(8,128)(2,1)S(1)} collective-permute-done((bf16[16,48,128]{2,1,0:T(8,128)(2,1)S(1)}, bf16[16,48,128]{2,1,0:T(8,128)(2,1)S(1)}, u32[]{:S(2)}, u32[]{:S(2)}) %collective-permute-start.1) | collective-permute-done | bytes 196640 | tf_op jit(solution)/shard_map/ppermute | solution.py:484
  89.9 0.0 collective-permute-done.refs_0_
  89.9 9.1 %shard_map.58 = bf16[1,3,2,512,1024]{4,3,2,1,0:T(8,128)(2,1)} custom-call(s32[16]{0:T(128)S(1)} %copy-done.2, s32[2]{0:T(128)S(1)} %pad_add_fusion.1.where, s32[1,1024]{1,0:T(1,128)S(1)} %pad_add_fusion.dest_ref, bf16[16,112,128]{2,1,0:T(8,128)(2,1)S(1)} %collective-permute-done.refs_0_, bf16[16,48,128]{2,1,0:T(8,128)(2,1)S(1)} %collective-permute-done.1.refs_1_, ...), custom_call_target="tpu_custom_call" | custom-call | tf_op jit(solution)/shard_map/pallas_call | solution.py:424
  (7 shorter events, 0.0 us)
Async XLA Ops:
  0.0 27.4 %copy-start = (bf16[4096,256]{1,0:T(8,128)(2,1)S(1)}, bf16[4096,256]{1,0:T(8,128)(2,1)}, u32[]{:S(2)}) copy-start(bf16[4096,256]{1,0:T(8,128)(2,1)} %constant.14.clone.u_hbm) | copy-start | bytes 6291460
  0.0 27.4 %copy-start.1 = (bf16[1024,512]{1,0:T(8,128)(2,1)S(1)}, bf16[1024,512]{1,0:T(8,128)(2,1)}, u32[]{:S(2)}) copy-start(bf16[1024,512]{1,0:T(8,128)(2,1)} %constant.15.clone.w_hbm) | copy-start | bytes 3145732
  0.0 27.4 %copy-start.2 = (s32[16]{0:T(128)S(1)}, s32[16]{0:T(128)}, u32[]{:S(2)}) copy-start(s32[16]{0:T(128)} %counts.3) | copy-start | bytes 196
  27.4 28.8 %copy-start.3 = (s32[512]{0:T(512)S(1)}, s32[512]{0:T(512)}, u32[]{:S(2)}) copy-start(s32[512]{0:T(512)} %param.6) | copy-start | bytes 6148
  52.4 17.0 %all-to-all-start = ((bf16[16,112,128]{2,1,0:T(8,128)(2,1)}), bf16[16,112,128]{2,1,0:T(8,128)(2,1)S(1)}, u32[]{:S(2)}, u32[]{:S(2)}) async-start(bf16[16,112,128]{2,1,0:T(8,128)(2,1)} %shard_map.55), calls=%async_computation | async-start | bytes 917504 | tf_op jit(solution)/shard_map/all_to_all | solution.py:477
  69.4 8.7 %all-to-all-start.2 = ((bf16[16,48,128]{2,1,0:T(8,128)(2,1)}), bf16[16,48,128]{2,1,0:T(8,128)(2,1)S(1)}, u32[]{:S(2)}, u32[]{:S(2)}) async-start(bf16[16,48,128]{2,1,0:T(8,128)(2,1)} %bitcast.8), calls=%async_computation.2 | async-start | bytes 393216 | tf_op jit(solution)/shard_map/all_to_all | solution.py:455
  72.8 17.1 %collective-permute-start = (bf16[16,112,128]{2,1,0:T(8,128)(2,1)S(1)}, bf16[16,112,128]{2,1,0:T(8,128)(2,1)S(1)}, u32[]{:S(2)}, u32[]{:S(2)}) collective-permute-start(bf16[16,112,128]{2,1,0:T(8,128)(2,1)S(1)} %all-to-all-done.part_hbm), channel_id=1, source_target_pairs={{0,1},{1,0},{2,3},{3,2},{4,5},{5,4},{6,7},{7,6},{8,9},{9,8},{10,11... | collective-permute-start | bytes 1376264 | tf_op jit(solution)/shard_map/ppermute | solution.py:484
  78.1 11.8 %collective-permute-start.1 = (bf16[16,48,128]{2,1,0:T(8,128)(2,1)S(1)}, bf16[16,48,128]{2,1,0:T(8,128)(2,1)S(1)}, u32[]{:S(2)}, u32[]{:S(2)}) collective-permute-start(bf16[16,48,128]{2,1,0:T(8,128)(2,1)S(1)} %all-to-all-done.2.refs_2_), channel_id=1, source_target_pairs={{0,1},{1,0},{2,3},{3,2},{4,5},{5,4},{6,7},{7,6},{8,9},{9,8},{10,11... | collective-permute-start | bytes 589832 | tf_op jit(solution)/shard_map/ppermute | solution.py:484

commit v11 on v10

--- a/solution.py
+++ b/solution.py
@@ -46,7 +46,7 @@
 
 
 def shifts_of(band):
-    return 8 if band <= 64 else 4
+    return 4
 
 
 def turn_lanes(value, shift):
@@ -121,8 +121,8 @@
         ]
 
     def begin(block):
-        for r, copy in enumerate(fetch(block)):
-            copy.start(priority=r % 2)
+        for copy in fetch(block):
+            copy.start()
 
     def analyse():
         signal = held[i % ahead].reshape(step * rows, FFT_LEN)
@@ -443,48 +443,27 @@
     )(chan_counts, where, dest, *operands)
 
 
-def two_stages(outgoing, inner):
-    dests = outgoing.shape[0]
-    outer = dests // inner
-    far = [[o * inner + i for o in range(outer)] for i in range(inner)]
-    near = [[o * inner + i for i in range(inner)] for o in range(outer)]
-    half = lax.all_to_all(
-        outgoing, "stn", split_axis=0, concat_axis=0, axis_index_groups=far, tiled=True
-    )
-    half = half.reshape((outer, inner) + outgoing.shape[1:]).swapaxes(0, 1).reshape(outgoing.shape)
-    return lax.all_to_all(
-        half, "stn", split_axis=0, concat_axis=0, axis_index_groups=near, tiled=True
-    )
-
-
 def body(voltages, station_map, chan_counts):
     dests = lax.axis_size("stn")
     streams = voltages.shape[0]
     total = dests * streams
     unit = min(streams, 16)
-    inner = 4
     plan = ((48, 4, 60), (16, 2, 32)) if streams == 64 else ((streams, 2, 60),)
     dest = (2 * station_map[:, None] + jnp.arange(2, dtype=jnp.int32)[None, :]).reshape(-1)
     dest = dest.reshape(dests, streams // unit, unit).transpose(1, 0, 2)
     where = jnp.stack([lax.axis_index("stn"), lax.axis_index("blk")]).astype(jnp.int32)
-    others, settled, spots = [], [], []
+    others, settled = [], []
     start = 0
     for size, step, room in plan:
         outgoing = channelize(voltages, chan_counts, dests, start, size, step, unit, room)
         chan_counts, outgoing = lax.optimization_barrier((chan_counts, outgoing))
+        own = lax.all_to_all(outgoing, "stn", split_axis=0, concat_axis=0, tiled=True)
         spot = dest[start // unit : (start + size) // unit]
         if start + size < streams:
-            own = lax.all_to_all(outgoing, "stn", split_axis=0, concat_axis=0, tiled=True)
-            spots.append(spot.reshape(1, -1))
-            settled.append(settle(own, spots[-1], total, unit))
-        else:
-            own = two_stages(outgoing, inner)
-            spot = spot.reshape(-1, dests // inner, inner, unit).swapaxes(1, 2)
-            spots.append(spot.reshape(1, -1))
+            settled.append(settle(own, spot.reshape(1, -1), total, unit))
         others.append(lax.ppermute(own, "blk", [(0, 1), (1, 0)]))
         start = start + size
-    spots = jnp.concatenate(spots, axis=1)
-    return correlate(others, [own] + settled, spots, chan_counts, where, unit)
+    return correlate(others, [own] + settled, dest.reshape(1, -1), chan_counts, where, unit)
 
 
 def solution(mesh):

time: 99.3 us -> 80.9 us (0.81)
  blocking collectives: 13.6 us -> 0 us
  waiting for transfers between devices: 23.9 us -> 12.4 us
  starting transfers between devices: 10.2 us -> 15.2 us
  Pallas kernels: 49.7 us -> 52.1 us
    all_to_all x1 -> x0, blocking collectives: 13.6 us -> none  [two_stages(): lax.all_to_all(outgoing, 'stn', split_axis=0, concat_axis=0, axis_index_g...]
    all_to_all x1 -> x2, starting transfers between devices: 3.76 us -> 12 us  [body(): lax.all_to_all(outgoing, 'stn', split_axis=0, concat_axis=0, tiled=True)]
    ppermute x2, waiting for transfers between devices: 7.98 us -> 3.92 us  [body(): others.append(lax.ppermute(own, 'blk', [(0, 1), (1, 0)]))]
    all_to_all x1 -> x2, waiting for transfers between devices: 12.3 us -> 8.47 us  [body(): lax.all_to_all(outgoing, 'stn', split_axis=0, concat_axis=0, tiled=True)]
    all_to_all x1 -> x0, waiting for transfers between devices: 3.64 us -> none  [two_stages(): lax.all_to_all(half, 'stn', split_axis=0, concat_axis=0, axis_index_group...]
    all_to_all x1 -> x0, starting transfers between devices: 3.36 us -> none  [two_stages(): lax.all_to_all(half, 'stn', split_axis=0, concat_axis=0, axis_index_group...]
    pallas_call x2, Pallas kernels: 38.7 us -> 40.7 us  [channelize(): pl.pallas_call(kernel, grid_spec=pltpu.PrefetchScalarGridSpec(num_scalar_...]
  transfers between devices with their start and end apart: 4 -> 4, of which waited for: 3 -> 3; matrix products, arithmetic and copies ran while one was open for 1% -> 1% of each run, Pallas kernels for 2% -> 18%
where the time goes in v11:
time: 80.9 us; the launch traced here: 80.5 us
  Pallas kernels  52.1 us (64%)
  starting transfers between devices  15.2 us (19%)
  waiting for transfers between devices  12.4 us (15%)
    pallas_call x2, Pallas kernels, channelize(): pl.pallas_call(kernel, grid_spec=pltpu.PrefetchScalarGridSpec(num_scalar_...  40.7 us
    all_to_all x2, starting transfers between devices, body(): lax.all_to_all(outgoing, 'stn', split_axis=0, concat_axis=0, tiled=True)  12 us
    pallas_call x1, Pallas kernels, correlate(): pl.pallas_call(functools.partial(correlator, unit, len(ours)), grid_spec=...  9.11 us
    all_to_all x2, waiting for transfers between devices, body(): lax.all_to_all(outgoing, 'stn', split_axis=0, concat_axis=0, tiled=True)  8.47 us
    ppermute x2, waiting for transfers between devices, body(): others.append(lax.ppermute(own, 'blk', [(0, 1), (1, 0)]))  3.92 us
    ppermute x2, starting transfers between devices, body(): others.append(lax.ppermute(own, 'blk', [(0, 1), (1, 0)]))  3.23 us
    pallas_call x1, Pallas kernels, settle(): pl.pallas_call(functools.partial(settler, unit), in_specs=[pl.BlockSpec(m...  2.26 us
  transfers between devices with their start and end apart: 4, of which 3 were waited for; matrix products, arithmetic and copies ran while one was open for 1% of the time, Pallas kernels for 18%

profile of v11, /device:TPU:0, one launch (start us, length us, event | category | flops | bytes accessed | tf_op | source)
XLA Modules:
  0.0 80.5 jit_solution(7472626594417369777)
XLA Ops:
  0.0 0.0 copy-start
  0.0 0.0 copy-start.1
  0.0 0.0 copy-start.2
  0.0 28.8 %shard_map.55 = bf16[16,112,128]{2,1,0:T(8,128)(2,1)} custom-call(s32[16]{0:T(128)} %counts.3, bf16[64,1,63,2,4096]{4,3,2,1,0:T(2,128)(2,1)} %v_ref.3, bf16[4096,256]{1,0:T(8,128)(2,1)} %constant.14.clone.u_hbm, bf16[2048,256]{1,0:T(8,128)(2,1)} %constant.15.clone.w_hbm), custom_call_target="tpu_custom_call" | custom-call | flops 12683575296 | bytes 49545216 | tf_op jit(solution)/shard_map/pallas_call | solution.py:252
  28.8 7.4 %all-to-all-start = ((bf16[16,112,128]{2,1,0:T(8,128)(2,1)}), bf16[16,112,128]{2,1,0:T(8,128)(2,1)}, u32[]{:S(2)}, u32[]{:S(2)}) async-start(bf16[16,112,128]{2,1,0:T(8,128)(2,1)} %shard_map.55), calls=%async_computation | async-start | bytes 917504 | tf_op jit(solution)/shard_map/all_to_all | solution.py:460
  36.3 0.0 copy-done
  36.3 0.0 copy-done.1
  36.3 0.0 copy-done.2
  36.3 0.0 copy-start.3
  36.3 11.9 %shard_map.56 = bf16[16,48,128]{2,1,0:T(8,128)(2,1)} custom-call(s32[16]{0:T(128)S(1)} %copy-done.2, bf16[64,1,63,2,4096]{4,3,2,1,0:T(2,128)(2,1)} %v_ref.3, bf16[4096,256]{1,0:T(8,128)(2,1)S(1)} %copy-done, bf16[2048,256]{1,0:T(8,128)(2,1)S(1)} %copy-done.1), custom_call_target="tpu_custom_call" | custom-call | flops 4227858432 | bytes 16515072 | tf_op jit(solution)/shard_map/pallas_call | solution.py:252
  48.2 1.4 %all-to-all-done.part_hbm = bf16[16,112,128]{2,1,0:T(8,128)(2,1)} async-done(((bf16[16,112,128]{2,1,0:T(8,128)(2,1)}), bf16[16,112,128]{2,1,0:T(8,128)(2,1)}, u32[]{:S(2)}, u32[]{:S(2)}) %all-to-all-start) | async-done | bytes 458784 | tf_op jit(solution)/shard_map/all_to_all | solution.py:460
  49.6 4.6 %all-to-all-start.1 = ((bf16[16,48,128]{2,1,0:T(8,128)(2,1)}), bf16[16,48,128]{2,1,0:T(8,128)(2,1)S(1)}, u32[]{:S(2)}, u32[]{:S(2)}) async-start(bf16[16,48,128]{2,1,0:T(8,128)(2,1)} %shard_map.56), calls=%async_computation.1 | async-start | bytes 393216 | tf_op jit(solution)/shard_map/all_to_all | solution.py:460
  54.1 1.6 %collective-permute-start = (bf16[16,112,128]{2,1,0:T(8,128)(2,1)}, bf16[16,112,128]{2,1,0:T(8,128)(2,1)S(1)}, u32[]{:S(2)}, u32[]{:S(2)}) collective-permute-start(bf16[16,112,128]{2,1,0:T(8,128)(2,1)} %all-to-all-done.part_hbm), channel_id=1, source_target_pairs={{0,1},{1,0},{2,3},{3,2},{4,5},{5,4},{6,7},{7,6},{8,9},{9,8},{10,11... | collective-permute-start | bytes 1376264 | tf_op jit(solution)/shard_map/ppermute | solution.py:464
  55.8 0.0 copy-done.3
  55.8 0.1 add.26
  55.9 0.1 add.22
  56.0 0.1 copy.6
  56.1 7.1 %all-to-all-done.1.refs_2_ = bf16[16,48,128]{2,1,0:T(8,128)(2,1)S(1)} async-done(((bf16[16,48,128]{2,1,0:T(8,128)(2,1)}), bf16[16,48,128]{2,1,0:T(8,128)(2,1)S(1)}, u32[]{:S(2)}, u32[]{:S(2)}) %all-to-all-start.1) | async-done | bytes 196640 | tf_op jit(solution)/shard_map/all_to_all | solution.py:460
  63.1 1.6 %collective-permute-start.1 = (bf16[16,48,128]{2,1,0:T(8,128)(2,1)S(1)}, bf16[16,48,128]{2,1,0:T(8,128)(2,1)S(1)}, u32[]{:S(2)}, u32[]{:S(2)}) collective-permute-start(bf16[16,48,128]{2,1,0:T(8,128)(2,1)S(1)} %all-to-all-done.1.refs_2_), channel_id=1, source_target_pairs={{0,1},{1,0},{2,3},{3,2},{4,5},{5,4},{6,7},{7,6},{8,9},{9,8},{10,11... | collective-permute-start | bytes 589832 | tf_op jit(solution)/shard_map/ppermute | solution.py:464
  64.7 0.1 add_bitcast_fusion
  64.8 0.1 copy.7
  64.9 0.1 reshape.12.dest_ref
  65.0 0.1 copy.8
  65.1 0.1 reshape.13.dest_ref
  65.1 0.1 pad_add_fusion.where
  65.2 2.3 %shard_map.57.refs_3_ = bf16[288,1024]{1,0:T(8,128)(2,1)S(1)} custom-call(s32[1,768]{1,0:T(1,128)S(1)} %reshape.13.dest_ref, bf16[16,112,128]{2,1,0:T(8,128)(2,1)} %all-to-all-done.part_hbm), custom_call_target="tpu_custom_call" | custom-call | flops 452984832 | bytes 1048576 | tf_op jit(solution)/shard_map/pallas_call | solution.py:339
  67.5 3.9 %collective-permute-done.1.refs_1_ = bf16[16,48,128]{2,1,0:T(8,128)(2,1)S(1)} collective-permute-done((bf16[16,48,128]{2,1,0:T(8,128)(2,1)S(1)}, bf16[16,48,128]{2,1,0:T(8,128)(2,1)S(1)}, u32[]{:S(2)}, u32[]{:S(2)}) %collective-permute-start.1) | collective-permute-done | bytes 196640 | tf_op jit(solution)/shard_map/ppermute | solution.py:464
  71.4 0.0 collective-permute-done.refs_0_
  71.4 9.1 %shard_map.58 = bf16[1,3,2,512,1024]{4,3,2,1,0:T(8,128)(2,1)} custom-call(s32[16]{0:T(128)S(1)} %copy-done.2, s32[2]{0:T(128)S(1)} %pad_add_fusion.where, s32[1,1024]{1,0:T(1,128)S(1)} %reshape.12.dest_ref, bf16[16,112,128]{2,1,0:T(8,128)(2,1)S(1)} %collective-permute-done.refs_0_, bf16[16,48,128]{2,1,0:T(8,128)(2,1)S(1)} %collective-permute-done.1.refs_1_, ...), custom_call_target="tpu_custom_call" | custom-call | tf_op jit(solution)/shard_map/pallas_call | solution.py:424
  (4 shorter events, 0.0 us)
Async XLA Ops:
  0.0 36.3 %copy-start = (bf16[4096,256]{1,0:T(8,128)(2,1)S(1)}, bf16[4096,256]{1,0:T(8,128)(2,1)}, u32[]{:S(2)}) copy-start(bf16[4096,256]{1,0:T(8,128)(2,1)} %constant.14.clone.u_hbm) | copy-start | bytes 6291460
  0.0 36.3 %copy-start.1 = (bf16[2048,256]{1,0:T(8,128)(2,1)S(1)}, bf16[2048,256]{1,0:T(8,128)(2,1)}, u32[]{:S(2)}) copy-start(bf16[2048,256]{1,0:T(8,128)(2,1)} %constant.15.clone.w_hbm) | copy-start | bytes 3145732
  0.0 36.3 %copy-start.2 = (s32[16]{0:T(128)S(1)}, s32[16]{0:T(128)}, u32[]{:S(2)}) copy-start(s32[16]{0:T(128)} %counts.3) | copy-start | bytes 196
  28.8 20.7 %all-to-all-start = ((bf16[16,112,128]{2,1,0:T(8,128)(2,1)}), bf16[16,112,128]{2,1,0:T(8,128)(2,1)}, u32[]{:S(2)}, u32[]{:S(2)}) async-start(bf16[16,112,128]{2,1,0:T(8,128)(2,1)} %shard_map.55), calls=%async_computation | async-start | bytes 917504 | tf_op jit(solution)/shard_map/all_to_all | solution.py:460
  36.3 19.5 %copy-start.3 = (s32[512]{0:T(512)S(1)}, s32[512]{0:T(512)}, u32[]{:S(2)}) copy-start(s32[512]{0:T(512)} %param.6) | copy-start | bytes 6148
  49.6 13.6 %all-to-all-start.1 = ((bf16[16,48,128]{2,1,0:T(8,128)(2,1)}), bf16[16,48,128]{2,1,0:T(8,128)(2,1)S(1)}, u32[]{:S(2)}, u32[]{:S(2)}) async-start(bf16[16,48,128]{2,1,0:T(8,128)(2,1)} %shard_map.56), calls=%async_computation.1 | async-start | bytes 393216 | tf_op jit(solution)/shard_map/all_to_all | solution.py:460
  54.1 17.3 %collective-permute-start = (bf16[16,112,128]{2,1,0:T(8,128)(2,1)}, bf16[16,112,128]{2,1,0:T(8,128)(2,1)S(1)}, u32[]{:S(2)}, u32[]{:S(2)}) collective-permute-start(bf16[16,112,128]{2,1,0:T(8,128)(2,1)} %all-to-all-done.part_hbm), channel_id=1, source_target_pairs={{0,1},{1,0},{2,3},{3,2},{4,5},{5,4},{6,7},{7,6},{8,9},{9,8},{10,11... | collective-permute-start | bytes 1376264 | tf_op jit(solution)/shard_map/ppermute | solution.py:464
  63.1 8.3 %collective-permute-start.1 = (bf16[16,48,128]{2,1,0:T(8,128)(2,1)S(1)}, bf16[16,48,128]{2,1,0:T(8,128)(2,1)S(1)}, u32[]{:S(2)}, u32[]{:S(2)}) collective-permute-start(bf16[16,48,128]{2,1,0:T(8,128)(2,1)S(1)} %all-to-all-done.1.refs_2_), channel_id=1, source_target_pairs={{0,1},{1,0},{2,3},{3,2},{4,5},{5,4},{6,7},{7,6},{8,9},{9,8},{10,11... | collective-permute-start | bytes 589832 | tf_op jit(solution)/shard_map/ppermute | solution.py:464

commit v12 on v11

--- a/solution.py
+++ b/solution.py
@@ -46,7 +46,7 @@
 
 
 def shifts_of(band):
-    return 4
+    return 8 if band <= 64 else 4
 
 
 def turn_lanes(value, shift):
@@ -121,8 +121,8 @@
         ]
 
     def begin(block):
-        for copy in fetch(block):
-            copy.start()
+        for r, copy in enumerate(fetch(block)):
+            copy.start(priority=r % 2)
 
     def analyse():
         signal = held[i % ahead].reshape(step * rows, FFT_LEN)
@@ -325,37 +325,43 @@
     )
 
 
-def settler(unit, dest_ref, part_hbm, out_ref, part, apart, pre, arrived):
-    copy = pltpu.make_async_copy(part_hbm, part, arrived)
-    copy.start()
-    turn = one_hot(dest_ref[...], out_ref.shape[1])
-    copy.wait()
-    regroup(part, apart, pre, unit, 0)
-    out_ref[...] = permute(pre[...], turn).astype(jnp.bfloat16)
-
-
-def settle(part, dest, total, unit):
+def settler(unit, dest_ref, own_hbm, other_hbm, out_ref, own, other, apart, pre, arrived):
+    copies = [
+        pltpu.make_async_copy(own_hbm, own, arrived.at[0]),
+        pltpu.make_async_copy(other_hbm, other, arrived.at[1]),
+    ]
+    for copy in copies:
+        copy.start()
+    turn = one_hot(dest_ref[...], out_ref.shape[2])
+    for h, part in enumerate((own, other)):
+        copies[h].wait()
+        regroup(part, apart, pre, unit, 0)
+        out_ref[h] = permute(pre[...], turn).astype(jnp.bfloat16)
+
+
+def settle(own, other, dest, total, unit):
     rows = 2 * CAP * NSPEC
     return pl.pallas_call(
         functools.partial(settler, unit),
-        in_specs=[pl.BlockSpec(memory_space=pltpu.VMEM), pl.BlockSpec(memory_space=pl.ANY)],
+        in_specs=[pl.BlockSpec(memory_space=pltpu.VMEM)] + [pl.BlockSpec(memory_space=pl.ANY)] * 2,
         out_specs=pl.BlockSpec(memory_space=pltpu.VMEM),
-        out_shape=jax.ShapeDtypeStruct((rows, total), jnp.bfloat16),
+        out_shape=jax.ShapeDtypeStruct((2, rows, total), jnp.bfloat16),
         scratch_shapes=[
-            pltpu.VMEM(part.shape, jnp.bfloat16),
-            pltpu.VMEM((2, part.shape[1] * LANES // unit, LANES), jnp.float32),
+            pltpu.VMEM(own.shape, jnp.bfloat16),
+            pltpu.VMEM(own.shape, jnp.bfloat16),
+            pltpu.VMEM((2, own.shape[1] * LANES // unit, LANES), jnp.float32),
             pltpu.VMEM((rows, dest.shape[1]), jnp.bfloat16),
-            pltpu.SemaphoreType.DMA,
+            pltpu.SemaphoreType.DMA((2,)),
         ],
         compiler_params=pltpu.CompilerParams(vmem_limit_bytes=32 * 1024 * 1024),
         cost_estimate=pl.CostEstimate(
-            flops=2 * rows * dest.shape[1] * total, bytes_accessed=2 * part.size + 2 * rows * total,
+            flops=4 * rows * dest.shape[1] * total, bytes_accessed=4 * own.size + 4 * rows * total,
             transcendentals=0,
         ),
-    )(dest, part)
-
-
-def correlator(unit, own_count, counts, where, dest_ref, *refs):
+    )(dest, own, other)
+
+
+def correlator(unit, counts, where, dest_ref, *refs):
     given = (len(refs) - 6) // 2
     sources, out_ref, held = refs[:given], refs[given], refs[given + 1 : 2 * given + 1]
     apart, pre, post, near, arrived = refs[2 * given + 1 :]
@@ -375,22 +381,12 @@
         turn = one_hot(dest_ref[...], total)
         for copy in copies:
             copy.wait()
-        other = held[:-own_count]
-        ours = held[len(held) - own_count :]
-        base = 0
-        for ref in other:
-            regroup(ref, apart, pre, unit, base)
-            base += streams_in(ref, unit)
-        halves = [permute(pre[...], turn)]
-        fresh = ours[0]
-        width = streams_in(fresh, unit)
-        regroup(fresh, apart, pre, unit, total - width)
-        mine = permute(pre[:, total - width :], turn[:, total - width :])
-        for ref in ours[1:]:
-            mine = mine + ref[...].astype(jnp.float32)
-        halves.append(mine)
-        for n in range(2 * CAP):
-            for h, half in enumerate(halves):
+        for h in range(2):
+            regroup(held[h], apart, pre, unit, 0)
+            half = permute(pre[...], turn)
+            for ref in held[2:]:
+                half = half + ref[h].astype(jnp.float32)
+            for n in range(2 * CAP):
                 first = n % 2 * time_len + h * NSPEC
                 post[n // 2, first : first + NSPEC] = half[n * NSPEC : (n + 1) * NSPEC].astype(
                     jnp.bfloat16
@@ -416,23 +412,22 @@
         put(jnp.concatenate([-post[k, time_len:], post[k, :time_len]], axis=0))
 
 
-def correlate(others, ours, dest, chan_counts, where, unit):
-    total = dest.shape[1]
-    operands = others + ours
-    most = max(a.shape[1] for a in operands if a.ndim == 3)
+def correlate(operands, dest, chan_counts, where, total, unit):
+    held = dest.shape[1]
+    most = operands[0].shape[1]
     rows = total // 2
     return pl.pallas_call(
-        functools.partial(correlator, unit, len(ours)),
+        functools.partial(correlator, unit),
         grid_spec=pltpu.PrefetchScalarGridSpec(
             num_scalar_prefetch=2,
             grid=(CAP, 2),
-            in_specs=[pl.BlockSpec((1, total), lambda k, p, c, w: (0, 0))]
+            in_specs=[pl.BlockSpec((1, held), lambda k, p, c, w: (0, 0))]
             + [pl.BlockSpec(memory_space=pl.ANY)] * len(operands),
             out_specs=pl.BlockSpec((1, 1, 1, rows, total), lambda k, p, c, w: (0, k, p, 0, 0)),
             scratch_shapes=[pltpu.VMEM(a.shape, jnp.bfloat16) for a in operands]
             + [
                 pltpu.VMEM((2, most * LANES // unit, LANES), jnp.float32),
-                pltpu.VMEM((2 * CAP * NSPEC, total), jnp.bfloat16),
+                pltpu.VMEM((2 * CAP * NSPEC, held), jnp.bfloat16),
                 pltpu.VMEM((CAP, 4 * NSPEC, total), jnp.bfloat16),
                 pltpu.VMEM((rows, 4 * NSPEC), jnp.bfloat16),
                 pltpu.SemaphoreType.DMA((len(operands),)),
@@ -452,18 +447,22 @@
     dest = (2 * station_map[:, None] + jnp.arange(2, dtype=jnp.int32)[None, :]).reshape(-1)
     dest = dest.reshape(dests, streams // unit, unit).transpose(1, 0, 2)
     where = jnp.stack([lax.axis_index("stn"), lax.axis_index("blk")]).astype(jnp.int32)
-    others, settled = [], []
+    settled = []
     start = 0
     for size, step, room in plan:
         outgoing = channelize(voltages, chan_counts, dests, start, size, step, unit, room)
         chan_counts, outgoing = lax.optimization_barrier((chan_counts, outgoing))
         own = lax.all_to_all(outgoing, "stn", split_axis=0, concat_axis=0, tiled=True)
-        spot = dest[start // unit : (start + size) // unit]
+        if settled:
+            own, other = lax.optimization_barrier((own, other))
+            settled = [settle(before, other, spot, total, unit)]
+        other = lax.ppermute(own, "blk", [(0, 1), (1, 0)])
+        spot = dest[start // unit : (start + size) // unit].reshape(1, -1)
         if start + size < streams:
-            settled.append(settle(own, spot.reshape(1, -1), total, unit))
-        others.append(lax.ppermute(own, "blk", [(0, 1), (1, 0)]))
+            before = own
+            settled = [None]
         start = start + size
-    return correlate(others, [own] + settled, dest.reshape(1, -1), chan_counts, where, unit)
+    return correlate([own, other] + settled, spot, chan_counts, where, total, unit)
 
 
 def solution(mesh):

time: 80.9 us -> 88.8 us (1.098)
  blocking collectives: 0 us -> 20.6 us
  starting transfers between devices: 15.2 us -> 5.95 us
  Pallas kernels: 52.1 us -> 50.4 us
  waiting for transfers between devices: 12.4 us -> 10.8 us
    all_to_all x0 -> x1, blocking collectives: none -> 20.6 us  [body(): lax.all_to_all(outgoing, 'stn', split_axis=0, concat_axis=0, tiled=True)]
    all_to_all x2 -> x1, starting transfers between devices: 12 us -> 3.91 us  [body(): lax.all_to_all(outgoing, 'stn', split_axis=0, concat_axis=0, tiled=True)]
    pallas_call x1, Pallas kernels: 9.11 us -> 7.54 us  [correlate(): pl.pallas_call(functools.partial(correlator, unit), grid_spec=pltpu.Prefe...]
    ppermute x2, waiting for transfers between devices: 3.92 us -> 2.5 us  [body(): other = lax.ppermute(own, 'blk', [(0, 1), (1, 0)])]
    pallas_call x2, Pallas kernels: 40.7 us -> 39.4 us  [channelize(): pl.pallas_call(kernel, grid_spec=pltpu.PrefetchScalarGridSpec(num_scalar_...]
    pallas_call x1, Pallas kernels: 2.26 us -> 3.46 us  [settle(): pl.pallas_call(functools.partial(settler, unit), in_specs=[pl.BlockSpec(m...]
    ppermute x2, starting transfers between devices: 3.23 us -> 2.04 us  [body(): other = lax.ppermute(own, 'blk', [(0, 1), (1, 0)])]
    all_to_all x2 -> x1, waiting for transfers between devices: 8.47 us -> 8.28 us  [body(): lax.all_to_all(outgoing, 'stn', split_axis=0, concat_axis=0, tiled=True)]
  transfers between devices with their start and end apart: 4 -> 3, of which waited for: 3 -> 2; matrix products, arithmetic and copies ran while one was open for 1% -> 1% of each run, Pallas kernels for 18% -> 17%
where the time goes in v12:
time: 88.8 us; the launch traced here: 88.5 us
  Pallas kernels  50.4 us (57%)
  blocking collectives  20.6 us (23%)
  waiting for transfers between devices  10.8 us (12%)
  starting transfers between devices  5.95 us (7%)
    pallas_call x2, Pallas kernels, channelize(): pl.pallas_call(kernel, grid_spec=pltpu.PrefetchScalarGridSpec(num_scalar_...  39.4 us
    all_to_all x1, blocking collectives, body(): lax.all_to_all(outgoing, 'stn', split_axis=0, concat_axis=0, tiled=True)  20.6 us
    all_to_all x1, waiting for transfers between devices, body(): lax.all_to_all(outgoing, 'stn', split_axis=0, concat_axis=0, tiled=True)  8.28 us
    pallas_call x1, Pallas kernels, correlate(): pl.pallas_call(functools.partial(correlator, unit), grid_spec=pltpu.Prefe...  7.54 us
    all_to_all x1, starting transfers between devices, body(): lax.all_to_all(outgoing, 'stn', split_axis=0, concat_axis=0, tiled=True)  3.91 us
    pallas_call x1, Pallas kernels, settle(): pl.pallas_call(functools.partial(settler, unit), in_specs=[pl.BlockSpec(m...  3.46 us
    ppermute x2, waiting for transfers between devices, body(): other = lax.ppermute(own, 'blk', [(0, 1), (1, 0)])  2.5 us
    ppermute x2, starting transfers between devices, body(): other = lax.ppermute(own, 'blk', [(0, 1), (1, 0)])  2.04 us
  transfers between devices with their start and end apart: 3, of which 2 were waited for; matrix products, arithmetic and copies ran while one was open for 1% of the time, Pallas kernels for 17%

profile of v12, /device:TPU:0, one launch (start us, length us, event | category | flops | bytes accessed | tf_op | source)
XLA Modules:
  0.0 88.5 jit_solution(11940409757477553612)
XLA Ops:
  0.0 0.0 copy-start
  0.0 0.0 copy-start.1
  0.0 0.0 copy-start.2
  0.0 27.4 %shard_map.55 = bf16[16,112,128]{2,1,0:T(8,128)(2,1)} custom-call(s32[16]{0:T(128)} %counts.3, bf16[64,1,63,2,4096]{4,3,2,1,0:T(2,128)(2,1)} %v_ref.3, bf16[4096,256]{1,0:T(8,128)(2,1)} %constant.14.clone.u_hbm, bf16[1024,512]{1,0:T(8,128)(2,1)} %constant.15.clone.w_hbm), custom_call_target="tpu_custom_call" | custom-call | flops 12683575296 | bytes 49545216 | tf_op jit(solution)/shard_map/pallas_call | solution.py:252
  27.4 20.6 %all_to_all.10.own_hbm = bf16[16,112,128]{2,1,0:T(8,128)(2,1)S(1)} all-to-all(bf16[16,112,128]{2,1,0:T(8,128)(2,1)} %shard_map.55), channel_id=1, replica_groups=mesh['stn'=16,'blk'=2] {'stn'}, dimensions={0} | all-to-all | bytes 917504 | tf_op jit(solution)/shard_map/all_to_all | solution.py:455
  48.0 0.0 copy-start.3
  48.0 1.5 %collective-permute-start = (bf16[16,112,128]{2,1,0:T(8,128)(2,1)S(1)}, bf16[16,112,128]{2,1,0:T(8,128)(2,1)S(1)}, u32[]{:S(2)}, u32[]{:S(2)}) collective-permute-start(bf16[16,112,128]{2,1,0:T(8,128)(2,1)S(1)} %all_to_all.10.own_hbm), channel_id=1, source_target_pairs={{0,1},{1,0},{2,3},{3,2},{4,5},{5,4},{6,7},{7,6},{8,9},{9,8},{10,11... | collective-permute-start | bytes 1376264 | tf_op jit(solution)/shard_map/ppermute | solution.py:459
  49.5 0.0 copy-done
  49.5 0.0 copy-done.1
  49.5 0.0 copy-done.2
  49.5 12.0 %shard_map.56 = bf16[16,48,128]{2,1,0:T(8,128)(2,1)} custom-call(s32[16]{0:T(128)S(1)} %copy-done.2, bf16[64,1,63,2,4096]{4,3,2,1,0:T(2,128)(2,1)} %v_ref.3, bf16[4096,256]{1,0:T(8,128)(2,1)S(1)} %copy-done, bf16[1024,512]{1,0:T(8,128)(2,1)S(1)} %copy-done.1), custom_call_target="tpu_custom_call" | custom-call | flops 4227858432 | bytes 16515072 | tf_op jit(solution)/shard_map/pallas_call | solution.py:252
  61.5 3.9 %all-to-all-start = ((bf16[16,48,128]{2,1,0:T(8,128)(2,1)}), bf16[16,48,128]{2,1,0:T(8,128)(2,1)S(1)}, u32[]{:S(2)}, u32[]{:S(2)}) async-start(bf16[16,48,128]{2,1,0:T(8,128)(2,1)} %shard_map.56), calls=%async_computation | async-start | bytes 393216 | tf_op jit(solution)/shard_map/all_to_all | solution.py:455
  65.5 0.1 add.26
  65.5 0.0 copy-done.3
  65.6 0.1 add.22
  65.7 0.1 copy.6
  65.8 0.1 add_bitcast_fusion
  65.9 0.1 copy.8
  65.9 0.1 reshape.13.dest_ref
  66.0 0.1 copy.7
  66.1 0.1 reshape.12.dest_ref
  66.2 8.3 %all-to-all-done.refs_0_ = bf16[16,48,128]{2,1,0:T(8,128)(2,1)S(1)} async-done(((bf16[16,48,128]{2,1,0:T(8,128)(2,1)}), bf16[16,48,128]{2,1,0:T(8,128)(2,1)S(1)}, u32[]{:S(2)}, u32[]{:S(2)}) %all-to-all-start) | async-done | bytes 196640 | tf_op jit(solution)/shard_map/all_to_all | solution.py:455
  74.4 0.0 collective-permute-done.other_hbm
  74.4 0.5 collective-permute-start.1
  75.0 0.1 pad_add_fusion.where
  75.0 3.5 %shard_map.57.refs_2_ = bf16[2,288,1024]{2,1,0:T(8,128)(2,1)S(1)} custom-call(s32[1,768]{1,0:T(1,128)S(1)} %reshape.13.dest_ref, bf16[16,112,128]{2,1,0:T(8,128)(2,1)S(1)} %all_to_all.10.own_hbm, bf16[16,112,128]{2,1,0:T(8,128)(2,1)S(1)} %collective-permute-done.other_hbm), custom_call_target="tpu_custom_call" | custom-call | flops 905969664 | bytes 2097152 | tf_op jit(solution)/shard_map/pallas_call | solution.py:344
  78.5 2.5 %collective-permute-done.1.refs_1_ = bf16[16,48,128]{2,1,0:T(8,128)(2,1)S(1)} collective-permute-done((bf16[16,48,128]{2,1,0:T(8,128)(2,1)S(1)}, bf16[16,48,128]{2,1,0:T(8,128)(2,1)S(1)}, u32[]{:S(2)}, u32[]{:S(2)}) %collective-permute-start.1) | collective-permute-done | bytes 196640 | tf_op jit(solution)/shard_map/ppermute | solution.py:459
  81.0 7.5 %shard_map.58 = bf16[1,3,2,512,1024]{4,3,2,1,0:T(8,128)(2,1)} custom-call(s32[16]{0:T(128)S(1)} %copy-done.2, s32[2]{0:T(128)S(1)} %pad_add_fusion.where, s32[1,256]{1,0:T(1,128)S(1)} %reshape.12.dest_ref, bf16[16,48,128]{2,1,0:T(8,128)(2,1)S(1)} %all-to-all-done.refs_0_, bf16[16,48,128]{2,1,0:T(8,128)(2,1)S(1)} %collective-permute-done.1.refs_1_, ...), custom_call_target="tpu_custom_call" | custom-call | tf_op jit(solution)/shard_map/pallas_call | solution.py:419
  (5 shorter events, 0.0 us)
Async XLA Ops:
  0.0 49.5 %copy-start = (bf16[4096,256]{1,0:T(8,128)(2,1)S(1)}, bf16[4096,256]{1,0:T(8,128)(2,1)}, u32[]{:S(2)}) copy-start(bf16[4096,256]{1,0:T(8,128)(2,1)} %constant.14.clone.u_hbm) | copy-start | bytes 6291460
  0.0 49.5 %copy-start.1 = (bf16[1024,512]{1,0:T(8,128)(2,1)S(1)}, bf16[1024,512]{1,0:T(8,128)(2,1)}, u32[]{:S(2)}) copy-start(bf16[1024,512]{1,0:T(8,128)(2,1)} %constant.15.clone.w_hbm) | copy-start | bytes 3145732
  0.0 49.5 %copy-start.2 = (s32[16]{0:T(128)S(1)}, s32[16]{0:T(128)}, u32[]{:S(2)}) copy-start(s32[16]{0:T(128)} %counts.3) | copy-start | bytes 196
  48.0 17.6 %copy-start.3 = (s32[512]{0:T(512)S(1)}, s32[512]{0:T(512)}, u32[]{:S(2)}) copy-start(s32[512]{0:T(512)} %param.6) | copy-start | bytes 6148
  48.0 26.5 %collective-permute-start = (bf16[16,112,128]{2,1,0:T(8,128)(2,1)S(1)}, bf16[16,112,128]{2,1,0:T(8,128)(2,1)S(1)}, u32[]{:S(2)}, u32[]{:S(2)}) collective-permute-start(bf16[16,112,128]{2,1,0:T(8,128)(2,1)S(1)} %all_to_all.10.own_hbm), channel_id=1, source_target_pairs={{0,1},{1,0},{2,3},{3,2},{4,5},{5,4},{6,7},{7,6},{8,9},{9,8},{10,11... | collective-permute-start | bytes 1376264 | tf_op jit(solution)/shard_map/ppermute | solution.py:459
  61.5 12.9 %all-to-all-start = ((bf16[16,48,128]{2,1,0:T(8,128)(2,1)}), bf16[16,48,128]{2,1,0:T(8,128)(2,1)S(1)}, u32[]{:S(2)}, u32[]{:S(2)}) async-start(bf16[16,48,128]{2,1,0:T(8,128)(2,1)} %shard_map.56), calls=%async_computation | async-start | bytes 393216 | tf_op jit(solution)/shard_map/all_to_all | solution.py:455
  74.4 6.5 %collective-permute-start.1 = (bf16[16,48,128]{2,1,0:T(8,128)(2,1)S(1)}, bf16[16,48,128]{2,1,0:T(8,128)(2,1)S(1)}, u32[]{:S(2)}, u32[]{:S(2)}) collective-permute-start(bf16[16,48,128]{2,1,0:T(8,128)(2,1)S(1)} %all-to-all-done.refs_0_), channel_id=1, source_target_pairs={{0,1},{1,0},{2,3},{3,2},{4,5},{5,4},{6,7},{7,6},{8,9},{9,8},{10,11... | collective-permute-start | bytes 589832 | tf_op jit(solution)/shard_map/ppermute | solution.py:459

commit v13 on v12

--- a/solution.py
+++ b/solution.py
@@ -443,25 +443,37 @@
     streams = voltages.shape[0]
     total = dests * streams
     unit = min(streams, 16)
-    plan = ((48, 4, 60), (16, 2, 32)) if streams == 64 else ((streams, 2, 60),)
     dest = (2 * station_map[:, None] + jnp.arange(2, dtype=jnp.int32)[None, :]).reshape(-1)
     dest = dest.reshape(dests, streams // unit, unit).transpose(1, 0, 2)
     where = jnp.stack([lax.axis_index("stn"), lax.axis_index("blk")]).astype(jnp.int32)
-    settled = []
-    start = 0
-    for size, step, room in plan:
-        outgoing = channelize(voltages, chan_counts, dests, start, size, step, unit, room)
+
+    def turn(outgoing):
+        return lax.all_to_all(outgoing, "stn", split_axis=0, concat_axis=0, tiled=True)
+
+    def swap(own):
+        return lax.ppermute(own, "blk", [(0, 1), (1, 0)])
+
+    def spots(start, size):
+        return dest[start // unit : (start + size) // unit].reshape(1, -1)
+
+    if streams == 64:
+        early, late = 48, 16
+        outgoing = channelize(voltages, chan_counts, dests, 0, early, 4, unit, 60)
         chan_counts, outgoing = lax.optimization_barrier((chan_counts, outgoing))
-        own = lax.all_to_all(outgoing, "stn", split_axis=0, concat_axis=0, tiled=True)
-        if settled:
-            own, other = lax.optimization_barrier((own, other))
-            settled = [settle(before, other, spot, total, unit)]
-        other = lax.ppermute(own, "blk", [(0, 1), (1, 0)])
-        spot = dest[start // unit : (start + size) // unit].reshape(1, -1)
-        if start + size < streams:
-            before = own
-            settled = [None]
-        start = start + size
+        first = turn(outgoing)
+        outgoing = channelize(voltages, chan_counts, dests, early, late, 2, unit, 32)
+        first, outgoing = lax.optimization_barrier((first, outgoing))
+        first_other = swap(first)
+        own = turn(outgoing)
+        own, first_other = lax.optimization_barrier((own, first_other))
+        other = swap(own)
+        settled = [settle(first, first_other, spots(0, early), total, unit)]
+    else:
+        late = streams
+        own = turn(channelize(voltages, chan_counts, dests, 0, late, 2, unit, 60))
+        other = swap(own)
+        settled = []
+    spot = spots(streams - late, late)
     return correlate([own, other] + settled, spot, chan_counts, where, total, unit)
 
 

time: 88.8 us -> 77.9 us (0.88)
  blocking collectives: 20.6 us -> 0 us
  starting transfers between devices: 5.95 us -> 14.2 us
  waiting for transfers between devices: 10.8 us -> 12.1 us
    all_to_all x1 -> x0, blocking collectives: 20.6 us -> none  [body(): lax.all_to_all(outgoing, 'stn', split_axis=0, concat_axis=0, tiled=True)]
    all_to_all x1 -> x2, starting transfers between devices: 3.91 us -> 12.2 us  [turn(): lax.all_to_all(outgoing, 'stn', split_axis=0, concat_axis=0, tiled=True)]
    all_to_all x1 -> x2, waiting for transfers between devices: 8.28 us -> 9.63 us  [turn(): lax.all_to_all(outgoing, 'stn', split_axis=0, concat_axis=0, tiled=True)]
  transfers between devices with their start and end apart: 3 -> 4, of which waited for: 2 -> 3; matrix products, arithmetic and copies ran while one was open for 1% -> 1% of each run, Pallas kernels for 17% -> 20%
where the time goes in v13:
time: 77.9 us; the launch traced here: 77.6 us
  Pallas kernels  50.5 us (65%)
  starting transfers between devices  14.2 us (18%)
  waiting for transfers between devices  12.1 us (16%)
    pallas_call x2, Pallas kernels, channelize(): pl.pallas_call(kernel, grid_spec=pltpu.PrefetchScalarGridSpec(num_scalar_...  39.4 us
    all_to_all x2, starting transfers between devices, turn(): lax.all_to_all(outgoing, 'stn', split_axis=0, concat_axis=0, tiled=True)  12.2 us
    all_to_all x2, waiting for transfers between devices, turn(): lax.all_to_all(outgoing, 'stn', split_axis=0, concat_axis=0, tiled=True)  9.63 us
    pallas_call x1, Pallas kernels, correlate(): pl.pallas_call(functools.partial(correlator, unit), grid_spec=pltpu.Prefe...  7.53 us
    pallas_call x1, Pallas kernels, settle(): pl.pallas_call(functools.partial(settler, unit), in_specs=[pl.BlockSpec(m...  3.54 us
    ppermute x2, waiting for transfers between devices, swap(): return lax.ppermute(own, 'blk', [(0, 1), (1, 0)])  2.44 us
    ppermute x2, starting transfers between devices, swap(): return lax.ppermute(own, 'blk', [(0, 1), (1, 0)])  2.02 us
  transfers between devices with their start and end apart: 4, of which 3 were waited for; matrix products, arithmetic and copies ran while one was open for 1% of the time, Pallas kernels for 20%

profile of v13, /device:TPU:0, one launch (start us, length us, event | category | flops | bytes accessed | tf_op | source)
XLA Modules:
  0.0 77.6 jit_solution(8770056588356769598)
XLA Ops:
  0.0 0.0 copy-start
  0.0 0.0 copy-start.1
  0.0 0.0 copy-start.2
  0.0 27.4 %shard_map.55 = bf16[16,112,128]{2,1,0:T(8,128)(2,1)} custom-call(s32[16]{0:T(128)} %counts.3, bf16[64,1,63,2,4096]{4,3,2,1,0:T(2,128)(2,1)} %v_ref.3, bf16[4096,256]{1,0:T(8,128)(2,1)} %constant.14.clone.u_hbm, bf16[1024,512]{1,0:T(8,128)(2,1)} %constant.15.clone.w_hbm), custom_call_target="tpu_custom_call" | custom-call | flops 12683575296 | bytes 49545216 | tf_op jit(solution)/shard_map/pallas_call | solution.py:252
  27.4 7.4 %all-to-all-start = ((bf16[16,112,128]{2,1,0:T(8,128)(2,1)}), bf16[16,112,128]{2,1,0:T(8,128)(2,1)}, u32[]{:S(2)}, u32[]{:S(2)}) async-start(bf16[16,112,128]{2,1,0:T(8,128)(2,1)} %shard_map.55), calls=%async_computation | async-start | bytes 917504 | tf_op jit(solution)/shard_map/all_to_all | solution.py:451
  34.8 0.0 copy-done
  34.8 0.0 copy-done.1
  34.8 0.0 copy-done.2
  34.8 0.0 copy-start.3
  34.8 12.0 %shard_map.56 = bf16[16,48,128]{2,1,0:T(8,128)(2,1)} custom-call(s32[16]{0:T(128)S(1)} %copy-done.2, bf16[64,1,63,2,4096]{4,3,2,1,0:T(2,128)(2,1)} %v_ref.3, bf16[4096,256]{1,0:T(8,128)(2,1)S(1)} %copy-done, bf16[1024,512]{1,0:T(8,128)(2,1)S(1)} %copy-done.1), custom_call_target="tpu_custom_call" | custom-call | flops 4227858432 | bytes 16515072 | tf_op jit(solution)/shard_map/pallas_call | solution.py:252
  46.8 1.3 %all-to-all-done.own_hbm = bf16[16,112,128]{2,1,0:T(8,128)(2,1)} async-done(((bf16[16,112,128]{2,1,0:T(8,128)(2,1)}), bf16[16,112,128]{2,1,0:T(8,128)(2,1)}, u32[]{:S(2)}, u32[]{:S(2)}) %all-to-all-start) | async-done | bytes 458784 | tf_op jit(solution)/shard_map/all_to_all | solution.py:451
  48.1 1.5 %collective-permute-start = (bf16[16,112,128]{2,1,0:T(8,128)(2,1)}, bf16[16,112,128]{2,1,0:T(8,128)(2,1)S(1)}, u32[]{:S(2)}, u32[]{:S(2)}) collective-permute-start(bf16[16,112,128]{2,1,0:T(8,128)(2,1)} %all-to-all-done.own_hbm), channel_id=1, source_target_pairs={{0,1},{1,0},{2,3},{3,2},{4,5},{5,4},{6,7},{7,6},{8,9},{9,8},{10,11... | collective-permute-start | bytes 1376264 | tf_op jit(solution)/shard_map/ppermute | solution.py:454
  49.6 0.1 add.26
  49.7 4.8 %all-to-all-start.1 = ((bf16[16,48,128]{2,1,0:T(8,128)(2,1)}), bf16[16,48,128]{2,1,0:T(8,128)(2,1)S(1)}, u32[]{:S(2)}, u32[]{:S(2)}) async-start(bf16[16,48,128]{2,1,0:T(8,128)(2,1)} %shard_map.56), calls=%async_computation.1 | async-start | bytes 393216 | tf_op jit(solution)/shard_map/all_to_all | solution.py:451
  54.5 0.0 copy-done.3
  54.5 0.1 add.22
  54.6 0.1 copy.6
  54.7 0.1 add_bitcast_fusion
  54.8 0.1 copy.8
  54.9 0.1 reshape.13.dest_ref
  55.0 0.1 copy.7
  55.0 0.1 reshape.12.dest_ref
  55.1 8.4 %all-to-all-done.1.refs_0_ = bf16[16,48,128]{2,1,0:T(8,128)(2,1)S(1)} async-done(((bf16[16,48,128]{2,1,0:T(8,128)(2,1)}), bf16[16,48,128]{2,1,0:T(8,128)(2,1)S(1)}, u32[]{:S(2)}, u32[]{:S(2)}) %all-to-all-start.1) | async-done | bytes 196640 | tf_op jit(solution)/shard_map/all_to_all | solution.py:451
  63.5 0.0 collective-permute-done.other_hbm
  63.5 0.5 collective-permute-start.1
  64.0 0.1 pad_add_fusion.where
  64.1 3.5 %shard_map.57.refs_2_ = bf16[2,288,1024]{2,1,0:T(8,128)(2,1)S(1)} custom-call(s32[1,768]{1,0:T(1,128)S(1)} %reshape.13.dest_ref, bf16[16,112,128]{2,1,0:T(8,128)(2,1)} %all-to-all-done.own_hbm, bf16[16,112,128]{2,1,0:T(8,128)(2,1)S(1)} %collective-permute-done.other_hbm), custom_call_target="tpu_custom_call" | custom-call | flops 905969664 | bytes 2097152 | tf_op jit(solution)/shard_map/pallas_call | solution.py:344
  67.6 2.4 %collective-permute-done.1.refs_1_ = bf16[16,48,128]{2,1,0:T(8,128)(2,1)S(1)} collective-permute-done((bf16[16,48,128]{2,1,0:T(8,128)(2,1)S(1)}, bf16[16,48,128]{2,1,0:T(8,128)(2,1)S(1)}, u32[]{:S(2)}, u32[]{:S(2)}) %collective-permute-start.1) | collective-permute-done | bytes 196640 | tf_op jit(solution)/shard_map/ppermute | solution.py:454
  70.0 7.5 %shard_map.58 = bf16[1,3,2,512,1024]{4,3,2,1,0:T(8,128)(2,1)} custom-call(s32[16]{0:T(128)S(1)} %copy-done.2, s32[2]{0:T(128)S(1)} %pad_add_fusion.where, s32[1,256]{1,0:T(1,128)S(1)} %reshape.12.dest_ref, bf16[16,48,128]{2,1,0:T(8,128)(2,1)S(1)} %all-to-all-done.1.refs_0_, bf16[16,48,128]{2,1,0:T(8,128)(2,1)S(1)} %collective-permute-done.1.refs_1_, ...), custom_call_target="tpu_custom_call" | custom-call | tf_op jit(solution)/shard_map/pallas_call | solution.py:419
  (5 shorter events, 0.0 us)
Async XLA Ops:
  0.0 34.8 %copy-start = (bf16[4096,256]{1,0:T(8,128)(2,1)S(1)}, bf16[4096,256]{1,0:T(8,128)(2,1)}, u32[]{:S(2)}) copy-start(bf16[4096,256]{1,0:T(8,128)(2,1)} %constant.14.clone.u_hbm) | copy-start | bytes 6291460
  0.0 34.8 %copy-start.1 = (bf16[1024,512]{1,0:T(8,128)(2,1)S(1)}, bf16[1024,512]{1,0:T(8,128)(2,1)}, u32[]{:S(2)}) copy-start(bf16[1024,512]{1,0:T(8,128)(2,1)} %constant.15.clone.w_hbm) | copy-start | bytes 3145732
  0.0 34.8 %copy-start.2 = (s32[16]{0:T(128)S(1)}, s32[16]{0:T(128)}, u32[]{:S(2)}) copy-start(s32[16]{0:T(128)} %counts.3) | copy-start | bytes 196
  27.4 20.7 %all-to-all-start = ((bf16[16,112,128]{2,1,0:T(8,128)(2,1)}), bf16[16,112,128]{2,1,0:T(8,128)(2,1)}, u32[]{:S(2)}, u32[]{:S(2)}) async-start(bf16[16,112,128]{2,1,0:T(8,128)(2,1)} %shard_map.55), calls=%async_computation | async-start | bytes 917504 | tf_op jit(solution)/shard_map/all_to_all | solution.py:451
  34.8 19.7 %copy-start.3 = (s32[512]{0:T(512)S(1)}, s32[512]{0:T(512)}, u32[]{:S(2)}) copy-start(s32[512]{0:T(512)} %param.6) | copy-start | bytes 6148
  48.1 15.4 %collective-permute-start = (bf16[16,112,128]{2,1,0:T(8,128)(2,1)}, bf16[16,112,128]{2,1,0:T(8,128)(2,1)S(1)}, u32[]{:S(2)}, u32[]{:S(2)}) collective-permute-start(bf16[16,112,128]{2,1,0:T(8,128)(2,1)} %all-to-all-done.own_hbm), channel_id=1, source_target_pairs={{0,1},{1,0},{2,3},{3,2},{4,5},{5,4},{6,7},{7,6},{8,9},{9,8},{10,11... | collective-permute-start | bytes 1376264 | tf_op jit(solution)/shard_map/ppermute | solution.py:454
  49.7 13.8 %all-to-all-start.1 = ((bf16[16,48,128]{2,1,0:T(8,128)(2,1)}), bf16[16,48,128]{2,1,0:T(8,128)(2,1)S(1)}, u32[]{:S(2)}, u32[]{:S(2)}) async-start(bf16[16,48,128]{2,1,0:T(8,128)(2,1)} %shard_map.56), calls=%async_computation.1 | async-start | bytes 393216 | tf_op jit(solution)/shard_map/all_to_all | solution.py:451
  63.5 6.5 %collective-permute-start.1 = (bf16[16,48,128]{2,1,0:T(8,128)(2,1)S(1)}, bf16[16,48,128]{2,1,0:T(8,128)(2,1)S(1)}, u32[]{:S(2)}, u32[]{:S(2)}) collective-permute-start(bf16[16,48,128]{2,1,0:T(8,128)(2,1)S(1)} %all-to-all-done.1.refs_0_), channel_id=1, source_target_pairs={{0,1},{1,0},{2,3},{3,2},{4,5},{5,4},{6,7},{7,6},{8,9},{9,8},{10,11... | collective-permute-start | bytes 589832 | tf_op jit(solution)/shard_map/ppermute | solution.py:454

commit v14 on v12

--- a/solution.py
+++ b/solution.py
@@ -212,6 +212,8 @@
     @pl.when(i == last)
     def _():
         mix(i - 1)
+
+    def finish(u):
         lane = lax.broadcasted_iota(jnp.int32, (8, wide * LANES), 1)
         row = lax.broadcasted_iota(jnp.int32, (8, wide * LANES), 0)
         slot = row // 2
@@ -219,27 +221,37 @@
         picks = []
         offset = jnp.int32(0)
         for d in range(dests):
-            held = counts[d]
-            want = offset + jnp.minimum(slot, held - 1) + base
+            held_here = counts[d]
+            want = offset + jnp.minimum(slot, held_here - 1) + base
             picks.append(jnp.where((lane == want) & (row < 2 * CAP), 1.0, 0.0))
-            offset = offset + held
+            offset = offset + held_here
         pick = jnp.concatenate(picks, axis=0).astype(jnp.bfloat16)
-        spectra = jnp.concatenate([x[n] for n in range(wide)], axis=1)
+        size = NSPEC * unit
+        from_row = pl.multiple_of(u * size, 8)
+        spectra = jnp.concatenate([x[n, pl.ds(from_row, size), :] for n in range(wide)], axis=1)
         out = lax.dot_general(
             pick, spectra.astype(jnp.bfloat16), (((1,), (1,)), ((), ())),
             preferred_element_type=jnp.float32,
         )
-        tiles = NSPEC * unit // LANES
+        tiles = size // LANES
         for d in range(dests):
-            for t in range(streams // unit * tiles):
-                row = t // tiles * (2 * CAP * tiles) + t % tiles
-                turned[d, pl.ds(row, 2 * CAP, stride=tiles), :] = out[
+            for t in range(tiles):
+                turned[d, pl.ds(u * (2 * CAP * tiles) + t, 2 * CAP, stride=tiles), :] = out[
                     8 * d : 8 * d + 2 * CAP, t * LANES : (t + 1) * LANES
                 ]
-        out_ref[...] = turned[...].astype(jnp.bfloat16)
-
-
-def channelize(voltages, chan_counts, dests, start, streams, step, unit, room):
+
+    @pl.when((i > 0) & (i % (unit // step) == 0))
+    def _():
+        finish(i // (unit // step) - 1)
+
+    @pl.when(i == last)
+    def _():
+        whole = turned[...].astype(jnp.bfloat16)
+        for n in range(out_ref.shape[1]):
+            out_ref[:, n] = whole
+
+
+def channelize(voltages, chan_counts, dests, start, streams, step, unit, room, copies):
     band = 2 * dests
     frames = voltages.shape[2]
     analysis, mixing = tables(band)
@@ -255,7 +267,7 @@
             num_scalar_prefetch=1,
             grid=(steps + 1,),
             in_specs=[pl.BlockSpec(memory_space=pl.ANY)] * 3,
-            out_specs=pl.BlockSpec((dests, payload, LANES), lambda i, c: (0, 0, 0)),
+            out_specs=pl.BlockSpec((dests, copies, payload, LANES), lambda i, c: (0, 0, 0, 0)),
             scratch_shapes=[
                 pltpu.VMEM((ahead, step, frames, 2, FFT_LEN), jnp.bfloat16),
                 pltpu.VMEM(analysis.shape, jnp.bfloat16),
@@ -267,7 +279,7 @@
                 pltpu.SemaphoreType.DMA((ahead + 1, step)),
             ],
         ),
-        out_shape=jax.ShapeDtypeStruct((dests, payload, LANES), jnp.bfloat16),
+        out_shape=jax.ShapeDtypeStruct((dests, copies, payload, LANES), jnp.bfloat16),
         compiler_params=pltpu.CompilerParams(
             vmem_limit_bytes=room * 1024 * 1024
         ),
@@ -275,24 +287,22 @@
             flops=2 * streams * 2 * frames * analysis.size,
             bytes_accessed=2 * 2 * frames * FFT_LEN * streams, transcendentals=0,
         ),
-    )(chan_counts, voltages, jnp.asarray(analysis), jnp.asarray(mixing))
+    )(chan_counts, voltages, jnp.asarray(analysis), jnp.asarray(mixing)).reshape(-1, payload, LANES)
 
 
 def payload_rows(units, unit):
     return -(-units * 2 * CAP * NSPEC * unit // (16 * LANES)) * 16
 
 
-def streams_in(part, unit):
-    return part.shape[0] * unit * (part.shape[1] * LANES // (2 * CAP * NSPEC * unit))
-
-
-def regroup(ref, apart, pre, unit, base):
+def regroup(ref, apart, pre, unit, every=1, first=0):
     spread = LANES // unit
-    sources, payload = ref.shape[:2]
-    units = streams_in(ref, unit) // (sources * unit)
+    sources, payload = ref.shape[0] // every, ref.shape[1]
+    units = payload * LANES // (2 * CAP * NSPEC * unit)
     lane = lax.broadcasted_iota(jnp.int32, (payload, LANES), 1) // unit
     for q in range(sources // spread):
-        parts = [ref[spread * q + a].astype(jnp.float32) for a in range(spread)]
+        parts = [
+            ref[every * (spread * q + a) + first].astype(jnp.float32) for a in range(spread)
+        ]
         bit = 1
         while bit < spread:
             even = lane // bit % 2 == 0
@@ -310,7 +320,7 @@
             apart[slot, pl.ds(g, payload, stride=spread), :] = parts[g]
         rows = 2 * CAP * NSPEC
         for u in range(units):
-            place = base + (u * (sources // spread) + q) * LANES
+            place = (u * (sources // spread) + q) * LANES
             pre[:, place : place + LANES] = apart[slot, u * rows : (u + 1) * rows].astype(jnp.bfloat16)
 
 
@@ -335,7 +345,7 @@
     turn = one_hot(dest_ref[...], out_ref.shape[2])
     for h, part in enumerate((own, other)):
         copies[h].wait()
-        regroup(part, apart, pre, unit, 0)
+        regroup(part, apart, pre, unit)
         out_ref[h] = permute(pre[...], turn).astype(jnp.bfloat16)
 
 
@@ -382,9 +392,9 @@
         for copy in copies:
             copy.wait()
         for h in range(2):
-            regroup(held[h], apart, pre, unit, 0)
+            regroup(held[0], apart, pre, unit, 2, where[1] if h == 0 else 1 - where[1])
             half = permute(pre[...], turn)
-            for ref in held[2:]:
+            for ref in held[1:]:
                 half = half + ref[h].astype(jnp.float32)
             for n in range(2 * CAP):
                 first = n % 2 * time_len + h * NSPEC
@@ -443,26 +453,32 @@
     streams = voltages.shape[0]
     total = dests * streams
     unit = min(streams, 16)
-    plan = ((48, 4, 60), (16, 2, 32)) if streams == 64 else ((streams, 2, 60),)
     dest = (2 * station_map[:, None] + jnp.arange(2, dtype=jnp.int32)[None, :]).reshape(-1)
     dest = dest.reshape(dests, streams // unit, unit).transpose(1, 0, 2)
     where = jnp.stack([lax.axis_index("stn"), lax.axis_index("blk")]).astype(jnp.int32)
+
+    def turn(outgoing, axes):
+        return lax.all_to_all(outgoing, axes, split_axis=0, concat_axis=0, tiled=True)
+
+    def spots(start, size):
+        return dest[start // unit : (start + size) // unit].reshape(1, -1)
+
     settled = []
-    start = 0
-    for size, step, room in plan:
-        outgoing = channelize(voltages, chan_counts, dests, start, size, step, unit, room)
+    early = 48 if streams == 64 else 0
+    late = streams - early
+    if early:
+        outgoing = channelize(voltages, chan_counts, dests, 0, early, 4, unit, 60, 1)
         chan_counts, outgoing = lax.optimization_barrier((chan_counts, outgoing))
-        own = lax.all_to_all(outgoing, "stn", split_axis=0, concat_axis=0, tiled=True)
-        if settled:
-            own, other = lax.optimization_barrier((own, other))
-            settled = [settle(before, other, spot, total, unit)]
-        other = lax.ppermute(own, "blk", [(0, 1), (1, 0)])
-        spot = dest[start // unit : (start + size) // unit].reshape(1, -1)
-        if start + size < streams:
-            before = own
-            settled = [None]
-        start = start + size
-    return correlate([own, other] + settled, spot, chan_counts, where, total, unit)
+        first = turn(outgoing, "stn")
+        outgoing = channelize(voltages, chan_counts, dests, early, late, 2, unit, 32, 2)
+        first, outgoing = lax.optimization_barrier((first, outgoing))
+        first_other = lax.ppermute(first, "blk", [(0, 1), (1, 0)])
+        settled.append(settle(first, first_other, spots(0, early), total, unit))
+    else:
+        outgoing = channelize(voltages, chan_counts, dests, 0, late, 2, unit, 60, 2)
+    both = turn(outgoing, ("stn", "blk"))
+    spot = spots(early, late)
+    return correlate([both] + settled, spot, chan_counts, where, total, unit)
 
 
 def solution(mesh):

time: 88.8 us -> 83.6 us (0.941)
  blocking collectives: 20.6 us -> 0 us
  starting transfers between devices: 5.95 us -> 14.6 us
  waiting for transfers between devices: 10.8 us -> 14.9 us
  Pallas kernels: 50.4 us -> 52.9 us
    all_to_all x1 -> x0, blocking collectives: 20.6 us -> none  [body(): lax.all_to_all(outgoing, 'stn', split_axis=0, concat_axis=0, tiled=True)]
    ppermute x2 -> x1, waiting for transfers between devices: 2.5 us -> 14.4 us  [body(): first_other = lax.ppermute(first, 'blk', [(0, 1), (1, 0)])]
    all_to_all x1 -> x2, starting transfers between devices: 3.91 us -> 12.8 us  [turn(): lax.all_to_all(outgoing, axes, split_axis=0, concat_axis=0, tiled=True)]
    all_to_all x1 -> x2, waiting for transfers between devices: 8.28 us -> 0.51 us  [turn(): lax.all_to_all(outgoing, axes, split_axis=0, concat_axis=0, tiled=True)]
    pallas_call x2, Pallas kernels: 39.4 us -> 42 us  [channelize(): pl.pallas_call(kernel, grid_spec=pltpu.PrefetchScalarGridSpec(num_scalar_...]
    ppermute x2 -> x1, starting transfers between devices: 2.04 us -> 1.77 us  [body(): first_other = lax.ppermute(first, 'blk', [(0, 1), (1, 0)])]
  transfers between devices with their start and end apart: 3 -> 3, of which waited for: 2 -> 2; matrix products, arithmetic and copies ran while one was open for 1% -> 1% of each run, Pallas kernels for 17% -> 20%
where the time goes in v14:
time: 83.6 us; the launch traced here: 83.2 us
  Pallas kernels  52.9 us (63%)
  waiting for transfers between devices  14.9 us (18%)
  starting transfers between devices  14.6 us (17%)
    pallas_call x2, Pallas kernels, channelize(): pl.pallas_call(kernel, grid_spec=pltpu.PrefetchScalarGridSpec(num_scalar_...  42 us
    ppermute x1, waiting for transfers between devices, body(): first_other = lax.ppermute(first, 'blk', [(0, 1), (1, 0)])  14.4 us
    all_to_all x2, starting transfers between devices, turn(): lax.all_to_all(outgoing, axes, split_axis=0, concat_axis=0, tiled=True)  12.8 us
    pallas_call x1, Pallas kernels, correlate(): pl.pallas_call(functools.partial(correlator, unit), grid_spec=pltpu.Prefe...  7.32 us
    pallas_call x1, Pallas kernels, settle(): pl.pallas_call(functools.partial(settler, unit), in_specs=[pl.BlockSpec(m...  3.54 us
    ppermute x1, starting transfers between devices, body(): first_other = lax.ppermute(first, 'blk', [(0, 1), (1, 0)])  1.77 us
  transfers between devices with their start and end apart: 3, of which 2 were waited for; matrix products, arithmetic and copies ran while one was open for 1% of the time, Pallas kernels for 20%

profile of v14, /device:TPU:0, one launch (start us, length us, event | category | flops | bytes accessed | tf_op | source)
XLA Modules:
  0.0 83.2 jit_solution(11782047484363734221)
XLA Ops:
  0.0 0.0 copy-start
  0.0 0.0 copy-start.1
  0.0 0.0 copy-start.2
  0.0 29.3 %shard_map.55 = bf16[16,1,112,128]{3,2,1,0:T(8,128)(2,1)} custom-call(s32[16]{0:T(128)} %counts.3, bf16[64,1,63,2,4096]{4,3,2,1,0:T(2,128)(2,1)} %v_ref.3, bf16[4096,256]{1,0:T(8,128)(2,1)} %constant.14.clone.u_hbm, bf16[1024,512]{1,0:T(8,128)(2,1)} %constant.15.clone.w_hbm), custom_call_target="tpu_custom_call" | custom-call | flops 12683575296 | bytes 49545216 | tf_op jit(solution)/shard_map/pallas_call | solution.py:264
  29.3 7.4 %all-to-all-start = ((bf16[16,112,128]{2,1,0:T(8,128)(2,1)}), bf16[16,112,128]{2,1,0:T(8,128)(2,1)}, u32[]{:S(2)}, u32[]{:S(2)}) async-start(bf16[16,112,128]{2,1,0:T(8,128)(2,1)} %bitcast.7), calls=%async_computation | async-start | bytes 917504 | tf_op jit(solution)/shard_map/all_to_all | solution.py:461
  36.7 0.0 copy-done
  36.7 0.0 copy-done.1
  36.7 0.0 copy-done.2
  36.7 0.0 copy-start.3
  36.7 12.8 %shard_map.56 = bf16[16,2,48,128]{3,2,1,0:T(8,128)(2,1)} custom-call(s32[16]{0:T(128)S(1)} %copy-done.2, bf16[64,1,63,2,4096]{4,3,2,1,0:T(2,128)(2,1)} %v_ref.3, bf16[4096,256]{1,0:T(8,128)(2,1)S(1)} %copy-done, bf16[1024,512]{1,0:T(8,128)(2,1)S(1)} %copy-done.1), custom_call_target="tpu_custom_call" | custom-call | flops 4227858432 | bytes 16515072 | tf_op jit(solution)/shard_map/pallas_call | solution.py:264
  49.5 0.5 all-to-all-done.own_hbm
  50.0 5.4 %all-to-all-start.1 = ((bf16[32,48,128]{2,1,0:T(8,128)(2,1)}), bf16[32,48,128]{2,1,0:T(8,128)(2,1)S(1)}, u32[]{:S(2)}, u32[]{:S(2)}) async-start(bf16[32,48,128]{2,1,0:T(8,128)(2,1)} %bitcast.5), calls=%async_computation.1 | async-start | bytes 786432 | tf_op jit(solution)/shard_map/all_to_all | solution.py:461
  55.4 0.1 add.26
  55.5 1.8 %collective-permute-start = (bf16[16,112,128]{2,1,0:T(8,128)(2,1)}, bf16[16,112,128]{2,1,0:T(8,128)(2,1)S(1)}, u32[]{:S(2)}, u32[]{:S(2)}) collective-permute-start(bf16[16,112,128]{2,1,0:T(8,128)(2,1)} %all-to-all-done.own_hbm), channel_id=1, source_target_pairs={{0,1},{1,0},{2,3},{3,2},{4,5},{5,4},{6,7},{7,6},{8,9},{9,8},{10,11... | collective-permute-start | bytes 1376264 | tf_op jit(solution)/shard_map/ppermute | solution.py:475
  57.3 0.0 copy-done.3
  57.3 0.1 add.22
  57.4 0.1 copy.6
  57.5 0.1 add_bitcast_fusion
  57.6 0.1 copy.8
  57.7 0.1 reshape.21.dest_ref
  57.7 0.1 copy.7
  57.8 0.1 reshape.19.dest_ref
  57.9 0.1 pad_add_fusion.where
  58.0 14.4 %collective-permute-done.other_hbm = bf16[16,112,128]{2,1,0:T(8,128)(2,1)S(1)} collective-permute-done((bf16[16,112,128]{2,1,0:T(8,128)(2,1)}, bf16[16,112,128]{2,1,0:T(8,128)(2,1)S(1)}, u32[]{:S(2)}, u32[]{:S(2)}) %collective-permute-start) | collective-permute-done | bytes 458784 | tf_op jit(solution)/shard_map/ppermute | solution.py:475
  72.3 3.5 %shard_map.57.refs_1_ = bf16[2,288,1024]{2,1,0:T(8,128)(2,1)S(1)} custom-call(s32[1,768]{1,0:T(1,128)S(1)} %reshape.21.dest_ref, bf16[16,112,128]{2,1,0:T(8,128)(2,1)} %all-to-all-done.own_hbm, bf16[16,112,128]{2,1,0:T(8,128)(2,1)S(1)} %collective-permute-done.other_hbm), custom_call_target="tpu_custom_call" | custom-call | flops 905969664 | bytes 2097152 | tf_op jit(solution)/shard_map/pallas_call | solution.py:354
  75.9 0.0 all-to-all-done.1.refs_0_
  75.9 7.3 %shard_map.58 = bf16[1,3,2,512,1024]{4,3,2,1,0:T(8,128)(2,1)} custom-call(s32[16]{0:T(128)S(1)} %copy-done.2, s32[2]{0:T(128)S(1)} %pad_add_fusion.where, s32[1,256]{1,0:T(1,128)S(1)} %reshape.19.dest_ref, bf16[32,48,128]{2,1,0:T(8,128)(2,1)S(1)} %all-to-all-done.1.refs_0_, bf16[2,288,1024]{2,1,0:T(8,128)(2,1)S(1)} %shard_map.57.refs_1_), custom_call_target="tpu_custom_call" | custom-call | tf_op jit(solution)/shard_map/pallas_call | solution.py:429
  (5 shorter events, 0.0 us)
Async XLA Ops:
  0.0 36.7 %copy-start = (bf16[4096,256]{1,0:T(8,128)(2,1)S(1)}, bf16[4096,256]{1,0:T(8,128)(2,1)}, u32[]{:S(2)}) copy-start(bf16[4096,256]{1,0:T(8,128)(2,1)} %constant.14.clone.u_hbm) | copy-start | bytes 6291460
  0.0 36.7 %copy-start.1 = (bf16[1024,512]{1,0:T(8,128)(2,1)S(1)}, bf16[1024,512]{1,0:T(8,128)(2,1)}, u32[]{:S(2)}) copy-start(bf16[1024,512]{1,0:T(8,128)(2,1)} %constant.15.clone.w_hbm) | copy-start | bytes 3145732
  0.0 36.7 %copy-start.2 = (s32[16]{0:T(128)S(1)}, s32[16]{0:T(128)}, u32[]{:S(2)}) copy-start(s32[16]{0:T(128)} %counts.3) | copy-start | bytes 196
  29.3 20.7 %all-to-all-start = ((bf16[16,112,128]{2,1,0:T(8,128)(2,1)}), bf16[16,112,128]{2,1,0:T(8,128)(2,1)}, u32[]{:S(2)}, u32[]{:S(2)}) async-start(bf16[16,112,128]{2,1,0:T(8,128)(2,1)} %bitcast.7), calls=%async_computation | async-start | bytes 917504 | tf_op jit(solution)/shard_map/all_to_all | solution.py:461
  36.7 20.6 %copy-start.3 = (s32[512]{0:T(512)S(1)}, s32[512]{0:T(512)}, u32[]{:S(2)}) copy-start(s32[512]{0:T(512)} %param.6) | copy-start | bytes 6148
  50.0 25.9 %all-to-all-start.1 = ((bf16[32,48,128]{2,1,0:T(8,128)(2,1)}), bf16[32,48,128]{2,1,0:T(8,128)(2,1)S(1)}, u32[]{:S(2)}, u32[]{:S(2)}) async-start(bf16[32,48,128]{2,1,0:T(8,128)(2,1)} %bitcast.5), calls=%async_computation.1 | async-start | bytes 786432 | tf_op jit(solution)/shard_map/all_to_all | solution.py:461
  55.5 16.8 %collective-permute-start = (bf16[16,112,128]{2,1,0:T(8,128)(2,1)}, bf16[16,112,128]{2,1,0:T(8,128)(2,1)S(1)}, u32[]{:S(2)}, u32[]{:S(2)}) collective-permute-start(bf16[16,112,128]{2,1,0:T(8,128)(2,1)} %all-to-all-done.own_hbm), channel_id=1, source_target_pairs={{0,1},{1,0},{2,3},{3,2},{4,5},{5,4},{6,7},{7,6},{8,9},{9,8},{10,11... | collective-permute-start | bytes 1376264 | tf_op jit(solution)/shard_map/ppermute | solution.py:475

commit v15 on v13

--- a/solution.py
+++ b/solution.py
@@ -182,17 +182,17 @@
         for copy in tables_in:
             copy.start()
         turned[...] = jnp.zeros(turned.shape, jnp.float32)
+
+    @pl.when((i > 0) & (i + ahead - 1 < last))
+    def _():
+        begin(i + ahead - 1)
+
+    @pl.when(i == 0)
+    def _():
+        for copy in tables_in:
+            copy.wait()
         if streams // step > 1:
             begin(1)
-
-    @pl.when((i > 0) & (i + ahead - 1 < last))
-    def _():
-        begin(i + ahead - 1)
-
-    @pl.when(i == 0)
-    def _():
-        for copy in tables_in:
-            copy.wait()
 
     @pl.when(i < last)
     def _():

time: 77.9 us -> 78.6 us (level)
  no operation moved by 1% of the time
where the time goes in v15:
time: 78.6 us; the launch traced here: 78.2 us
  Pallas kernels  51.1 us (65%)
  starting transfers between devices  14.2 us (18%)
  waiting for transfers between devices  12.1 us (15%)
    pallas_call x2, Pallas kernels, channelize(): pl.pallas_call(kernel, grid_spec=pltpu.PrefetchScalarGridSpec(num_scalar_...  40 us
    all_to_all x2, starting transfers between devices, turn(): lax.all_to_all(outgoing, 'stn', split_axis=0, concat_axis=0, tiled=True)  12.2 us
    all_to_all x2, waiting for transfers between devices, turn(): lax.all_to_all(outgoing, 'stn', split_axis=0, concat_axis=0, tiled=True)  9.61 us
    pallas_call x1, Pallas kernels, correlate(): pl.pallas_call(functools.partial(correlator, unit), grid_spec=pltpu.Prefe...  7.54 us
    pallas_call x1, Pallas kernels, settle(): pl.pallas_call(functools.partial(settler, unit), in_specs=[pl.BlockSpec(m...  3.52 us
    ppermute x2, waiting for transfers between devices, swap(): return lax.ppermute(own, 'blk', [(0, 1), (1, 0)])  2.45 us
    ppermute x2, starting transfers between devices, swap(): return lax.ppermute(own, 'blk', [(0, 1), (1, 0)])  2.03 us
  transfers between devices with their start and end apart: 4, of which 3 were waited for; matrix products, arithmetic and copies ran while one was open for 1% of the time, Pallas kernels for 20%

profile of v15, /device:TPU:0, one launch (start us, length us, event | category | flops | bytes accessed | tf_op | source)
XLA Modules:
  0.0 78.2 jit_solution(17004814713010261531)
XLA Ops:
  0.0 0.0 copy-start
  0.0 0.0 copy-start.1
  0.0 0.0 copy-start.2
  0.0 28.0 %shard_map.55 = bf16[16,112,128]{2,1,0:T(8,128)(2,1)} custom-call(s32[16]{0:T(128)} %counts.3, bf16[64,1,63,2,4096]{4,3,2,1,0:T(2,128)(2,1)} %v_ref.3, bf16[4096,256]{1,0:T(8,128)(2,1)} %constant.14.clone.u_hbm, bf16[1024,512]{1,0:T(8,128)(2,1)} %constant.15.clone.w_hbm), custom_call_target="tpu_custom_call" | custom-call | flops 12683575296 | bytes 49545216 | tf_op jit(solution)/shard_map/pallas_call | solution.py:252
  28.0 7.4 %all-to-all-start = ((bf16[16,112,128]{2,1,0:T(8,128)(2,1)}), bf16[16,112,128]{2,1,0:T(8,128)(2,1)}, u32[]{:S(2)}, u32[]{:S(2)}) async-start(bf16[16,112,128]{2,1,0:T(8,128)(2,1)} %shard_map.55), calls=%async_computation | async-start | bytes 917504 | tf_op jit(solution)/shard_map/all_to_all | solution.py:451
  35.4 0.0 copy-done
  35.4 0.0 copy-done.1
  35.4 0.0 copy-done.2
  35.4 0.0 copy-start.3
  35.4 12.0 %shard_map.56 = bf16[16,48,128]{2,1,0:T(8,128)(2,1)} custom-call(s32[16]{0:T(128)S(1)} %copy-done.2, bf16[64,1,63,2,4096]{4,3,2,1,0:T(2,128)(2,1)} %v_ref.3, bf16[4096,256]{1,0:T(8,128)(2,1)S(1)} %copy-done, bf16[1024,512]{1,0:T(8,128)(2,1)S(1)} %copy-done.1), custom_call_target="tpu_custom_call" | custom-call | flops 4227858432 | bytes 16515072 | tf_op jit(solution)/shard_map/pallas_call | solution.py:252
  47.5 1.2 %all-to-all-done.own_hbm = bf16[16,112,128]{2,1,0:T(8,128)(2,1)} async-done(((bf16[16,112,128]{2,1,0:T(8,128)(2,1)}), bf16[16,112,128]{2,1,0:T(8,128)(2,1)}, u32[]{:S(2)}, u32[]{:S(2)}) %all-to-all-start) | async-done | bytes 458784 | tf_op jit(solution)/shard_map/all_to_all | solution.py:451
  48.7 1.5 %collective-permute-start = (bf16[16,112,128]{2,1,0:T(8,128)(2,1)}, bf16[16,112,128]{2,1,0:T(8,128)(2,1)S(1)}, u32[]{:S(2)}, u32[]{:S(2)}) collective-permute-start(bf16[16,112,128]{2,1,0:T(8,128)(2,1)} %all-to-all-done.own_hbm), channel_id=1, source_target_pairs={{0,1},{1,0},{2,3},{3,2},{4,5},{5,4},{6,7},{7,6},{8,9},{9,8},{10,11... | collective-permute-start | bytes 1376264 | tf_op jit(solution)/shard_map/ppermute | solution.py:454
  50.2 0.1 add.26
  50.3 4.8 %all-to-all-start.1 = ((bf16[16,48,128]{2,1,0:T(8,128)(2,1)}), bf16[16,48,128]{2,1,0:T(8,128)(2,1)S(1)}, u32[]{:S(2)}, u32[]{:S(2)}) async-start(bf16[16,48,128]{2,1,0:T(8,128)(2,1)} %shard_map.56), calls=%async_computation.1 | async-start | bytes 393216 | tf_op jit(solution)/shard_map/all_to_all | solution.py:451
  55.1 0.0 copy-done.3
  55.2 0.1 add.22
  55.3 0.1 copy.6
  55.4 0.1 add_bitcast_fusion
  55.4 0.1 copy.8
  55.5 0.1 reshape.13.dest_ref
  55.6 0.1 copy.7
  55.7 0.1 reshape.12.dest_ref
  55.8 8.4 %all-to-all-done.1.refs_0_ = bf16[16,48,128]{2,1,0:T(8,128)(2,1)S(1)} async-done(((bf16[16,48,128]{2,1,0:T(8,128)(2,1)}), bf16[16,48,128]{2,1,0:T(8,128)(2,1)S(1)}, u32[]{:S(2)}, u32[]{:S(2)}) %all-to-all-start.1) | async-done | bytes 196640 | tf_op jit(solution)/shard_map/all_to_all | solution.py:451
  64.1 0.0 collective-permute-done.other_hbm
  64.1 0.5 collective-permute-start.1
  64.6 0.1 pad_add_fusion.where
  64.7 3.5 %shard_map.57.refs_2_ = bf16[2,288,1024]{2,1,0:T(8,128)(2,1)S(1)} custom-call(s32[1,768]{1,0:T(1,128)S(1)} %reshape.13.dest_ref, bf16[16,112,128]{2,1,0:T(8,128)(2,1)} %all-to-all-done.own_hbm, bf16[16,112,128]{2,1,0:T(8,128)(2,1)S(1)} %collective-permute-done.other_hbm), custom_call_target="tpu_custom_call" | custom-call | flops 905969664 | bytes 2097152 | tf_op jit(solution)/shard_map/pallas_call | solution.py:344
  68.2 2.4 %collective-permute-done.1.refs_1_ = bf16[16,48,128]{2,1,0:T(8,128)(2,1)S(1)} collective-permute-done((bf16[16,48,128]{2,1,0:T(8,128)(2,1)S(1)}, bf16[16,48,128]{2,1,0:T(8,128)(2,1)S(1)}, u32[]{:S(2)}, u32[]{:S(2)}) %collective-permute-start.1) | collective-permute-done | bytes 196640 | tf_op jit(solution)/shard_map/ppermute | solution.py:454
  70.7 7.5 %shard_map.58 = bf16[1,3,2,512,1024]{4,3,2,1,0:T(8,128)(2,1)} custom-call(s32[16]{0:T(128)S(1)} %copy-done.2, s32[2]{0:T(128)S(1)} %pad_add_fusion.where, s32[1,256]{1,0:T(1,128)S(1)} %reshape.12.dest_ref, bf16[16,48,128]{2,1,0:T(8,128)(2,1)S(1)} %all-to-all-done.1.refs_0_, bf16[16,48,128]{2,1,0:T(8,128)(2,1)S(1)} %collective-permute-done.1.refs_1_, ...), custom_call_target="tpu_custom_call" | custom-call | tf_op jit(solution)/shard_map/pallas_call | solution.py:419
  (5 shorter events, 0.0 us)
Async XLA Ops:
  0.0 35.4 %copy-start = (bf16[4096,256]{1,0:T(8,128)(2,1)S(1)}, bf16[4096,256]{1,0:T(8,128)(2,1)}, u32[]{:S(2)}) copy-start(bf16[4096,256]{1,0:T(8,128)(2,1)} %constant.14.clone.u_hbm) | copy-start | bytes 6291460
  0.0 35.4 %copy-start.1 = (bf16[1024,512]{1,0:T(8,128)(2,1)S(1)}, bf16[1024,512]{1,0:T(8,128)(2,1)}, u32[]{:S(2)}) copy-start(bf16[1024,512]{1,0:T(8,128)(2,1)} %constant.15.clone.w_hbm) | copy-start | bytes 3145732
  0.0 35.4 %copy-start.2 = (s32[16]{0:T(128)S(1)}, s32[16]{0:T(128)}, u32[]{:S(2)}) copy-start(s32[16]{0:T(128)} %counts.3) | copy-start | bytes 196
  28.0 20.7 %all-to-all-start = ((bf16[16,112,128]{2,1,0:T(8,128)(2,1)}), bf16[16,112,128]{2,1,0:T(8,128)(2,1)}, u32[]{:S(2)}, u32[]{:S(2)}) async-start(bf16[16,112,128]{2,1,0:T(8,128)(2,1)} %shard_map.55), calls=%async_computation | async-start | bytes 917504 | tf_op jit(solution)/shard_map/all_to_all | solution.py:451
  35.4 19.7 %copy-start.3 = (s32[512]{0:T(512)S(1)}, s32[512]{0:T(512)}, u32[]{:S(2)}) copy-start(s32[512]{0:T(512)} %param.6) | copy-start | bytes 6148
  48.7 15.4 %collective-permute-start = (bf16[16,112,128]{2,1,0:T(8,128)(2,1)}, bf16[16,112,128]{2,1,0:T(8,128)(2,1)S(1)}, u32[]{:S(2)}, u32[]{:S(2)}) collective-permute-start(bf16[16,112,128]{2,1,0:T(8,128)(2,1)} %all-to-all-done.own_hbm), channel_id=1, source_target_pairs={{0,1},{1,0},{2,3},{3,2},{4,5},{5,4},{6,7},{7,6},{8,9},{9,8},{10,11... | collective-permute-start | bytes 1376264 | tf_op jit(solution)/shard_map/ppermute | solution.py:454
  50.3 13.8 %all-to-all-start.1 = ((bf16[16,48,128]{2,1,0:T(8,128)(2,1)}), bf16[16,48,128]{2,1,0:T(8,128)(2,1)S(1)}, u32[]{:S(2)}, u32[]{:S(2)}) async-start(bf16[16,48,128]{2,1,0:T(8,128)(2,1)} %shard_map.56), calls=%async_computation.1 | async-start | bytes 393216 | tf_op jit(solution)/shard_map/all_to_all | solution.py:451
  64.1 6.5 %collective-permute-start.1 = (bf16[16,48,128]{2,1,0:T(8,128)(2,1)S(1)}, bf16[16,48,128]{2,1,0:T(8,128)(2,1)S(1)}, u32[]{:S(2)}, u32[]{:S(2)}) collective-permute-start(bf16[16,48,128]{2,1,0:T(8,128)(2,1)S(1)} %all-to-all-done.1.refs_0_), channel_id=1, source_target_pairs={{0,1},{1,0},{2,3},{3,2},{4,5},{5,4},{6,7},{7,6},{8,9},{9,8},{10,11... | collective-permute-start | bytes 589832 | tf_op jit(solution)/shard_map/ppermute | solution.py:454
